TPU v7x, 256 devices: a whole 4x4x8 slice. The times are simulated.
256 devices in a mesh: band: 32 (over z_hi, x, core), grid: 8 (over y, z_lo).
Axes of the slice: x: 4, y: 4, z: 8 (z_hi: 4, z_lo: 2; z = z_hi * 2 + z_lo), core: 2. Of those that a mesh axis runs over, the one named last changes fastest.
Arguments:
- orbitals: bfloat16 [64, 192, 36864], P('band', 'grid'), may hold values from -6 to 6
Outputs:
- exchange_applied: float32 [32, 192, 36864], P('band', 'grid')
All inputs are finite; a program needn't handle non-finite values.
Results may differ from a plain program's by a relative error of at most 0.0062.
Values may be sent and summed in bfloat16 or wider, within the bound.
No kernel may reach another device: no remote copies, remote signals or barrier semaphores. Data moves between devices by JAX's collectives and lax.ppermute only.
A program may use at most 128 MiB of HBM per device.

v0:
```python
import jax
import jax.numpy as jnp
import numpy as np
from jax import lax
from jax.experimental import pallas as pl
from jax.experimental.pallas import tpu as pltpu
from jax.sharding import PartitionSpec as P

SIDE = 192
PARTS = 8
ROWS = SIDE // PARTS
QUADS = ROWS // 4
DUOS = SIDE // 2
CELLS = SIDE * SIDE
COUL = 160.0
PITCH = 104
PER_CUT = DUOS // 4
PIECE = (QUADS, 2 * ROWS, 384)
VECTOR = pl.BlockSpec(memory_space=pltpu.VMEM)
SCALAR = pl.BlockSpec(memory_space=pltpu.SMEM)
F32 = jnp.float32
BF16 = jnp.bfloat16


def cas_matrix():
    index = np.arange(SIDE, dtype=np.int32)
    phases = (index[:, None] * index[None, :] % SIDE).astype(np.float32) * np.float32(2.0 * np.pi / SIDE)
    return np.cos(phases) + np.sin(phases)


CAS = cas_matrix()
BY_PARITY = np.concatenate([np.arange(0, SIDE, 2), np.arange(1, SIDE, 2)])
Y_TABLE = CAS[:, BY_PARITY]
Y_BACK = CAS[BY_PARITY, :]
X_TABLE = CAS[:, BY_PARITY]
X_BACK = CAS[BY_PARITY, :]


def z_tables():
    gap = np.zeros((64, 256), np.float32)
    space = np.zeros((SIDE, 64), np.float32)
    first = np.concatenate([CAS, space], axis=1)
    second = np.concatenate([CAS[:, :128], space, CAS[:, 128:]], axis=1)
    return np.stack([np.concatenate(part, axis=0) for table in (first, second) for part in ((table, gap), (gap, table))])


Z_TABLES = z_tables()
Z_BACKS = np.swapaxes(Z_TABLES, 1, 2)


def wave(index):
    return jnp.where(index < SIDE // 2, index, index - SIDE).astype(F32)


def coulomb(me):
    shape = (ROWS // 2, SIDE, 384)
    pair = lax.broadcasted_iota(jnp.int32, shape, 0)
    row = lax.broadcasted_iota(jnp.int32, shape, 1)
    col = lax.broadcasted_iota(jnp.int32, shape, 2)
    late = jnp.where(col < 256, col >= 128, col >= 320)
    kz = jnp.where(col < 256, col % 128, 128 + col % 64)
    ky = me * ROWS + pair + jnp.where(late, ROWS // 2, 0)
    mx, my, mz = wave(row), wave(ky), wave(kz)
    norm_sq = mx * mx + my * my + mz * mz
    bounded = jnp.maximum(norm_sq, 1.0)
    return jnp.where(norm_sq > 0.5, COUL / bounded, 0.0) / float(SIDE) ** 3


def dot(left, right):
    return jnp.dot(left, right, preferred_element_type=F32)


def tiles(lots, rows):
    return jnp.concatenate([lot[rows, :] for lot in lots], axis=1)


def forward_body(column, target, *refs):
    sources, (z_tables, y_table, out), lots = refs[:-6], refs[-6:-3], refs[-3:]
    for which in range(len(sources) // 4):
        for slot in range(4):
            source = sources[which * 4 + slot]

            def form(part, carry, source=source, slot=slot):
                duo = (column[0] ^ slot) * PER_CUT + part
                left = target[:, pl.ds(pl.multiple_of(duo * 384, 128), 384)].astype(F32)
                right = source[:, pl.ds(pl.multiple_of(part * 384, 128), 384)].astype(F32)
                density = left * right
                for tile, lot in enumerate(lots):
                    lot[pl.ds(duo, ROWS, stride=PITCH), :] = density[:, tile * 128 : (tile + 1) * 128]
                return carry

            lax.fori_loop(0, PER_CUT, form, 0, unroll=12)

        def planes(quad, carry, which=which):
            along_z = []
            for pair in range(2):
                halves = []
                for plane in range(2):
                    rows = pl.ds(pl.multiple_of((quad * 4 + pair * 2 + plane) * PITCH, 8), DUOS)
                    density = tiles(lots, rows).astype(BF16)
                    even = dot(density[:, :256], z_tables[2 * plane])
                    odd = dot(density[:, 128:], z_tables[2 * plane + 1])
                    halves.append(jnp.concatenate([even, odd], axis=0))
                low, high = halves
                along_z += [low[:, :128], high[:, :128], low[:, 128:] + high[:, 128:]]
            along_y = dot(y_table[...], jnp.concatenate(along_z, axis=1).astype(BF16))
            for part in range(PARTS):
                rows = slice(part * ROWS, (part + 1) * ROWS)
                out[part, which, quad] = jnp.concatenate([along_y[rows, :384], along_y[rows, 384:]], axis=0).astype(BF16)
            return carry

        lax.fori_loop(0, QUADS, planes, 0, unroll=6)


def cost(pairs):
    return pl.CostEstimate(flops=pairs * 1400 * 10**6, bytes_accessed=pairs * 7 * 10**6, transcendentals=0)


def forward(column, target, sources):
    cuts = [cut for source in sources for cut in source]
    return pl.pallas_call(
        forward_body,
        in_specs=[SCALAR] + [VECTOR] * (len(cuts) + 3),
        out_specs=VECTOR,
        out_shape=jax.ShapeDtypeStruct((PARTS, len(sources), *PIECE), BF16),
        scratch_shapes=[pltpu.VMEM((ROWS * PITCH, 128), F32)] * 3,
        compiler_params=pltpu.CompilerParams(vmem_limit_bytes=32 * 2**20),
        cost_estimate=cost(len(sources)),
        name="forward_zy",
    )(column, target, *cuts, jnp.asarray(Z_TABLES, BF16), jnp.asarray(Y_TABLE, BF16))


def middle_body(pieces, kernel, x_table, x_back, out, head0, head1, tail):
    lots = (head0, head1, tail)
    block = QUADS * 2 * ROWS
    low = lax.broadcasted_iota(jnp.int32, (DUOS, 128), 1) < 64

    def step(i, carry):
        here = pl.ds(i, DUOS, stride=ROWS)
        there = pl.ds(i + ROWS // 2, DUOS, stride=ROWS)
        tail_a, tail_b = tail[here, :], tail[there, :]
        tail_first = jnp.where(low, tail_a, pltpu.roll(tail_b, 64, 1))
        tail_second = jnp.where(low, pltpu.roll(tail_a, 64, 1), tail_b)
        columns = jnp.concatenate(
            [
                jnp.concatenate([head0[here, :], head0[there, :], tail_first], axis=1),
                jnp.concatenate([head1[here, :], head1[there, :], tail_second], axis=1),
            ],
            axis=0,
        ).astype(BF16)
        spectrum = (kernel[i] * dot(x_table[...], columns)).astype(BF16)
        back = dot(x_back[...], spectrum)
        head0[here, :] = back[:DUOS, :128]
        head1[here, :] = back[DUOS:, :128]
        head0[there, :] = back[:DUOS, 128:256]
        head1[there, :] = back[DUOS:, 128:256]
        first, second = back[:DUOS, 256:], back[DUOS:, 256:]
        tail[here, :] = jnp.where(low, first, pltpu.roll(second, 64, 1))
        tail[there, :] = jnp.where(low, pltpu.roll(first, 64, 1), second)
        return carry

    for which in range(pieces.shape[1]):
        for part in range(PARTS):
            for tile, lot in enumerate(lots):
                lot[part * block : (part + 1) * block] = (
                    pieces[part, which, :, :, tile * 128 : (tile + 1) * 128].astype(F32).reshape(block, 128)
                )
        lax.fori_loop(0, ROWS // 2, step, 0, unroll=6)
        for part in range(PARTS):
            for tile, lot in enumerate(lots):
                out[part, which, :, :, tile * 128 : (tile + 1) * 128] = (
                    lot[part * block : (part + 1) * block].astype(BF16).reshape(QUADS, 2 * ROWS, 128)
                )


def middle(pieces, kernel):
    return pl.pallas_call(
        middle_body,
        in_specs=[VECTOR] * 4,
        out_specs=VECTOR,
        out_shape=jax.ShapeDtypeStruct(pieces.shape, BF16),
        scratch_shapes=[pltpu.VMEM((DUOS * ROWS, 128), F32)] * 3,
        compiler_params=pltpu.CompilerParams(vmem_limit_bytes=32 * 2**20),
        cost_estimate=cost(pieces.shape[1]),
        name="middle_x",
    )(pieces, kernel, jnp.asarray(X_TABLE, BF16), jnp.asarray(X_BACK, BF16))


def backward_body(column, pieces, *refs):
    pairs = pieces.shape[1]
    sources, refs = refs[: 4 * pairs], refs[4 * pairs :]
    (total, y_table, z_tables, out), lots = ((None,) + refs[:3], refs[3:]) if len(refs) == 6 else (refs[:4], refs[4:])

    for which in range(pairs):

        def planes(quad, carry, which=which):
            parts = [pieces[part, which, quad].astype(F32) for part in range(PARTS)]
            stacks = [
                jnp.concatenate([part[pair * ROWS : (pair + 1) * ROWS] for part in parts], axis=0) for pair in range(2)
            ]
            both = dot(y_table[...], jnp.concatenate(stacks, axis=1).astype(BF16)).astype(BF16)
            for pair in range(2):
                fields = both[:, pair * 384 : (pair + 1) * 384]
                for plane in range(2):
                    lanes = fields[:, 128:] if plane else jnp.concatenate([fields[:, :128], fields[:, 256:]], axis=1)
                    even = dot(lanes[:DUOS], z_tables[2 * plane])
                    odd = dot(lanes[DUOS:], z_tables[2 * plane + 1])
                    rows = pl.ds(pl.multiple_of((quad * 4 + pair * 2 + plane) * PITCH, 8), DUOS)
                    lots[0][rows, :] = even[:, :128]
                    lots[1][rows, :] = even[:, 128:] + odd[:, :128]
                    lots[2][rows, :] = odd[:, 128:]
            return carry

        lax.fori_loop(0, QUADS, planes, 0, unroll=3)
        base = total if which == 0 else out

        for slot in range(4):
            source = sources[which * 4 + slot]

            def gather(part, carry, source=source, slot=slot, base=base):
                duo = (column[0] ^ slot) * PER_CUT + part
                potential = tiles(lots, pl.ds(duo, ROWS, stride=PITCH))
                here = pl.ds(pl.multiple_of(duo * 384, 128), 384)
                right = source[:, pl.ds(pl.multiple_of(part * 384, 128), 384)].astype(F32)
                term = potential * right
                out[:, here] = -term if base is None else base[:, here] - term
                return carry

            lax.fori_loop(0, PER_CUT, gather, 0, unroll=12)


def backward(column, pieces, sources, total):
    cuts = [cut for source in sources for cut in source]
    return pl.pallas_call(
        backward_body,
        in_specs=[SCALAR] + [VECTOR] * (1 + len(cuts) + 2 + (total is not None)),
        out_specs=VECTOR,
        out_shape=jax.ShapeDtypeStruct((ROWS, CELLS), F32),
        scratch_shapes=[pltpu.VMEM((ROWS * PITCH, 128), F32)] * 3,
        compiler_params=pltpu.CompilerParams(vmem_limit_bytes=32 * 2**20),
        cost_estimate=cost(len(sources)),
        name="backward_yz",
    )(column, pieces, *cuts, *([] if total is None else [total]), jnp.asarray(Y_BACK, BF16), jnp.asarray(Z_BACKS, BF16))


def exchange(pieces):
    return lax.all_to_all(pieces, "grid", 0, 0, tiled=True)


def band_of(z_hi, x, core):
    return z_hi % 4 * 8 + x * 2 + core


def move(array, pairs):
    return lax.ppermute(array, "band", pairs)


def after(array, *others):
    return lax.optimization_barrier((array, *others))[0]


def scatter(orbital):
    cut = CELLS // 4
    return sum(
        move(
            orbital[:, step * cut : (step + 1) * cut],
            [(band_of(2 * root, 0, 0), band_of(2 * root, step, root)) for root in range(2)],
        )
        for step in range(4)
    )


def beside(mine, is_root):
    away = sum(
        move(mine, [(band_of(2 * c, x, c), band_of(2 * c + up, x, c)) for c in range(2) for x in range(4)]) for up in (1, 3)
    )
    return jnp.where(is_root, mine, away)


def beyond(mine):
    half = mine.shape[1] // 2
    parts = [
        move(part, [(band_of(2 * c + up, x, c), band_of(2 * c + 2, x, c)) for c in range(2) for x in range(4)])
        for up, part in ((1, mine[:, :half]), (3, mine[:, half:]))
    ]
    return mine + jnp.concatenate(parts, axis=1)


def gather_x(mine):
    return [mine] + [
        move(mine, [(band_of(z, x, c), band_of(z, x ^ step, c)) for z in range(4) for x in range(4) for c in range(2)])
        for step in range(1, 4)
    ]


def other_core(source):
    pairs = [(band_of(z, x, c), band_of(z, x, 1 - c)) for z in range(4) for x in range(4) for c in range(2)]
    return [move(cut, pairs) for cut in source]


def local(orbitals):
    band = lax.axis_index("band")
    z_hi, x, core = band // 8, (band // 2) % 4, band % 2
    column = x[None].astype(jnp.int32)
    kernel = coulomb(lax.axis_index("grid"))
    target = orbitals[0]
    is_root = z_hi == 2 * core

    cut_0 = scatter(orbitals[0])
    near_0 = beside(cut_0, is_root)
    cut_1 = scatter(after(orbitals[1], near_0))
    full_0 = beyond(near_0)
    mine_0 = gather_x(full_0)
    near_1 = beside(after(cut_1, full_0), is_root)
    full_1 = beyond(near_1)
    mine_1 = gather_x(after(full_1, *mine_0))

    batches = [[mine_0], [other_core(mine_0), mine_1], [other_core(mine_1)]]
    there = [exchange(forward(column, target, batch)) for batch in batches]
    backs = [exchange(middle(pieces, kernel)) for pieces in there]
    total = None
    for pieces, batch in zip(backs, batches):
        total = backward(column, pieces, batch, total)
    return total[None]


def solution(mesh):
    return jax.shard_map(
        local,
        mesh=mesh,
        in_specs=(P("band", "grid", None),),
        out_specs=P("band", "grid", None),
        check_vma=False,
    )
```

profile of v0, /device:TPU:128, one launch (start us, length us, event | category | flops | bytes accessed | tf_op | source)
XLA Modules:
  0.0 310.1 jit_solution(6021353508946751256)
XLA Ops:
  11.7 4.7 %collective-permute-done.2 = bf16[24,9216]{1,0:T(8,128)(2,1)S(1)} collective-permute-done((bf16[24,9216]{1,0:T(8,128)(2,1)S(1)}, bf16[24,9216]{1,0:T(8,128)(2,1)S(1)}, u32[]{:S(2)}, u32[]{:S(2)}) %collective-permute-start.2) | collective-permute-done | bytes 442400 | tf_op jit(solution)/shard_map/ppermute | solution.py:255
  26.3 7.5 %collective-permute-start.7 = (bf16[24,9216]{1,0:T(8,128)(2,1)S(1)}, bf16[24,9216]{1,0:T(8,128)(2,1)S(1)}, u32[]{:S(2)}, u32[]{:S(2)}) collective-permute-start(bf16[24,9216]{1,0:T(8,128)(2,1)S(1)} %get-tuple-element.13), channel_id=1, source_target_pairs={{0,16},{128,152},{1,17},{129,153},{2,18},{130,154},{3,19},{131,155... | collective-permute-start | bytes 1327112 | tf_op jit(solution)/shard_map/ppermute | solution.py:255
  33.8 6.9 %collective-permute-start.8 = (bf16[24,9216]{1,0:T(8,128)(2,1)S(1)}, bf16[24,9216]{1,0:T(8,128)(2,1)S(1)}, u32[]{:S(2)}, u32[]{:S(2)}) collective-permute-start(bf16[24,9216]{1,0:T(8,128)(2,1)S(1)} %get-tuple-element.15), channel_id=1, source_target_pairs={{0,32},{128,168},{1,33},{129,169},{2,34},{130,170},{3,35},{131,171... | collective-permute-start | bytes 1327112 | tf_op jit(solution)/shard_map/ppermute | solution.py:255
  42.2 5.9 %collective-permute-done.8 = bf16[24,9216]{1,0:T(8,128)(2,1)S(1)} collective-permute-done((bf16[24,9216]{1,0:T(8,128)(2,1)S(1)}, bf16[24,9216]{1,0:T(8,128)(2,1)S(1)}, u32[]{:S(2)}, u32[]{:S(2)}) %collective-permute-start.8) | collective-permute-done | bytes 442400 | tf_op jit(solution)/shard_map/ppermute | solution.py:255
  49.8 4.6 %collective-permute-start.18 = (bf16[24,9216]{1,0:T(8,128)(2,1)S(1)}, bf16[24,9216]{1,0:T(8,128)(2,1)}, u32[]{:S(2)}, u32[]{:S(2)}) collective-permute-start(bf16[24,9216]{1,0:T(8,128)(2,1)S(1)} %maximum_add_fusion.refs_0_), channel_id=1, source_target_pairs={{0,48},{8,56},{16,32},{24,40},{32,16},{40,24},{48,0},{56,8},{64,11... | collective-permute-start | bytes 1327112 | tf_op jit(solution)/shard_map/ppermute | solution.py:255
  59.5 6.0 %collective-permute-done.17.refs_2_ = bf16[24,9216]{1,0:T(8,128)(2,1)} collective-permute-done((bf16[24,9216]{1,0:T(8,128)(2,1)S(1)}, bf16[24,9216]{1,0:T(8,128)(2,1)}, u32[]{:S(2)}, u32[]{:S(2)}) %collective-permute-start.17) | collective-permute-done | bytes 442400 | tf_op jit(solution)/shard_map/ppermute | solution.py:255
  65.5 8.9 %collective-permute-done.18.refs_3_ = bf16[24,9216]{1,0:T(8,128)(2,1)} collective-permute-done((bf16[24,9216]{1,0:T(8,128)(2,1)S(1)}, bf16[24,9216]{1,0:T(8,128)(2,1)}, u32[]{:S(2)}, u32[]{:S(2)}) %collective-permute-start.18) | collective-permute-done | bytes 442400 | tf_op jit(solution)/shard_map/ppermute | solution.py:255
  85.7 5.2 %collective-permute-start.22 = (bf16[24,9216]{1,0:T(8,128)(2,1)S(1)}, bf16[24,9216]{1,0:T(8,128)(2,1)S(1)}, u32[]{:S(2)}, u32[]{:S(2)}) collective-permute-start(bf16[24,9216]{1,0:T(8,128)(2,1)S(1)} %maximum_add_fusion.1.refs_4_), channel_id=1, source_target_pairs={{0,32},{8,40},{16,48},{24,56},{32,0},{40,8},{48,16},{56,24},{64,96... | collective-permute-start | bytes 1327112 | tf_op jit(solution)/shard_map/ppermute | solution.py:255
  91.7 7.0 %collective-permute-done.20.refs_5_ = bf16[24,9216]{1,0:T(8,128)(2,1)S(1)} collective-permute-done((bf16[24,9216]{1,0:T(8,128)(2,1)S(1)}, bf16[24,9216]{1,0:T(8,128)(2,1)S(1)}, u32[]{:S(2)}, u32[]{:S(2)}) %collective-permute-start.20) | collective-permute-done | bytes 442400 | tf_op jit(solution)/shard_map/ppermute | solution.py:255
  99.5 10.9 %collective-permute-done.22.refs_6_ = bf16[24,9216]{1,0:T(8,128)(2,1)S(1)} collective-permute-done((bf16[24,9216]{1,0:T(8,128)(2,1)S(1)}, bf16[24,9216]{1,0:T(8,128)(2,1)S(1)}, u32[]{:S(2)}, u32[]{:S(2)}) %collective-permute-start.22) | collective-permute-done | bytes 442400 | tf_op jit(solution)/shard_map/ppermute | solution.py:255
  124.0 5.4 %all-to-all-start = ((bf16[8,1,6,48,384]{4,3,2,1,0:T(8,128)(2,1)}), bf16[8,1,6,48,384]{4,3,2,1,0:T(8,128)(2,1)}, u32[]{:S(2)}, u32[]{:S(2)}) async-start(bf16[8,1,6,48,384]{4,3,2,1,0:T(8,128)(2,1)} %copy-done.6), calls=%async_computation | async-start | bytes 3538944 | tf_op jit(solution)/shard_map/all_to_all | solution.py:247
  139.3 6.0 %forward_zy.4 = bf16[8,2,6,48,384]{4,3,2,1,0:T(8,128)(2,1)S(1)} custom-call(s32[1]{0:T(128)} %bitcast.column, bf16[24,36864]{1,0:T(8,128)(2,1)S(1)} %get-tuple-element.12.target, bf16[24,9216]{1,0:T(8,128)(2,1)S(1)} %collective-permute-done.26.refs_0_, bf16[24,9216]{1,0:T(8,128)(2,1)S(1)} %collective-permute-done.27.refs_1_, ...), custom_call_target="tpu_custom_call" | custom-call | flops 2800000000 | bytes 14000000 | tf_op jit(solution)/shard_map/forward_zy/pallas_call | solution.py:121
  153.3 4.7 %all-to-all-start.2 = ((bf16[8,2,6,48,384]{4,3,2,1,0:T(8,128)(2,1)}), bf16[8,2,6,48,384]{4,3,2,1,0:T(8,128)(2,1)}, u32[]{:S(2)}, u32[]{:S(2)}) async-start(bf16[8,2,6,48,384]{4,3,2,1,0:T(8,128)(2,1)} %copy-done.18), calls=%async_computation.2 | async-start | bytes 7077888 | tf_op jit(solution)/shard_map/all_to_all | solution.py:247
  167.6 32.0 %all-to-all-done.2.pieces = bf16[8,2,6,48,384]{4,3,2,1,0:T(8,128)(2,1)} async-done(((bf16[8,2,6,48,384]{4,3,2,1,0:T(8,128)(2,1)}), bf16[8,2,6,48,384]{4,3,2,1,0:T(8,128)(2,1)}, u32[]{:S(2)}, u32[]{:S(2)}) %all-to-all-start.2) | async-done | bytes 3538976 | tf_op jit(solution)/shard_map/all_to_all | solution.py:247
  205.8 9.8 %middle_x.4 = bf16[8,2,6,48,384]{4,3,2,1,0:T(8,128)(2,1)S(1)} custom-call(bf16[8,2,6,48,384]{4,3,2,1,0:T(8,128)(2,1)} %all-to-all-done.2.pieces, f32[12,192,384]{2,1,0:T(8,128)S(1)} %select_multiply_fusion.kernel, bf16[192,192]{1,0:T(8,128)(2,1)S(1)} %copy-done.23, bf16[192,192]{1,0:T(8,128)(2,1)S(1)} %copy-done.13), custom_call_target="tpu_custom_call" | custom-call | flops 2800000000 | bytes 14000000 | tf_op jit(solution)/shard_map/middle_x/pallas_call | solution.py:177
  217.4 8.7 %all-to-all-done.5.pieces = bf16[8,1,6,48,384]{4,3,2,1,0:T(8,128)(2,1)} async-done(((bf16[8,1,6,48,384]{4,3,2,1,0:T(8,128)(2,1)}), bf16[8,1,6,48,384]{4,3,2,1,0:T(8,128)(2,1)}, u32[]{:S(2)}, u32[]{:S(2)}) %all-to-all-start.5) | async-done | bytes 1769504 | tf_op jit(solution)/shard_map/all_to_all | solution.py:247
  226.1 4.5 %all-to-all-start.3 = ((bf16[8,2,6,48,384]{4,3,2,1,0:T(8,128)(2,1)}), bf16[8,2,6,48,384]{4,3,2,1,0:T(8,128)(2,1)}, u32[]{:S(2)}, u32[]{:S(2)}) async-start(bf16[8,2,6,48,384]{4,3,2,1,0:T(8,128)(2,1)} %copy-done), calls=%async_computation.3 | async-start | bytes 7077888 | tf_op jit(solution)/shard_map/all_to_all | solution.py:247
  232.3 5.4 %middle_x.3 = bf16[8,1,6,48,384]{4,3,2,1,0:T(8,128)(2,1)S(1)} custom-call(bf16[8,1,6,48,384]{4,3,2,1,0:T(8,128)(2,1)} %all-to-all-done.pieces, f32[12,192,384]{2,1,0:T(8,128)S(1)} %select_multiply_fusion.kernel, bf16[192,192]{1,0:T(8,128)(2,1)S(1)} %copy-done.24, bf16[192,192]{1,0:T(8,128)(2,1)S(1)} %copy-done.14), custom_call_target="tpu_custom_call" | custom-call | flops 1400000000 | bytes 7000000 | tf_op jit(solution)/shard_map/middle_x/pallas_call | solution.py:177
  239.0 32.1 %all-to-all-done.3.pieces = bf16[8,2,6,48,384]{4,3,2,1,0:T(8,128)(2,1)} async-done(((bf16[8,2,6,48,384]{4,3,2,1,0:T(8,128)(2,1)}), bf16[8,2,6,48,384]{4,3,2,1,0:T(8,128)(2,1)}, u32[]{:S(2)}, u32[]{:S(2)}) %all-to-all-start.3) | async-done | bytes 3538976 | tf_op jit(solution)/shard_map/all_to_all | solution.py:247
  271.1 4.6 %all-to-all-start.1 = ((bf16[8,1,6,48,384]{4,3,2,1,0:T(8,128)(2,1)}), bf16[8,1,6,48,384]{4,3,2,1,0:T(8,128)(2,1)}, u32[]{:S(2)}, u32[]{:S(2)}) async-start(bf16[8,1,6,48,384]{4,3,2,1,0:T(8,128)(2,1)} %copy-done.3), calls=%async_computation.1 | async-start | bytes 3538944 | tf_op jit(solution)/shard_map/all_to_all | solution.py:247
  275.8 4.9 %backward_yz.3.refs_8_ = f32[24,36864]{1,0:T(8,128)S(1)} custom-call(s32[1]{0:T(128)} %bitcast.column, bf16[8,1,6,48,384]{4,3,2,1,0:T(8,128)(2,1)} %all-to-all-done.5.pieces, bf16[24,9216]{1,0:T(8,128)(2,1)S(1)} %copy-done.11, bf16[24,9216]{1,0:T(8,128)(2,1)S(1)} %copy-done.40, bf16[24,9216]{1,0:T(8,128)(2,1)} %collective-permute-done.17.refs_2_, ...), custom_call_target="tpu_custom_call" | custom-call | flops 1400000000 | bytes 7000000 | tf_op jit(solution)/shard_map/backward_yz/pallas_call | solution.py:234
  280.9 8.5 %backward_yz.4.refs_4_ = f32[24,36864]{1,0:T(8,128)S(1)} custom-call(s32[1]{0:T(128)} %bitcast.column, bf16[8,2,6,48,384]{4,3,2,1,0:T(8,128)(2,1)} %all-to-all-done.3.pieces, bf16[24,9216]{1,0:T(8,128)(2,1)S(1)} %copy-done.51, bf16[24,9216]{1,0:T(8,128)(2,1)S(1)} %copy-done.53, bf16[24,9216]{1,0:T(8,128)(2,1)S(1)} %copy-done.55, ...), custom_call_target="tpu_custom_call" | custom-call | flops 2800000000 | bytes 14000000 | tf_op jit(solution)/shard_map/backward_yz/pallas_call | solution.py:234
  289.4 8.1 %all-to-all-done.1.pieces = bf16[8,1,6,48,384]{4,3,2,1,0:T(8,128)(2,1)} async-done(((bf16[8,1,6,48,384]{4,3,2,1,0:T(8,128)(2,1)}), bf16[8,1,6,48,384]{4,3,2,1,0:T(8,128)(2,1)}, u32[]{:S(2)}, u32[]{:S(2)}) %all-to-all-start.1) | async-done | bytes 1769504 | tf_op jit(solution)/shard_map/all_to_all | solution.py:247
  303.5 6.6 %backward_yz.5 = f32[24,36864]{1,0:T(8,128)} custom-call(s32[1]{0:T(128)} %bitcast.column, bf16[8,1,6,48,384]{4,3,2,1,0:T(8,128)(2,1)} %all-to-all-done.1.pieces, bf16[24,9216]{1,0:T(8,128)(2,1)S(1)} %copy-done.29, bf16[24,9216]{1,0:T(8,128)(2,1)S(1)} %copy-done.31, bf16[24,9216]{1,0:T(8,128)(2,1)S(1)} %copy-done.33, bf16[24,9216]{1,0:T(8,128)(2,1)S(1)} %copy-done.35, ...), custom_call_target="tpu_custom_call" | custom-call | flops 1400000000 | bytes 7000000 | tf_op jit(solution)/shard_map/backward_yz/pallas_call | solution.py:234
  (195 shorter events, 100.3 us)
Async XLA Ops:
  4.1 7.6 %collective-permute-start.1 = (bf16[24,9216]{1,0:T(8,128)(2,1)S(1)}, bf16[24,9216]{1,0:T(8,128)(2,1)S(1)}, u32[]{:S(2)}, u32[]{:S(2)}) collective-permute-start(bf16[24,9216]{1,0:T(8,128)(2,1)S(1)} %get-tuple-element.17), channel_id=1, source_target_pairs={{0,16},{128,152},{1,17},{129,153},{2,18},{130,154},{3,19},{131,155... | collective-permute-start | bytes 1327112 | tf_op jit(solution)/shard_map/ppermute | solution.py:255
  5.9 10.5 %collective-permute-start.2 = (bf16[24,9216]{1,0:T(8,128)(2,1)S(1)}, bf16[24,9216]{1,0:T(8,128)(2,1)S(1)}, u32[]{:S(2)}, u32[]{:S(2)}) collective-permute-start(bf16[24,9216]{1,0:T(8,128)(2,1)S(1)} %get-tuple-element.19), channel_id=1, source_target_pairs={{0,32},{128,168},{1,33},{129,169},{2,34},{130,170},{3,35},{131,171... | collective-permute-start | bytes 1327112 | tf_op jit(solution)/shard_map/ppermute | solution.py:255
  8.2 8.3 %collective-permute-start.3 = (bf16[24,9216]{1,0:T(8,128)(2,1)S(1)}, bf16[24,9216]{1,0:T(8,128)(2,1)S(1)}, u32[]{:S(2)}, u32[]{:S(2)}) collective-permute-start(bf16[24,9216]{1,0:T(8,128)(2,1)S(1)} %get-tuple-element.18), channel_id=1, source_target_pairs={{0,48},{128,184},{1,49},{129,185},{2,50},{130,186},{3,51},{131,187... | collective-permute-start | bytes 1327112 | tf_op jit(solution)/shard_map/ppermute | solution.py:255
  21.4 19.3 %collective-permute-start.10 = (bf16[24,4608]{1,0:T(8,128)(2,1)S(1)}, bf16[24,4608]{1,0:T(8,128)(2,1)S(1)}, u32[]{:S(2)}, u32[]{:S(2)}) collective-permute-start(bf16[24,4608]{1,0:T(8,128)(2,1)S(1)} %get-tuple-element.23), channel_id=1, source_target_pairs={{64,128},{80,144},{96,160},{112,176},{200,8},{216,24},{232,40},{24... | collective-permute-start | bytes 663560 | tf_op jit(solution)/shard_map/ppermute | solution.py:255
  22.7 19.3 %collective-permute-start.11 = (bf16[24,4608]{1,0:T(8,128)(2,1)S(1)}, bf16[24,4608]{1,0:T(8,128)(2,1)S(1)}, u32[]{:S(2)}, u32[]{:S(2)}) collective-permute-start(bf16[24,4608]{1,0:T(8,128)(2,1)S(1)} %get-tuple-element.24), channel_id=1, source_target_pairs={{192,128},{208,144},{224,160},{240,176},{72,8},{88,24},{104,40},{1... | collective-permute-start | bytes 663560 | tf_op jit(solution)/shard_map/ppermute | solution.py:255
  24.2 18.0 %collective-permute-start.6 = (bf16[24,9216]{1,0:T(8,128)(2,1)S(1)}, bf16[24,9216]{1,0:T(8,128)(2,1)S(1)}, u32[]{:S(2)}, u32[]{:S(2)}) collective-permute-start(bf16[24,9216]{1,0:T(8,128)(2,1)S(1)} %get-tuple-element.16), channel_id=1, source_target_pairs={{0,0},{128,136},{1,1},{129,137},{2,2},{130,138},{3,3},{131,139},{4... | collective-permute-start | bytes 1327112 | tf_op jit(solution)/shard_map/ppermute | solution.py:255
  26.3 15.9 %collective-permute-start.7 = (bf16[24,9216]{1,0:T(8,128)(2,1)S(1)}, bf16[24,9216]{1,0:T(8,128)(2,1)S(1)}, u32[]{:S(2)}, u32[]{:S(2)}) collective-permute-start(bf16[24,9216]{1,0:T(8,128)(2,1)S(1)} %get-tuple-element.13), channel_id=1, source_target_pairs={{0,16},{128,152},{1,17},{129,153},{2,18},{130,154},{3,19},{131,155... | collective-permute-start | bytes 1327112 | tf_op jit(solution)/shard_map/ppermute | solution.py:255
  33.8 14.3 %collective-permute-start.8 = (bf16[24,9216]{1,0:T(8,128)(2,1)S(1)}, bf16[24,9216]{1,0:T(8,128)(2,1)S(1)}, u32[]{:S(2)}, u32[]{:S(2)}) collective-permute-start(bf16[24,9216]{1,0:T(8,128)(2,1)S(1)} %get-tuple-element.15), channel_id=1, source_target_pairs={{0,32},{128,168},{1,33},{129,169},{2,34},{130,170},{3,35},{131,171... | collective-permute-start | bytes 1327112 | tf_op jit(solution)/shard_map/ppermute | solution.py:255
  49.6 9.9 %collective-permute-start.16 = (bf16[24,9216]{1,0:T(8,128)(2,1)S(1)}, bf16[24,9216]{1,0:T(8,128)(2,1)S(1)}, u32[]{:S(2)}, u32[]{:S(2)}) collective-permute-start(bf16[24,9216]{1,0:T(8,128)(2,1)S(1)} %maximum_add_fusion.refs_0_), channel_id=1, source_target_pairs={{0,16},{8,24},{16,0},{24,8},{32,48},{40,56},{48,32},{56,40},{64,80... | collective-permute-start | bytes 1327112 | tf_op jit(solution)/shard_map/ppermute | solution.py:255
  49.7 15.8 %collective-permute-start.17 = (bf16[24,9216]{1,0:T(8,128)(2,1)S(1)}, bf16[24,9216]{1,0:T(8,128)(2,1)}, u32[]{:S(2)}, u32[]{:S(2)}) collective-permute-start(bf16[24,9216]{1,0:T(8,128)(2,1)S(1)} %maximum_add_fusion.refs_0_), channel_id=1, source_target_pairs={{0,32},{8,40},{16,48},{24,56},{32,0},{40,8},{48,16},{56,24},{64,96... | collective-permute-start | bytes 1327112 | tf_op jit(solution)/shard_map/ppermute | solution.py:255
  49.8 24.6 %collective-permute-start.18 = (bf16[24,9216]{1,0:T(8,128)(2,1)S(1)}, bf16[24,9216]{1,0:T(8,128)(2,1)}, u32[]{:S(2)}, u32[]{:S(2)}) collective-permute-start(bf16[24,9216]{1,0:T(8,128)(2,1)S(1)} %maximum_add_fusion.refs_0_), channel_id=1, source_target_pairs={{0,48},{8,56},{16,32},{24,40},{32,16},{40,24},{48,0},{56,8},{64,11... | collective-permute-start | bytes 1327112 | tf_op jit(solution)/shard_map/ppermute | solution.py:255
  56.0 28.3 %collective-permute-start.14 = (bf16[24,4608]{1,0:T(8,128)(2,1)}, bf16[24,4608]{1,0:T(8,128)(2,1)}, u32[]{:S(2)}, u32[]{:S(2)}) collective-permute-start(bf16[24,4608]{1,0:T(8,128)(2,1)} %get-tuple-element.21), channel_id=1, source_target_pairs={{64,128},{80,144},{96,160},{112,176},{200,8},{216,24},{232,40},{24... | collective-permute-start | bytes 663560 | tf_op jit(solution)/shard_map/ppermute | solution.py:255
  57.3 27.0 %collective-permute-start.15 = (bf16[24,4608]{1,0:T(8,128)(2,1)}, bf16[24,4608]{1,0:T(8,128)(2,1)}, u32[]{:S(2)}, u32[]{:S(2)}) collective-permute-start(bf16[24,4608]{1,0:T(8,128)(2,1)} %get-tuple-element.22), channel_id=1, source_target_pairs={{192,128},{208,144},{224,160},{240,176},{72,8},{88,24},{104,40},{1... | collective-permute-start | bytes 663560 | tf_op jit(solution)/shard_map/ppermute | solution.py:255
  79.8 44.2 %all-to-all-start.4 = ((bf16[8,1,6,48,384]{4,3,2,1,0:T(8,128)(2,1)}), bf16[8,1,6,48,384]{4,3,2,1,0:T(8,128)(2,1)S(1)}, u32[]{:S(2)}, u32[]{:S(2)}) async-start(bf16[8,1,6,48,384]{4,3,2,1,0:T(8,128)(2,1)} %copy-done.5), calls=%async_computation.4 | async-start | bytes 3538944 | tf_op jit(solution)/shard_map/all_to_all | solution.py:247
  85.6 13.1 %collective-permute-start.20 = (bf16[24,9216]{1,0:T(8,128)(2,1)S(1)}, bf16[24,9216]{1,0:T(8,128)(2,1)S(1)}, u32[]{:S(2)}, u32[]{:S(2)}) collective-permute-start(bf16[24,9216]{1,0:T(8,128)(2,1)S(1)} %maximum_add_fusion.1.refs_4_), channel_id=1, source_target_pairs={{0,16},{8,24},{16,0},{24,8},{32,48},{40,56},{48,32},{56,40},{64,80... | collective-permute-start | bytes 1327112 | tf_op jit(solution)/shard_map/ppermute | solution.py:255
  85.7 24.7 %collective-permute-start.22 = (bf16[24,9216]{1,0:T(8,128)(2,1)S(1)}, bf16[24,9216]{1,0:T(8,128)(2,1)S(1)}, u32[]{:S(2)}, u32[]{:S(2)}) collective-permute-start(bf16[24,9216]{1,0:T(8,128)(2,1)S(1)} %maximum_add_fusion.1.refs_4_), channel_id=1, source_target_pairs={{0,32},{8,40},{16,48},{24,56},{32,0},{40,8},{48,16},{56,24},{64,96... | collective-permute-start | bytes 1327112 | tf_op jit(solution)/shard_map/ppermute | solution.py:255
  90.9 22.0 %collective-permute-start.24 = (bf16[24,9216]{1,0:T(8,128)(2,1)S(1)}, bf16[24,9216]{1,0:T(8,128)(2,1)S(1)}, u32[]{:S(2)}, u32[]{:S(2)}) collective-permute-start(bf16[24,9216]{1,0:T(8,128)(2,1)S(1)} %maximum_add_fusion.1.refs_4_), channel_id=1, source_target_pairs={{0,48},{8,56},{16,32},{24,40},{32,16},{40,24},{48,0},{56,8},{64,11... | collective-permute-start | bytes 1327112 | tf_op jit(solution)/shard_map/ppermute | solution.py:255
  90.9 22.8 %collective-permute-start.19 = (bf16[24,9216]{1,0:T(8,128)(2,1)S(1)}, bf16[24,9216]{1,0:T(8,128)(2,1)S(1)}, u32[]{:S(2)}, u32[]{:S(2)}) collective-permute-start(bf16[24,9216]{1,0:T(8,128)(2,1)S(1)} %maximum_add_fusion.1.refs_4_), channel_id=1, source_target_pairs={{0,8},{8,0},{16,24},{24,16},{32,40},{40,32},{48,56},{56,48},{64,72... | collective-permute-start | bytes 1327112 | tf_op jit(solution)/shard_map/ppermute | solution.py:255
  98.7 15.0 %collective-permute-start.21 = (bf16[24,9216]{1,0:T(8,128)(2,1)S(1)}, bf16[24,9216]{1,0:T(8,128)(2,1)S(1)}, u32[]{:S(2)}, u32[]{:S(2)}) collective-permute-start(bf16[24,9216]{1,0:T(8,128)(2,1)S(1)} %collective-permute-done.20.refs_5_), channel_id=1, source_target_pairs={{0,8},{8,0},{16,24},{24,16},{32,40},{40,32},{48,56},{56,48},{64,72... | collective-permute-start | bytes 1327112 | tf_op jit(solution)/shard_map/ppermute | solution.py:255
  124.0 29.3 %all-to-all-start = ((bf16[8,1,6,48,384]{4,3,2,1,0:T(8,128)(2,1)}), bf16[8,1,6,48,384]{4,3,2,1,0:T(8,128)(2,1)}, u32[]{:S(2)}, u32[]{:S(2)}) async-start(bf16[8,1,6,48,384]{4,3,2,1,0:T(8,128)(2,1)} %copy-done.6), calls=%async_computation | async-start | bytes 3538944 | tf_op jit(solution)/shard_map/all_to_all | solution.py:247
  153.3 46.4 %all-to-all-start.2 = ((bf16[8,2,6,48,384]{4,3,2,1,0:T(8,128)(2,1)}), bf16[8,2,6,48,384]{4,3,2,1,0:T(8,128)(2,1)}, u32[]{:S(2)}, u32[]{:S(2)}) async-start(bf16[8,2,6,48,384]{4,3,2,1,0:T(8,128)(2,1)} %copy-done.18), calls=%async_computation.2 | async-start | bytes 7077888 | tf_op jit(solution)/shard_map/all_to_all | solution.py:247
  199.7 26.4 %all-to-all-start.5 = ((bf16[8,1,6,48,384]{4,3,2,1,0:T(8,128)(2,1)}), bf16[8,1,6,48,384]{4,3,2,1,0:T(8,128)(2,1)}, u32[]{:S(2)}, u32[]{:S(2)}) async-start(bf16[8,1,6,48,384]{4,3,2,1,0:T(8,128)(2,1)} %copy-done.4), calls=%async_computation.5 | async-start | bytes 3538944 | tf_op jit(solution)/shard_map/all_to_all | solution.py:247
  226.1 45.0 %all-to-all-start.3 = ((bf16[8,2,6,48,384]{4,3,2,1,0:T(8,128)(2,1)}), bf16[8,2,6,48,384]{4,3,2,1,0:T(8,128)(2,1)}, u32[]{:S(2)}, u32[]{:S(2)}) async-start(bf16[8,2,6,48,384]{4,3,2,1,0:T(8,128)(2,1)} %copy-done), calls=%async_computation.3 | async-start | bytes 7077888 | tf_op jit(solution)/shard_map/all_to_all | solution.py:247
  271.1 26.4 %all-to-all-start.1 = ((bf16[8,1,6,48,384]{4,3,2,1,0:T(8,128)(2,1)}), bf16[8,1,6,48,384]{4,3,2,1,0:T(8,128)(2,1)}, u32[]{:S(2)}, u32[]{:S(2)}) async-start(bf16[8,1,6,48,384]{4,3,2,1,0:T(8,128)(2,1)} %copy-done.3), calls=%async_computation.1 | async-start | bytes 3538944 | tf_op jit(solution)/shard_map/all_to_all | solution.py:247
  (71 other events, 461.7 us)
where the time goes:
time: 312 us; the launch traced here: 310 us
  waiting for transfers between devices  136 us (44%)
  starting transfers between devices  73.4 us (24%)
  Pallas kernels  52.3 us (17%)
  local copies, waits for them, and re-layouts  42.7 us (14%)
  other arithmetic  4.69 us (2%)
    all_to_all x6, waiting for transfers between devices, exchange(): return lax.all_to_all(pieces, 'grid', 0, 0, tiled=True)  84 us
    ppermute x30, waiting for transfers between devices, move(): return lax.ppermute(array, 'band', pairs)  52.2 us
    ppermute x30, starting transfers between devices, move(): return lax.ppermute(array, 'band', pairs)  45.4 us
    unnamed x118, local copies, waits for them, and re-layouts  39.4 us
    all_to_all x6, starting transfers between devices, exchange(): return lax.all_to_all(pieces, 'grid', 0, 0, tiled=True)  28 us
    pallas_call x3, Pallas kernels, backward(): pl.pallas_call(backward_body, in_specs=[SCALAR] + [VECTOR] * (1 + len(cut...  20 us
    pallas_call x3, Pallas kernels, middle(): pl.pallas_call(middle_body, in_specs=[VECTOR] * 4, out_specs=VECTOR, out_...  19 us
    pallas_call x3, Pallas kernels, forward(): pl.pallas_call(forward_body, in_specs=[SCALAR] + [VECTOR] * (len(cuts) +...  13.2 us
  transfers between devices with their start and end apart: 36, of which 19 were waited for; matrix products, arithmetic and copies ran while one was open for 1% of the time, Pallas kernels for 15%

commit v1 on v0

--- a/solution.py
+++ b/solution.py
@@ -124,7 +124,7 @@
         out_specs=VECTOR,
         out_shape=jax.ShapeDtypeStruct((PARTS, len(sources), *PIECE), BF16),
         scratch_shapes=[pltpu.VMEM((ROWS * PITCH, 128), F32)] * 3,
-        compiler_params=pltpu.CompilerParams(vmem_limit_bytes=32 * 2**20),
+        compiler_params=pltpu.CompilerParams(vmem_limit_bytes=16 * 2**20),
         cost_estimate=cost(len(sources)),
         name="forward_zy",
     )(column, target, *cuts, jnp.asarray(Z_TABLES, BF16), jnp.asarray(Y_TABLE, BF16))
@@ -180,7 +180,7 @@
         out_specs=VECTOR,
         out_shape=jax.ShapeDtypeStruct(pieces.shape, BF16),
         scratch_shapes=[pltpu.VMEM((DUOS * ROWS, 128), F32)] * 3,
-        compiler_params=pltpu.CompilerParams(vmem_limit_bytes=32 * 2**20),
+        compiler_params=pltpu.CompilerParams(vmem_limit_bytes=16 * 2**20),
         cost_estimate=cost(pieces.shape[1]),
         name="middle_x",
     )(pieces, kernel, jnp.asarray(X_TABLE, BF16), jnp.asarray(X_BACK, BF16))
@@ -237,7 +237,7 @@
         out_specs=VECTOR,
         out_shape=jax.ShapeDtypeStruct((ROWS, CELLS), F32),
         scratch_shapes=[pltpu.VMEM((ROWS * PITCH, 128), F32)] * 3,
-        compiler_params=pltpu.CompilerParams(vmem_limit_bytes=32 * 2**20),
+        compiler_params=pltpu.CompilerParams(vmem_limit_bytes=16 * 2**20),
         cost_estimate=cost(len(sources)),
         name="backward_yz",
     )(column, pieces, *cuts, *([] if total is None else [total]), jnp.asarray(Y_BACK, BF16), jnp.asarray(Z_BACKS, BF16))
@@ -307,20 +307,22 @@
     is_root = z_hi == 2 * core
 
     cut_0 = scatter(orbitals[0])
-    near_0 = beside(cut_0, is_root)
-    cut_1 = scatter(after(orbitals[1], near_0))
-    full_0 = beyond(near_0)
+    cut_1 = scatter(after(orbitals[1], cut_0))
+    full_0 = beyond(beside(cut_0, is_root))
     mine_0 = gather_x(full_0)
-    near_1 = beside(after(cut_1, full_0), is_root)
-    full_1 = beyond(near_1)
+    other_0 = other_core(mine_0)
+    full_1 = beyond(beside(after(cut_1, full_0), is_root))
     mine_1 = gather_x(after(full_1, *mine_0))
-
-    batches = [[mine_0], [other_core(mine_0), mine_1], [other_core(mine_1)]]
-    there = [exchange(forward(column, target, batch)) for batch in batches]
-    backs = [exchange(middle(pieces, kernel)) for pieces in there]
-    total = None
-    for pieces, batch in zip(backs, batches):
-        total = backward(column, pieces, batch, total)
+    other_1 = other_core(mine_1)
+
+    batches = [[mine_0], [other_0], [mine_1, other_1]]
+    ready = [middle(exchange(forward(column, target, batch)), kernel) for batch in batches]
+    back_0 = exchange(ready[0])
+    back_2 = exchange(ready[2])
+    back_1 = exchange(after(ready[1], back_2))
+    total = backward(column, back_0, batches[0], None)
+    total = backward(column, back_2, batches[2], total)
+    total = backward(column, back_1, batches[1], total)
     return total[None]
 
 

time: 312 us -> 311 us (level)
  the two profiles are of different devices: /device:TPU:128 before, /device:TPU:32 now
where the time goes in v1:
time: 311 us; the launch traced here: 308 us
  waiting for transfers between devices  126 us (41%)
  starting transfers between devices  84 us (27%)
  Pallas kernels  53.5 us (17%)
  local copies, waits for them, and re-layouts  39.7 us (13%)
  other arithmetic  4.2 us (1%)
    all_to_all x6, waiting for transfers between devices, exchange(): return lax.all_to_all(pieces, 'grid', 0, 0, tiled=True)  86.9 us
    ppermute x30, starting transfers between devices, move(): return lax.ppermute(array, 'band', pairs)  50.6 us
    ppermute x30, waiting for transfers between devices, move(): return lax.ppermute(array, 'band', pairs)  39.1 us
    unnamed x108, local copies, waits for them, and re-layouts  35.3 us
    all_to_all x6, starting transfers between devices, exchange(): return lax.all_to_all(pieces, 'grid', 0, 0, tiled=True)  33.4 us
    pallas_call x3, Pallas kernels, backward(): pl.pallas_call(backward_body, in_specs=[SCALAR] + [VECTOR] * (1 + len(cut...  20 us
    pallas_call x3, Pallas kernels, middle(): pl.pallas_call(middle_body, in_specs=[VECTOR] * 4, out_specs=VECTOR, out_...  19 us
    pallas_call x3, Pallas kernels, forward(): pl.pallas_call(forward_body, in_specs=[SCALAR] + [VECTOR] * (len(cuts) +...  14.5 us
  transfers between devices with their start and end apart: 36, of which 20 were waited for; matrix products, arithmetic and copies ran while one was open for 1% of the time, Pallas kernels for 15%

profile of v1, /device:TPU:32, one launch (start us, length us, event | category | flops | bytes accessed | tf_op | source)
XLA Modules:
  0.0 308.0 jit_solution(12069246517478935371)
XLA Ops:
  3.5 4.2 %collective-permute-start.1 = (bf16[24,9216]{1,0:T(8,128)(2,1)}, bf16[24,9216]{1,0:T(8,128)(2,1)}, u32[]{:S(2)}, u32[]{:S(2)}) collective-permute-start(bf16[24,9216]{1,0:T(8,128)(2,1)} %get-tuple-element.19), channel_id=1, source_target_pairs={{0,16},{128,152},{1,17},{129,153},{2,18},{130,154},{3,19},{131,155... | collective-permute-start | bytes 1327112 | tf_op jit(solution)/shard_map/ppermute | solution.py:255
  12.4 5.0 %collective-permute-start = (bf16[24,9216]{1,0:T(8,128)(2,1)}, bf16[24,9216]{1,0:T(8,128)(2,1)}, u32[]{:S(2)}, u32[]{:S(2)}) collective-permute-start(bf16[24,9216]{1,0:T(8,128)(2,1)} %get-tuple-element.22), channel_id=1, source_target_pairs={{0,0},{128,136},{1,1},{129,137},{2,2},{130,138},{3,3},{131,139},{4... | collective-permute-start | bytes 1327112 | tf_op jit(solution)/shard_map/ppermute | solution.py:255
  35.4 10.1 %collective-permute-start.20 = (bf16[24,9216]{1,0:T(8,128)(2,1)S(1)}, bf16[24,9216]{1,0:T(8,128)(2,1)S(1)}, u32[]{:S(2)}, u32[]{:S(2)}) collective-permute-start(bf16[24,9216]{1,0:T(8,128)(2,1)S(1)} %add_add_fusion), channel_id=1, source_target_pairs={{0,192},{16,208},{32,224},{48,240},{136,72},{152,88},{168,104},{18... | collective-permute-start | bytes 1327112 | tf_op jit(solution)/shard_map/ppermute | solution.py:255
  51.4 6.3 %collective-permute-done.19 = bf16[24,9216]{1,0:T(8,128)(2,1)S(1)} collective-permute-done((bf16[24,9216]{1,0:T(8,128)(2,1)S(1)}, bf16[24,9216]{1,0:T(8,128)(2,1)S(1)}, u32[]{:S(2)}, u32[]{:S(2)}) %collective-permute-start.19) | collective-permute-done | bytes 442400 | tf_op jit(solution)/shard_map/ppermute | solution.py:255
  68.1 4.1 %forward_zy.5 = bf16[8,1,6,48,384]{4,3,2,1,0:T(8,128)(2,1)S(1)} custom-call(s32[1]{0:T(128)} %bitcast.column, bf16[24,36864]{1,0:T(8,128)(2,1)S(1)} %get-tuple-element.14.target, bf16[24,9216]{1,0:T(8,128)(2,1)S(1)} %maximum_add_fusion.refs_0_, bf16[24,9216]{1,0:T(8,128)(2,1)} %collective-permute-done.9.refs_1_, ...), custom_call_target="tpu_custom_call" | custom-call | flops 1400000000 | bytes 7000000 | tf_op jit(solution)/shard_map/forward_zy/pallas_call | solution.py:121
  73.4 5.9 %all-to-all-start.4 = ((bf16[8,1,6,48,384]{4,3,2,1,0:T(8,128)(2,1)}), bf16[8,1,6,48,384]{4,3,2,1,0:T(8,128)(2,1)S(1)}, u32[]{:S(2)}, u32[]{:S(2)}) async-start(bf16[8,1,6,48,384]{4,3,2,1,0:T(8,128)(2,1)} %copy-done.5), calls=%async_computation.4 | async-start | bytes 3538944 | tf_op jit(solution)/shard_map/all_to_all | solution.py:247
  84.8 17.7 %collective-permute-done.25.refs_3_ = bf16[24,9216]{1,0:T(8,128)(2,1)S(1)} collective-permute-done((bf16[24,9216]{1,0:T(8,128)(2,1)S(1)}, bf16[24,9216]{1,0:T(8,128)(2,1)S(1)}, u32[]{:S(2)}, u32[]{:S(2)}) %collective-permute-start.25) | collective-permute-done | bytes 442400 | tf_op jit(solution)/shard_map/ppermute | solution.py:255
  107.5 6.0 %forward_zy.4 = bf16[8,2,6,48,384]{4,3,2,1,0:T(8,128)(2,1)S(1)} custom-call(s32[1]{0:T(128)} %bitcast.column, bf16[24,36864]{1,0:T(8,128)(2,1)S(1)} %get-tuple-element.14.target, bf16[24,9216]{1,0:T(8,128)(2,1)S(1)} %maximum_add_fusion.1.refs_0_, bf16[24,9216]{1,0:T(8,128)(2,1)S(1)} %collective-permute-done.23.refs_1_, ...), custom_call_target="tpu_custom_call" | custom-call | flops 2800000000 | bytes 14000000 | tf_op jit(solution)/shard_map/forward_zy/pallas_call | solution.py:121
  122.9 5.7 %all-to-all-start.1 = ((bf16[8,2,6,48,384]{4,3,2,1,0:T(8,128)(2,1)}), bf16[8,2,6,48,384]{4,3,2,1,0:T(8,128)(2,1)}, u32[]{:S(2)}, u32[]{:S(2)}) async-start(bf16[8,2,6,48,384]{4,3,2,1,0:T(8,128)(2,1)} %copy-done.17), calls=%async_computation.1 | async-start | bytes 7077888 | tf_op jit(solution)/shard_map/all_to_all | solution.py:247
  134.4 4.3 %forward_zy.3 = bf16[8,1,6,48,384]{4,3,2,1,0:T(8,128)(2,1)} custom-call(s32[1]{0:T(128)} %bitcast.column, bf16[24,36864]{1,0:T(8,128)(2,1)S(1)} %get-tuple-element.14.target, bf16[24,9216]{1,0:T(8,128)(2,1)S(1)} %collective-permute-done.8.refs_0_, bf16[24,9216]{1,0:T(8,128)(2,1)S(1)} %collective-permute-done.10.refs_1_, ...), custom_call_target="tpu_custom_call" | custom-call | flops 1400000000 | bytes 7000000 | tf_op jit(solution)/shard_map/forward_zy/pallas_call | solution.py:121
  141.8 28.4 %all-to-all-done.1.pieces = bf16[8,2,6,48,384]{4,3,2,1,0:T(8,128)(2,1)} async-done(((bf16[8,2,6,48,384]{4,3,2,1,0:T(8,128)(2,1)}), bf16[8,2,6,48,384]{4,3,2,1,0:T(8,128)(2,1)}, u32[]{:S(2)}, u32[]{:S(2)}) %all-to-all-start.1) | async-done | bytes 3538976 | tf_op jit(solution)/shard_map/all_to_all | solution.py:247
  170.2 5.4 %all-to-all-start = ((bf16[8,1,6,48,384]{4,3,2,1,0:T(8,128)(2,1)}), bf16[8,1,6,48,384]{4,3,2,1,0:T(8,128)(2,1)}, u32[]{:S(2)}, u32[]{:S(2)}) async-start(bf16[8,1,6,48,384]{4,3,2,1,0:T(8,128)(2,1)} %forward_zy.3), calls=%async_computation | async-start | bytes 3538944 | tf_op jit(solution)/shard_map/all_to_all | solution.py:247
  178.5 9.8 %middle_x.4 = bf16[8,2,6,48,384]{4,3,2,1,0:T(8,128)(2,1)S(1)} custom-call(bf16[8,2,6,48,384]{4,3,2,1,0:T(8,128)(2,1)} %all-to-all-done.1.pieces, f32[12,192,384]{2,1,0:T(8,128)S(1)} %select_multiply_fusion.kernel, bf16[192,192]{1,0:T(8,128)(2,1)S(1)} %copy-done.21, bf16[192,192]{1,0:T(8,128)(2,1)S(1)} %copy-done.11), custom_call_target="tpu_custom_call" | custom-call | flops 2800000000 | bytes 14000000 | tf_op jit(solution)/shard_map/middle_x/pallas_call | solution.py:177
  190.1 7.3 %all-to-all-done.pieces = bf16[8,1,6,48,384]{4,3,2,1,0:T(8,128)(2,1)} async-done(((bf16[8,1,6,48,384]{4,3,2,1,0:T(8,128)(2,1)}), bf16[8,1,6,48,384]{4,3,2,1,0:T(8,128)(2,1)}, u32[]{:S(2)}, u32[]{:S(2)}) %all-to-all-start) | async-done | bytes 1769504 | tf_op jit(solution)/shard_map/all_to_all | solution.py:247
  197.5 5.6 %all-to-all-start.2 = ((bf16[8,2,6,48,384]{4,3,2,1,0:T(8,128)(2,1)}), bf16[8,2,6,48,384]{4,3,2,1,0:T(8,128)(2,1)}, u32[]{:S(2)}, u32[]{:S(2)}) async-start(bf16[8,2,6,48,384]{4,3,2,1,0:T(8,128)(2,1)} %copy-done), calls=%async_computation.2 | async-start | bytes 7077888 | tf_op jit(solution)/shard_map/all_to_all | solution.py:247
  211.5 31.4 %all-to-all-done.2.pieces = bf16[8,2,6,48,384]{4,3,2,1,0:T(8,128)(2,1)} async-done(((bf16[8,2,6,48,384]{4,3,2,1,0:T(8,128)(2,1)}), bf16[8,2,6,48,384]{4,3,2,1,0:T(8,128)(2,1)}, u32[]{:S(2)}, u32[]{:S(2)}) %all-to-all-start.2) | async-done | bytes 3538976 | tf_op jit(solution)/shard_map/all_to_all | solution.py:247
  242.9 5.4 %all-to-all-start.5 = ((bf16[8,1,6,48,384]{4,3,2,1,0:T(8,128)(2,1)}), bf16[8,1,6,48,384]{4,3,2,1,0:T(8,128)(2,1)}, u32[]{:S(2)}, u32[]{:S(2)}) async-start(bf16[8,1,6,48,384]{4,3,2,1,0:T(8,128)(2,1)} %copy-done.4), calls=%async_computation.5 | async-start | bytes 3538944 | tf_op jit(solution)/shard_map/all_to_all | solution.py:247
  250.1 5.4 %middle_x.3 = bf16[8,1,6,48,384]{4,3,2,1,0:T(8,128)(2,1)S(1)} custom-call(bf16[8,1,6,48,384]{4,3,2,1,0:T(8,128)(2,1)} %all-to-all-done.pieces, f32[12,192,384]{2,1,0:T(8,128)S(1)} %select_multiply_fusion.kernel, bf16[192,192]{1,0:T(8,128)(2,1)S(1)} %copy-done.23, bf16[192,192]{1,0:T(8,128)(2,1)S(1)} %copy-done.13), custom_call_target="tpu_custom_call" | custom-call | flops 1400000000 | bytes 7000000 | tf_op jit(solution)/shard_map/middle_x/pallas_call | solution.py:177
  256.7 12.6 %all-to-all-done.5.pieces = bf16[8,1,6,48,384]{4,3,2,1,0:T(8,128)(2,1)} async-done(((bf16[8,1,6,48,384]{4,3,2,1,0:T(8,128)(2,1)}), bf16[8,1,6,48,384]{4,3,2,1,0:T(8,128)(2,1)}, u32[]{:S(2)}, u32[]{:S(2)}) %all-to-all-start.5) | async-done | bytes 1769504 | tf_op jit(solution)/shard_map/all_to_all | solution.py:247
  269.3 5.4 %all-to-all-start.3 = ((bf16[8,1,6,48,384]{4,3,2,1,0:T(8,128)(2,1)}), bf16[8,1,6,48,384]{4,3,2,1,0:T(8,128)(2,1)}, u32[]{:S(2)}, u32[]{:S(2)}) async-start(bf16[8,1,6,48,384]{4,3,2,1,0:T(8,128)(2,1)} %copy-done.3), calls=%async_computation.3 | async-start | bytes 3538944 | tf_op jit(solution)/shard_map/all_to_all | solution.py:247
  274.8 4.9 %backward_yz.3.refs_8_ = f32[24,36864]{1,0:T(8,128)S(1)} custom-call(s32[1]{0:T(128)} %bitcast.column, bf16[8,1,6,48,384]{4,3,2,1,0:T(8,128)(2,1)} %all-to-all-done.5.pieces, bf16[24,9216]{1,0:T(8,128)(2,1)S(1)} %copy-done.10, bf16[24,9216]{1,0:T(8,128)(2,1)} %collective-permute-done.9.refs_1_, bf16[24,9216]{1,0:T(8,128)(2,1)} %collective-permute-done.11.refs_2_, ...), custom_call_target="tpu_custom_call" | custom-call | flops 1400000000 | bytes 7000000 | tf_op jit(solution)/shard_map/backward_yz/pallas_call | solution.py:234
  279.9 8.5 %backward_yz.4.refs_4_ = f32[24,36864]{1,0:T(8,128)S(1)} custom-call(s32[1]{0:T(128)} %bitcast.column, bf16[8,2,6,48,384]{4,3,2,1,0:T(8,128)(2,1)} %all-to-all-done.2.pieces, bf16[24,9216]{1,0:T(8,128)(2,1)S(1)} %copy-done.36, bf16[24,9216]{1,0:T(8,128)(2,1)S(1)} %copy-done.44, bf16[24,9216]{1,0:T(8,128)(2,1)S(1)} %copy-done.42, ...), custom_call_target="tpu_custom_call" | custom-call | flops 2800000000 | bytes 14000000 | tf_op jit(solution)/shard_map/backward_yz/pallas_call | solution.py:234
  288.4 7.0 %all-to-all-done.3.pieces = bf16[8,1,6,48,384]{4,3,2,1,0:T(8,128)(2,1)} async-done(((bf16[8,1,6,48,384]{4,3,2,1,0:T(8,128)(2,1)}), bf16[8,1,6,48,384]{4,3,2,1,0:T(8,128)(2,1)}, u32[]{:S(2)}, u32[]{:S(2)}) %all-to-all-start.3) | async-done | bytes 1769504 | tf_op jit(solution)/shard_map/all_to_all | solution.py:247
  301.4 6.6 %backward_yz.5 = f32[24,36864]{1,0:T(8,128)} custom-call(s32[1]{0:T(128)} %bitcast.column, bf16[8,1,6,48,384]{4,3,2,1,0:T(8,128)(2,1)} %all-to-all-done.3.pieces, bf16[24,9216]{1,0:T(8,128)(2,1)S(1)} %copy-done.28, bf16[24,9216]{1,0:T(8,128)(2,1)S(1)} %copy-done.34, bf16[24,9216]{1,0:T(8,128)(2,1)S(1)} %copy-done.32, bf16[24,9216]{1,0:T(8,128)(2,1)S(1)} %copy-done.30, ...), custom_call_target="tpu_custom_call" | custom-call | flops 1400000000 | bytes 7000000 | tf_op jit(solution)/shard_map/backward_yz/pallas_call | solution.py:234
  (185 shorter events, 94.2 us)
Async XLA Ops:
  3.5 14.0 %collective-permute-start.1 = (bf16[24,9216]{1,0:T(8,128)(2,1)}, bf16[24,9216]{1,0:T(8,128)(2,1)}, u32[]{:S(2)}, u32[]{:S(2)}) collective-permute-start(bf16[24,9216]{1,0:T(8,128)(2,1)} %get-tuple-element.19), channel_id=1, source_target_pairs={{0,16},{128,152},{1,17},{129,153},{2,18},{130,154},{3,19},{131,155... | collective-permute-start | bytes 1327112 | tf_op jit(solution)/shard_map/ppermute | solution.py:255
  7.7 9.8 %collective-permute-start.3 = (bf16[24,9216]{1,0:T(8,128)(2,1)}, bf16[24,9216]{1,0:T(8,128)(2,1)}, u32[]{:S(2)}, u32[]{:S(2)}) collective-permute-start(bf16[24,9216]{1,0:T(8,128)(2,1)} %get-tuple-element.20), channel_id=1, source_target_pairs={{0,48},{128,184},{1,49},{129,185},{2,50},{130,186},{3,51},{131,187... | collective-permute-start | bytes 1327112 | tf_op jit(solution)/shard_map/ppermute | solution.py:255
  19.3 10.1 %collective-permute-start.5 = (bf16[24,9216]{1,0:T(8,128)(2,1)S(1)}, bf16[24,9216]{1,0:T(8,128)(2,1)S(1)}, u32[]{:S(2)}, u32[]{:S(2)}) collective-permute-start(bf16[24,9216]{1,0:T(8,128)(2,1)S(1)} %add_add_fusion.1), channel_id=1, source_target_pairs={{0,192},{16,208},{32,224},{48,240},{136,72},{152,88},{168,104},{18... | collective-permute-start | bytes 1327112 | tf_op jit(solution)/shard_map/ppermute | solution.py:255
  20.6 11.4 %collective-permute-start.4 = (bf16[24,9216]{1,0:T(8,128)(2,1)S(1)}, bf16[24,9216]{1,0:T(8,128)(2,1)S(1)}, u32[]{:S(2)}, u32[]{:S(2)}) collective-permute-start(bf16[24,9216]{1,0:T(8,128)(2,1)S(1)} %add_add_fusion.1), channel_id=1, source_target_pairs={{0,64},{16,80},{32,96},{48,112},{136,200},{152,216},{168,232},{184... | collective-permute-start | bytes 1327112 | tf_op jit(solution)/shard_map/ppermute | solution.py:255
  22.0 10.9 %collective-permute-start.16 = (bf16[24,9216]{1,0:T(8,128)(2,1)S(1)}, bf16[24,9216]{1,0:T(8,128)(2,1)S(1)}, u32[]{:S(2)}, u32[]{:S(2)}) collective-permute-start(bf16[24,9216]{1,0:T(8,128)(2,1)S(1)} %get-tuple-element.15), channel_id=1, source_target_pairs={{0,16},{128,152},{1,17},{129,153},{2,18},{130,154},{3,19},{131,155... | collective-permute-start | bytes 1327112 | tf_op jit(solution)/shard_map/ppermute | solution.py:255
  23.4 10.3 %collective-permute-start.18 = (bf16[24,9216]{1,0:T(8,128)(2,1)S(1)}, bf16[24,9216]{1,0:T(8,128)(2,1)S(1)}, u32[]{:S(2)}, u32[]{:S(2)}) collective-permute-start(bf16[24,9216]{1,0:T(8,128)(2,1)S(1)} %get-tuple-element.16), channel_id=1, source_target_pairs={{0,48},{128,184},{1,49},{129,185},{2,50},{130,186},{3,51},{131,187... | collective-permute-start | bytes 1327112 | tf_op jit(solution)/shard_map/ppermute | solution.py:255
  26.3 8.8 %collective-permute-start.17 = (bf16[24,9216]{1,0:T(8,128)(2,1)S(1)}, bf16[24,9216]{1,0:T(8,128)(2,1)S(1)}, u32[]{:S(2)}, u32[]{:S(2)}) collective-permute-start(bf16[24,9216]{1,0:T(8,128)(2,1)S(1)} %get-tuple-element.17), channel_id=1, source_target_pairs={{0,32},{128,168},{1,33},{129,169},{2,34},{130,170},{3,35},{131,171... | collective-permute-start | bytes 1327112 | tf_op jit(solution)/shard_map/ppermute | solution.py:255
  35.4 16.0 %collective-permute-start.20 = (bf16[24,9216]{1,0:T(8,128)(2,1)S(1)}, bf16[24,9216]{1,0:T(8,128)(2,1)S(1)}, u32[]{:S(2)}, u32[]{:S(2)}) collective-permute-start(bf16[24,9216]{1,0:T(8,128)(2,1)S(1)} %add_add_fusion), channel_id=1, source_target_pairs={{0,192},{16,208},{32,224},{48,240},{136,72},{152,88},{168,104},{18... | collective-permute-start | bytes 1327112 | tf_op jit(solution)/shard_map/ppermute | solution.py:255
  45.5 12.2 %collective-permute-start.19 = (bf16[24,9216]{1,0:T(8,128)(2,1)S(1)}, bf16[24,9216]{1,0:T(8,128)(2,1)S(1)}, u32[]{:S(2)}, u32[]{:S(2)}) collective-permute-start(bf16[24,9216]{1,0:T(8,128)(2,1)S(1)} %add_add_fusion), channel_id=1, source_target_pairs={{0,64},{16,80},{32,96},{48,112},{136,200},{152,216},{168,232},{184... | collective-permute-start | bytes 1327112 | tf_op jit(solution)/shard_map/ppermute | solution.py:255
  47.2 18.7 %collective-permute-start.13 = (bf16[24,9216]{1,0:T(8,128)(2,1)S(1)}, bf16[24,9216]{1,0:T(8,128)(2,1)S(1)}, u32[]{:S(2)}, u32[]{:S(2)}) collective-permute-start(bf16[24,9216]{1,0:T(8,128)(2,1)S(1)} %maximum_add_fusion.refs_0_), channel_id=1, source_target_pairs={{0,48},{8,56},{16,32},{24,40},{32,16},{40,24},{48,0},{56,8},{64,11... | collective-permute-start | bytes 1327112 | tf_op jit(solution)/shard_map/ppermute | solution.py:255
  47.3 18.6 %collective-permute-start.11 = (bf16[24,9216]{1,0:T(8,128)(2,1)S(1)}, bf16[24,9216]{1,0:T(8,128)(2,1)}, u32[]{:S(2)}, u32[]{:S(2)}) collective-permute-start(bf16[24,9216]{1,0:T(8,128)(2,1)S(1)} %maximum_add_fusion.refs_0_), channel_id=1, source_target_pairs={{0,32},{8,40},{16,48},{24,56},{32,0},{40,8},{48,16},{56,24},{64,96... | collective-permute-start | bytes 1327112 | tf_op jit(solution)/shard_map/ppermute | solution.py:255
  47.4 20.7 %collective-permute-start.9 = (bf16[24,9216]{1,0:T(8,128)(2,1)S(1)}, bf16[24,9216]{1,0:T(8,128)(2,1)}, u32[]{:S(2)}, u32[]{:S(2)}) collective-permute-start(bf16[24,9216]{1,0:T(8,128)(2,1)S(1)} %maximum_add_fusion.refs_0_), channel_id=1, source_target_pairs={{0,16},{8,24},{16,0},{24,8},{32,48},{40,56},{48,32},{56,40},{64,80... | collective-permute-start | bytes 1327112 | tf_op jit(solution)/shard_map/ppermute | solution.py:255
  59.3 20.0 %collective-permute-start.21 = (bf16[24,4608]{1,0:T(8,128)(2,1)}, bf16[24,4608]{1,0:T(8,128)(2,1)}, u32[]{:S(2)}, u32[]{:S(2)}) collective-permute-start(bf16[24,4608]{1,0:T(8,128)(2,1)} %get-tuple-element.23), channel_id=1, source_target_pairs={{64,128},{80,144},{96,160},{112,176},{200,8},{216,24},{232,40},{24... | collective-permute-start | bytes 663560 | tf_op jit(solution)/shard_map/ppermute | solution.py:255
  60.7 18.7 %collective-permute-start.22 = (bf16[24,4608]{1,0:T(8,128)(2,1)}, bf16[24,4608]{1,0:T(8,128)(2,1)}, u32[]{:S(2)}, u32[]{:S(2)}) collective-permute-start(bf16[24,4608]{1,0:T(8,128)(2,1)} %get-tuple-element.24), channel_id=1, source_target_pairs={{192,128},{208,144},{224,160},{240,176},{72,8},{88,24},{104,40},{1... | collective-permute-start | bytes 663560 | tf_op jit(solution)/shard_map/ppermute | solution.py:255
  73.4 48.2 %all-to-all-start.4 = ((bf16[8,1,6,48,384]{4,3,2,1,0:T(8,128)(2,1)}), bf16[8,1,6,48,384]{4,3,2,1,0:T(8,128)(2,1)S(1)}, u32[]{:S(2)}, u32[]{:S(2)}) async-start(bf16[8,1,6,48,384]{4,3,2,1,0:T(8,128)(2,1)} %copy-done.5), calls=%async_computation.4 | async-start | bytes 3538944 | tf_op jit(solution)/shard_map/all_to_all | solution.py:247
  80.6 21.9 %collective-permute-start.25 = (bf16[24,9216]{1,0:T(8,128)(2,1)S(1)}, bf16[24,9216]{1,0:T(8,128)(2,1)S(1)}, u32[]{:S(2)}, u32[]{:S(2)}) collective-permute-start(bf16[24,9216]{1,0:T(8,128)(2,1)S(1)} %maximum_add_fusion.1.refs_0_), channel_id=1, source_target_pairs={{0,48},{8,56},{16,32},{24,40},{32,16},{40,24},{48,0},{56,8},{64,11... | collective-permute-start | bytes 1327112 | tf_op jit(solution)/shard_map/ppermute | solution.py:255
  82.6 20.0 %collective-permute-start.24 = (bf16[24,9216]{1,0:T(8,128)(2,1)S(1)}, bf16[24,9216]{1,0:T(8,128)(2,1)S(1)}, u32[]{:S(2)}, u32[]{:S(2)}) collective-permute-start(bf16[24,9216]{1,0:T(8,128)(2,1)S(1)} %maximum_add_fusion.1.refs_0_), channel_id=1, source_target_pairs={{0,32},{8,40},{16,48},{24,56},{32,0},{40,8},{48,16},{56,24},{64,96... | collective-permute-start | bytes 1327112 | tf_op jit(solution)/shard_map/ppermute | solution.py:255
  84.7 18.5 %collective-permute-start.23 = (bf16[24,9216]{1,0:T(8,128)(2,1)S(1)}, bf16[24,9216]{1,0:T(8,128)(2,1)S(1)}, u32[]{:S(2)}, u32[]{:S(2)}) collective-permute-start(bf16[24,9216]{1,0:T(8,128)(2,1)S(1)} %maximum_add_fusion.1.refs_0_), channel_id=1, source_target_pairs={{0,16},{8,24},{16,0},{24,8},{32,48},{40,56},{48,32},{56,40},{64,80... | collective-permute-start | bytes 1327112 | tf_op jit(solution)/shard_map/ppermute | solution.py:255
  84.8 18.5 %collective-permute-start.26 = (bf16[24,9216]{1,0:T(8,128)(2,1)S(1)}, bf16[24,9216]{1,0:T(8,128)(2,1)S(1)}, u32[]{:S(2)}, u32[]{:S(2)}) collective-permute-start(bf16[24,9216]{1,0:T(8,128)(2,1)S(1)} %maximum_add_fusion.1.refs_0_), channel_id=1, source_target_pairs={{0,8},{8,0},{16,24},{24,16},{32,40},{40,32},{48,56},{56,48},{64,72... | collective-permute-start | bytes 1327112 | tf_op jit(solution)/shard_map/ppermute | solution.py:255
  122.9 47.3 %all-to-all-start.1 = ((bf16[8,2,6,48,384]{4,3,2,1,0:T(8,128)(2,1)}), bf16[8,2,6,48,384]{4,3,2,1,0:T(8,128)(2,1)}, u32[]{:S(2)}, u32[]{:S(2)}) async-start(bf16[8,2,6,48,384]{4,3,2,1,0:T(8,128)(2,1)} %copy-done.17), calls=%async_computation.1 | async-start | bytes 7077888 | tf_op jit(solution)/shard_map/all_to_all | solution.py:247
  170.2 27.2 %all-to-all-start = ((bf16[8,1,6,48,384]{4,3,2,1,0:T(8,128)(2,1)}), bf16[8,1,6,48,384]{4,3,2,1,0:T(8,128)(2,1)}, u32[]{:S(2)}, u32[]{:S(2)}) async-start(bf16[8,1,6,48,384]{4,3,2,1,0:T(8,128)(2,1)} %forward_zy.3), calls=%async_computation | async-start | bytes 3538944 | tf_op jit(solution)/shard_map/all_to_all | solution.py:247
  197.5 45.4 %all-to-all-start.2 = ((bf16[8,2,6,48,384]{4,3,2,1,0:T(8,128)(2,1)}), bf16[8,2,6,48,384]{4,3,2,1,0:T(8,128)(2,1)}, u32[]{:S(2)}, u32[]{:S(2)}) async-start(bf16[8,2,6,48,384]{4,3,2,1,0:T(8,128)(2,1)} %copy-done), calls=%async_computation.2 | async-start | bytes 7077888 | tf_op jit(solution)/shard_map/all_to_all | solution.py:247
  242.9 26.4 %all-to-all-start.5 = ((bf16[8,1,6,48,384]{4,3,2,1,0:T(8,128)(2,1)}), bf16[8,1,6,48,384]{4,3,2,1,0:T(8,128)(2,1)}, u32[]{:S(2)}, u32[]{:S(2)}) async-start(bf16[8,1,6,48,384]{4,3,2,1,0:T(8,128)(2,1)} %copy-done.4), calls=%async_computation.5 | async-start | bytes 3538944 | tf_op jit(solution)/shard_map/all_to_all | solution.py:247
  269.3 26.1 %all-to-all-start.3 = ((bf16[8,1,6,48,384]{4,3,2,1,0:T(8,128)(2,1)}), bf16[8,1,6,48,384]{4,3,2,1,0:T(8,128)(2,1)}, u32[]{:S(2)}, u32[]{:S(2)}) async-start(bf16[8,1,6,48,384]{4,3,2,1,0:T(8,128)(2,1)} %copy-done.3), calls=%async_computation.3 | async-start | bytes 3538944 | tf_op jit(solution)/shard_map/all_to_all | solution.py:247
  (66 other events, 315.7 us)

commit v2 on v1

--- a/solution.py
+++ b/solution.py
@@ -17,6 +17,7 @@
 PER_CUT = DUOS // 4
 PIECE = (QUADS, 2 * ROWS, 384)
 VECTOR = pl.BlockSpec(memory_space=pltpu.VMEM)
+FAR = pl.BlockSpec(memory_space=pl.ANY)
 SCALAR = pl.BlockSpec(memory_space=pltpu.SMEM)
 F32 = jnp.float32
 BF16 = jnp.bfloat16
@@ -186,10 +187,19 @@
     )(pieces, kernel, jnp.asarray(X_TABLE, BF16), jnp.asarray(X_BACK, BF16))
 
 
-def backward_body(column, pieces, *refs):
-    pairs = pieces.shape[1]
-    sources, refs = refs[: 4 * pairs], refs[4 * pairs :]
-    (total, y_table, z_tables, out), lots = ((None,) + refs[:3], refs[3:]) if len(refs) == 6 else (refs[:4], refs[4:])
+def backward_body(column, far_pieces, *refs):
+    pairs = far_pieces.shape[1]
+    far_sources, refs = refs[: 4 * pairs], refs[4 * pairs :]
+    total = refs[0] if len(refs) == 9 + 4 * pairs else None
+    y_table, z_tables, out, *refs = refs[total is not None :]
+    lots, (pieces, arrived), sources = refs[:3], refs[3:5], refs[5:]
+    copies = [pltpu.make_async_copy(far_pieces, pieces, arrived.at[0])]
+    copies += [
+        pltpu.make_async_copy(far, near, arrived.at[1 + i]) for i, (far, near) in enumerate(zip(far_sources, sources))
+    ]
+    for copy in copies:
+        copy.start()
+    copies[0].wait()
 
     for which in range(pairs):
 
@@ -216,6 +226,7 @@
 
         for slot in range(4):
             source = sources[which * 4 + slot]
+            copies[1 + which * 4 + slot].wait()
 
             def gather(part, carry, source=source, slot=slot, base=base):
                 duo = (column[0] ^ slot) * PER_CUT + part
@@ -233,11 +244,13 @@
     cuts = [cut for source in sources for cut in source]
     return pl.pallas_call(
         backward_body,
-        in_specs=[SCALAR] + [VECTOR] * (1 + len(cuts) + 2 + (total is not None)),
+        in_specs=[SCALAR] + [FAR] * (1 + len(cuts)) + [VECTOR] * (2 + (total is not None)),
         out_specs=VECTOR,
         out_shape=jax.ShapeDtypeStruct((ROWS, CELLS), F32),
-        scratch_shapes=[pltpu.VMEM((ROWS * PITCH, 128), F32)] * 3,
-        compiler_params=pltpu.CompilerParams(vmem_limit_bytes=16 * 2**20),
+        scratch_shapes=[pltpu.VMEM((ROWS * PITCH, 128), F32)] * 3
+        + [pltpu.VMEM(pieces.shape, BF16), pltpu.SemaphoreType.DMA((1 + len(cuts),))]
+        + [pltpu.VMEM(cut.shape, BF16) for cut in cuts],
+        compiler_params=pltpu.CompilerParams(vmem_limit_bytes=24 * 2**20),
         cost_estimate=cost(len(sources)),
         name="backward_yz",
     )(column, pieces, *cuts, *([] if total is None else [total]), jnp.asarray(Y_BACK, BF16), jnp.asarray(Z_BACKS, BF16))
@@ -308,22 +321,16 @@
 
     cut_0 = scatter(orbitals[0])
     cut_1 = scatter(after(orbitals[1], cut_0))
-    full_0 = beyond(beside(cut_0, is_root))
-    mine_0 = gather_x(full_0)
-    other_0 = other_core(mine_0)
-    full_1 = beyond(beside(after(cut_1, full_0), is_root))
-    mine_1 = gather_x(after(full_1, *mine_0))
-    other_1 = other_core(mine_1)
-
-    batches = [[mine_0], [other_0], [mine_1, other_1]]
-    ready = [middle(exchange(forward(column, target, batch)), kernel) for batch in batches]
-    back_0 = exchange(ready[0])
-    back_2 = exchange(ready[2])
-    back_1 = exchange(after(ready[1], back_2))
-    total = backward(column, back_0, batches[0], None)
-    total = backward(column, back_2, batches[2], total)
-    total = backward(column, back_1, batches[1], total)
-    return total[None]
+    mine_0 = gather_x(beyond(beside(cut_0, is_root)))
+    batch_0 = [mine_0, other_core(mine_0)]
+    pieces_0 = forward(column, target, batch_0)
+    mine_1 = gather_x(beyond(beside(after(cut_1, pieces_0), is_root)))
+    batch_1 = [mine_1, other_core(mine_1)]
+    pieces_1 = forward(column, target, batch_1)
+    back_0 = exchange(middle(exchange(pieces_0), kernel))
+    back_1 = exchange(middle(exchange(pieces_1), kernel))
+    total = backward(column, back_0, batch_0, None)
+    return backward(column, back_1, batch_1, total)[None]
 
 
 def solution(mesh):

time: 311 us -> 326 us (1.048)
  starting transfers between devices: 84 us -> 107 us
  waiting for transfers between devices: 126 us -> 111 us
  local copies, waits for them, and re-layouts: 39.7 us -> 47.8 us
  Pallas kernels: 53.5 us -> 48.6 us
    ppermute x30, starting transfers between devices: 50.6 us -> 84.8 us  [move(): return lax.ppermute(array, 'band', pairs)]
    all_to_all x6 -> x4, starting transfers between devices: 33.4 us -> 22.2 us  [exchange(): return lax.all_to_all(pieces, 'grid', 0, 0, tiled=True)]
    all_to_all x6 -> x4, waiting for transfers between devices: 86.9 us -> 77.2 us  [exchange(): return lax.all_to_all(pieces, 'grid', 0, 0, tiled=True)]
    unnamed x108 -> x112, local copies, waits for them, and re-layouts: 35.3 us -> 44.4 us
    ppermute x30, waiting for transfers between devices: 39.1 us -> 34.3 us  [move(): return lax.ppermute(array, 'band', pairs)]
    pallas_call x3 -> x2, Pallas kernels: 14.5 us -> 12.1 us  [forward(): pl.pallas_call(forward_body, in_specs=[SCALAR] + [VECTOR] * (len(cuts) +...]
    pallas_call x3 -> x2, Pallas kernels: 19 us -> 17.5 us  [middle(): pl.pallas_call(middle_body, in_specs=[VECTOR] * 4, out_specs=VECTOR, out_...]
    pallas_call x3 -> x2, Pallas kernels: 20 us -> 19 us  [backward(): pl.pallas_call(backward_body, in_specs=[SCALAR] + [FAR] * (1 + len(cuts))...]
  transfers between devices with their start and end apart: 36 -> 34, of which waited for: 20 -> 14; matrix products, arithmetic and copies ran while one was open for 1% -> 2% of each run, Pallas kernels for 15% -> 10%
where the time goes in v2:
time: 326 us; the launch traced here: 323 us
  waiting for transfers between devices  111 us (34%)
  starting transfers between devices  107 us (33%)
  Pallas kernels  48.6 us (15%)
  local copies, waits for them, and re-layouts  47.8 us (15%)
  other arithmetic  7.3 us (2%)
    ppermute x30, starting transfers between devices, move(): return lax.ppermute(array, 'band', pairs)  84.8 us
    all_to_all x4, waiting for transfers between devices, exchange(): return lax.all_to_all(pieces, 'grid', 0, 0, tiled=True)  77.2 us
    unnamed x112, local copies, waits for them, and re-layouts  44.4 us
    ppermute x30, waiting for transfers between devices, move(): return lax.ppermute(array, 'band', pairs)  34.3 us
    all_to_all x4, starting transfers between devices, exchange(): return lax.all_to_all(pieces, 'grid', 0, 0, tiled=True)  22.2 us
    pallas_call x2, Pallas kernels, backward(): pl.pallas_call(backward_body, in_specs=[SCALAR] + [FAR] * (1 + len(cuts))...  19 us
    pallas_call x2, Pallas kernels, middle(): pl.pallas_call(middle_body, in_specs=[VECTOR] * 4, out_specs=VECTOR, out_...  17.5 us
    pallas_call x2, Pallas kernels, forward(): pl.pallas_call(forward_body, in_specs=[SCALAR] + [VECTOR] * (len(cuts) +...  12.1 us
  transfers between devices with their start and end apart: 34, of which 14 were waited for; matrix products, arithmetic and copies ran while one was open for 2% of the time, Pallas kernels for 10%

profile of v2, /device:TPU:32, one launch (start us, length us, event | category | flops | bytes accessed | tf_op | source)
XLA Modules:
  0.0 323.0 jit_solution(12593144742678951563)
XLA Ops:
  2.4 3.4 %collective-permute-start.1 = (bf16[24,9216]{1,0:T(8,128)(2,1)S(1)}, bf16[24,9216]{1,0:T(8,128)(2,1)S(1)}, u32[]{:S(2)}, u32[]{:S(2)}) collective-permute-start(bf16[24,9216]{1,0:T(8,128)(2,1)S(1)} %get-tuple-element.15), channel_id=1, source_target_pairs={{0,16},{128,152},{1,17},{129,153},{2,18},{130,154},{3,19},{131,155... | collective-permute-start | bytes 1327112 | tf_op jit(solution)/shard_map/ppermute | solution.py:268
  13.6 2.8 collective-permute-done.2
  21.3 3.4 %collective-permute-done.9 = bf16[24,9216]{1,0:T(8,128)(2,1)} collective-permute-done((bf16[24,9216]{1,0:T(8,128)(2,1)}, bf16[24,9216]{1,0:T(8,128)(2,1)}, u32[]{:S(2)}, u32[]{:S(2)}) %collective-permute-start.9) | collective-permute-done | bytes 442400 | tf_op jit(solution)/shard_map/ppermute | solution.py:268
  24.6 6.3 %collective-permute-done.8 = bf16[24,9216]{1,0:T(8,128)(2,1)} collective-permute-done((bf16[24,9216]{1,0:T(8,128)(2,1)}, bf16[24,9216]{1,0:T(8,128)(2,1)}, u32[]{:S(2)}, u32[]{:S(2)}) %collective-permute-start.8) | collective-permute-done | bytes 442400 | tf_op jit(solution)/shard_map/ppermute | solution.py:268
  38.3 4.5 %collective-permute-start.6 = (bf16[24,9216]{1,0:T(8,128)(2,1)}, bf16[24,9216]{1,0:T(8,128)(2,1)}, u32[]{:S(2)}, u32[]{:S(2)}) collective-permute-start(bf16[24,9216]{1,0:T(8,128)(2,1)} %get-tuple-element.13), channel_id=1, source_target_pairs={{0,32},{128,168},{1,33},{129,169},{2,34},{130,170},{3,35},{131,171... | collective-permute-start | bytes 1327112 | tf_op jit(solution)/shard_map/ppermute | solution.py:268
  43.1 4.0 %collective-permute-start.12 = (bf16[24,9216]{1,0:T(8,128)(2,1)S(1)}, bf16[24,9216]{1,0:T(8,128)(2,1)S(1)}, u32[]{:S(2)}, u32[]{:S(2)}) collective-permute-start(bf16[24,9216]{1,0:T(8,128)(2,1)S(1)} %maximum_add_fusion.refs_0_), channel_id=1, source_target_pairs={{0,16},{8,24},{16,0},{24,8},{32,48},{40,56},{48,32},{56,40},{64,80... | collective-permute-start | bytes 1327112 | tf_op jit(solution)/shard_map/ppermute | solution.py:268
  47.9 5.0 %collective-permute-start.4 = (bf16[24,9216]{1,0:T(8,128)(2,1)}, bf16[24,9216]{1,0:T(8,128)(2,1)}, u32[]{:S(2)}, u32[]{:S(2)}) collective-permute-start(bf16[24,9216]{1,0:T(8,128)(2,1)} %get-tuple-element.14), channel_id=1, source_target_pairs={{0,0},{128,136},{1,1},{129,137},{2,2},{130,138},{3,3},{131,139},{4... | collective-permute-start | bytes 1327112 | tf_op jit(solution)/shard_map/ppermute | solution.py:268
  52.9 10.7 %collective-permute-done.14.refs_3_ = bf16[24,9216]{1,0:T(8,128)(2,1)S(1)} collective-permute-done((bf16[24,9216]{1,0:T(8,128)(2,1)S(1)}, bf16[24,9216]{1,0:T(8,128)(2,1)S(1)}, u32[]{:S(2)}, u32[]{:S(2)}) %collective-permute-start.14) | collective-permute-done | bytes 442400 | tf_op jit(solution)/shard_map/ppermute | solution.py:268
  64.1 2.9 collective-permute-done.12.refs_1_
  71.6 6.0 %forward_zy.2 = bf16[8,2,6,48,384]{4,3,2,1,0:T(8,128)(2,1)S(1)} custom-call(s32[1]{0:T(128)} %bitcast.column, bf16[24,36864]{1,0:T(8,128)(2,1)S(1)} %get-tuple-element.10.target, bf16[24,9216]{1,0:T(8,128)(2,1)S(1)} %maximum_add_fusion.refs_0_, bf16[24,9216]{1,0:T(8,128)(2,1)S(1)} %collective-permute-done.12.refs_1_, ...), custom_call_target="tpu_custom_call" | custom-call | flops 2800000000 | bytes 14000000 | tf_op jit(solution)/shard_map/forward_zy/pallas_call | solution.py:122
  81.9 5.9 %all-to-all-start.2 = ((bf16[8,2,6,48,384]{4,3,2,1,0:T(8,128)(2,1)}), bf16[8,2,6,48,384]{4,3,2,1,0:T(8,128)(2,1)S(1)}, u32[]{:S(2)}, u32[]{:S(2)}) async-start(bf16[8,2,6,48,384]{4,3,2,1,0:T(8,128)(2,1)} %copy-done.8), calls=%async_computation.2 | async-start | bytes 7077888 | tf_op jit(solution)/shard_map/all_to_all | solution.py:260
  97.3 34.6 %collective-permute-start.26 = (bf16[24,9216]{1,0:T(8,128)(2,1)S(1)}, bf16[24,9216]{1,0:T(8,128)(2,1)S(1)}, u32[]{:S(2)}, u32[]{:S(2)}) collective-permute-start(bf16[24,9216]{1,0:T(8,128)(2,1)S(1)} %maximum_add_fusion.1.refs_0_), channel_id=1, source_target_pairs={{0,8},{8,0},{16,24},{24,16},{32,40},{40,32},{48,56},{56,48},{64,72... | collective-permute-start | bytes 1327112 | tf_op jit(solution)/shard_map/ppermute | solution.py:268
  131.9 9.4 %collective-permute-start.29 = (bf16[24,9216]{1,0:T(8,128)(2,1)S(1)}, bf16[24,9216]{1,0:T(8,128)(2,1)S(1)}, u32[]{:S(2)}, u32[]{:S(2)}) collective-permute-start(bf16[24,9216]{1,0:T(8,128)(2,1)S(1)} %collective-permute-done.25.refs_3_), channel_id=1, source_target_pairs={{0,8},{8,0},{16,24},{24,16},{32,40},{40,32},{48,56},{56,48},{64,72... | collective-permute-start | bytes 1327112 | tf_op jit(solution)/shard_map/ppermute | solution.py:268
  144.0 6.0 %forward_zy.3 = bf16[8,2,6,48,384]{4,3,2,1,0:T(8,128)(2,1)S(1)} custom-call(s32[1]{0:T(128)} %bitcast.column, bf16[24,36864]{1,0:T(8,128)(2,1)S(1)} %copy-done.7, bf16[24,9216]{1,0:T(8,128)(2,1)S(1)} %maximum_add_fusion.1.refs_0_, bf16[24,9216]{1,0:T(8,128)(2,1)S(1)} %collective-permute-done.23.refs_1_, ...), custom_call_target="tpu_custom_call" | custom-call | flops 2800000000 | bytes 14000000 | tf_op jit(solution)/shard_map/forward_zy/pallas_call | solution.py:122
  159.8 5.9 %all-to-all-start = ((bf16[8,2,6,48,384]{4,3,2,1,0:T(8,128)(2,1)}), bf16[8,2,6,48,384]{4,3,2,1,0:T(8,128)(2,1)}, u32[]{:S(2)}, u32[]{:S(2)}) async-start(bf16[8,2,6,48,384]{4,3,2,1,0:T(8,128)(2,1)} %copy-done.9), calls=%async_computation | async-start | bytes 7077888 | tf_op jit(solution)/shard_map/all_to_all | solution.py:260
  169.5 7.8 %middle_x.3 = bf16[8,2,6,48,384]{4,3,2,1,0:T(8,128)(2,1)S(1)} custom-call(bf16[8,2,6,48,384]{4,3,2,1,0:T(8,128)(2,1)S(1)} %copy-done.3, f32[12,192,384]{2,1,0:T(8,128)S(1)} %select_multiply_fusion.kernel, bf16[192,192]{1,0:T(8,128)(2,1)S(1)} %copy-done.50, bf16[192,192]{1,0:T(8,128)(2,1)S(1)} %copy-done.16), custom_call_target="tpu_custom_call" | custom-call | flops 2800000000 | bytes 14000000 | tf_op jit(solution)/shard_map/middle_x/pallas_call | solution.py:178
  179.0 28.8 %all-to-all-done.pieces = bf16[8,2,6,48,384]{4,3,2,1,0:T(8,128)(2,1)} async-done(((bf16[8,2,6,48,384]{4,3,2,1,0:T(8,128)(2,1)}), bf16[8,2,6,48,384]{4,3,2,1,0:T(8,128)(2,1)}, u32[]{:S(2)}, u32[]{:S(2)}) %all-to-all-start) | async-done | bytes 3538976 | tf_op jit(solution)/shard_map/all_to_all | solution.py:260
  207.8 5.6 %all-to-all-start.3 = ((bf16[8,2,6,48,384]{4,3,2,1,0:T(8,128)(2,1)}), bf16[8,2,6,48,384]{4,3,2,1,0:T(8,128)(2,1)}, u32[]{:S(2)}, u32[]{:S(2)}) async-start(bf16[8,2,6,48,384]{4,3,2,1,0:T(8,128)(2,1)} %copy-done.5), calls=%async_computation.3 | async-start | bytes 7077888 | tf_op jit(solution)/shard_map/all_to_all | solution.py:260
  215.2 9.8 %middle_x.2 = bf16[8,2,6,48,384]{4,3,2,1,0:T(8,128)(2,1)S(1)} custom-call(bf16[8,2,6,48,384]{4,3,2,1,0:T(8,128)(2,1)} %all-to-all-done.pieces, f32[12,192,384]{2,1,0:T(8,128)S(1)} %select_multiply_fusion.kernel, bf16[192,192]{1,0:T(8,128)(2,1)S(1)} %copy-done.51, bf16[192,192]{1,0:T(8,128)(2,1)S(1)} %copy-done.17), custom_call_target="tpu_custom_call" | custom-call | flops 2800000000 | bytes 14000000 | tf_op jit(solution)/shard_map/middle_x/pallas_call | solution.py:178
  226.8 28.0 %all-to-all-done.3.far_pieces = bf16[8,2,6,48,384]{4,3,2,1,0:T(8,128)(2,1)} async-done(((bf16[8,2,6,48,384]{4,3,2,1,0:T(8,128)(2,1)}), bf16[8,2,6,48,384]{4,3,2,1,0:T(8,128)(2,1)}, u32[]{:S(2)}, u32[]{:S(2)}) %all-to-all-start.3) | async-done | bytes 3538976 | tf_op jit(solution)/shard_map/all_to_all | solution.py:260
  254.8 4.8 %all-to-all-start.1 = ((bf16[8,2,6,48,384]{4,3,2,1,0:T(8,128)(2,1)}), bf16[8,2,6,48,384]{4,3,2,1,0:T(8,128)(2,1)S(1)}, u32[]{:S(2)}, u32[]{:S(2)}) async-start(bf16[8,2,6,48,384]{4,3,2,1,0:T(8,128)(2,1)} %copy-done.4), calls=%async_computation.1 | async-start | bytes 7077888 | tf_op jit(solution)/shard_map/all_to_all | solution.py:260
  269.6 8.3 %backward_yz.2.refs_8_ = f32[24,36864]{1,0:T(8,128)S(1)} custom-call(s32[1]{0:T(128)} %bitcast.column, bf16[8,2,6,48,384]{4,3,2,1,0:T(8,128)(2,1)} %all-to-all-done.3.far_pieces, bf16[24,9216]{1,0:T(8,128)(2,1)S(1)} %copy-done.13, bf16[24,9216]{1,0:T(8,128)(2,1)S(1)} %copy-done.25, bf16[24,9216]{1,0:T(8,128)(2,1)S(1)} %copy-done.23, ...), custom_call_target="tpu_custom_call" | custom-call | flops 2800000000 | bytes 14000000 | tf_op jit(solution)/shard_map/backward_yz/pallas_call | solution.py:245
  279.7 20.3 %all-to-all-done.1.far_pieces = bf16[8,2,6,48,384]{4,3,2,1,0:T(8,128)(2,1)S(1)} async-done(((bf16[8,2,6,48,384]{4,3,2,1,0:T(8,128)(2,1)}), bf16[8,2,6,48,384]{4,3,2,1,0:T(8,128)(2,1)S(1)}, u32[]{:S(2)}, u32[]{:S(2)}) %all-to-all-start.1) | async-done | bytes 3538976 | tf_op jit(solution)/shard_map/all_to_all | solution.py:260
  312.1 10.7 %backward_yz.3 = f32[24,36864]{1,0:T(8,128)} custom-call(s32[1]{0:T(128)} %bitcast.column, bf16[8,2,6,48,384]{4,3,2,1,0:T(8,128)(2,1)S(1)} %all-to-all-done.1.far_pieces, bf16[24,9216]{1,0:T(8,128)(2,1)S(1)} %copy-done.15, bf16[24,9216]{1,0:T(8,128)(2,1)S(1)} %copy-done.39, bf16[24,9216]{1,0:T(8,128)(2,1)S(1)} %copy-done.37, ...), custom_call_target="tpu_custom_call" | custom-call | flops 2800000000 | bytes 14000000 | tf_op jit(solution)/shard_map/backward_yz/pallas_call | solution.py:245
  (182 shorter events, 87.4 us)
Async XLA Ops:
  2.4 9.2 %collective-permute-start.1 = (bf16[24,9216]{1,0:T(8,128)(2,1)S(1)}, bf16[24,9216]{1,0:T(8,128)(2,1)S(1)}, u32[]{:S(2)}, u32[]{:S(2)}) collective-permute-start(bf16[24,9216]{1,0:T(8,128)(2,1)S(1)} %get-tuple-element.15), channel_id=1, source_target_pairs={{0,16},{128,152},{1,17},{129,153},{2,18},{130,154},{3,19},{131,155... | collective-permute-start | bytes 1327112 | tf_op jit(solution)/shard_map/ppermute | solution.py:268
  7.8 8.6 %collective-permute-start.2 = (bf16[24,9216]{1,0:T(8,128)(2,1)S(1)}, bf16[24,9216]{1,0:T(8,128)(2,1)S(1)}, u32[]{:S(2)}, u32[]{:S(2)}) collective-permute-start(bf16[24,9216]{1,0:T(8,128)(2,1)S(1)} %get-tuple-element.17), channel_id=1, source_target_pairs={{0,32},{128,168},{1,33},{129,169},{2,34},{130,170},{3,35},{131,171... | collective-permute-start | bytes 1327112 | tf_op jit(solution)/shard_map/ppermute | solution.py:268
  19.2 11.7 %collective-permute-start.8 = (bf16[24,9216]{1,0:T(8,128)(2,1)}, bf16[24,9216]{1,0:T(8,128)(2,1)}, u32[]{:S(2)}, u32[]{:S(2)}) collective-permute-start(bf16[24,9216]{1,0:T(8,128)(2,1)} %add_add_fusion.1), channel_id=1, source_target_pairs={{0,64},{16,80},{32,96},{48,112},{136,200},{152,216},{168,232},{184... | collective-permute-start | bytes 1327112 | tf_op jit(solution)/shard_map/ppermute | solution.py:268
  32.3 10.4 %collective-permute-start.10 = (bf16[24,4608]{1,0:T(8,128)(2,1)S(1)}, bf16[24,4608]{1,0:T(8,128)(2,1)S(1)}, u32[]{:S(2)}, u32[]{:S(2)}) collective-permute-start(bf16[24,4608]{1,0:T(8,128)(2,1)S(1)} %get-tuple-element.21), channel_id=1, source_target_pairs={{64,128},{80,144},{96,160},{112,176},{200,8},{216,24},{232,40},{24... | collective-permute-start | bytes 663560 | tf_op jit(solution)/shard_map/ppermute | solution.py:268
  33.0 9.8 %collective-permute-start.11 = (bf16[24,4608]{1,0:T(8,128)(2,1)S(1)}, bf16[24,4608]{1,0:T(8,128)(2,1)S(1)}, u32[]{:S(2)}, u32[]{:S(2)}) collective-permute-start(bf16[24,4608]{1,0:T(8,128)(2,1)S(1)} %get-tuple-element.22), channel_id=1, source_target_pairs={{192,128},{208,144},{224,160},{240,176},{72,8},{88,24},{104,40},{1... | collective-permute-start | bytes 663560 | tf_op jit(solution)/shard_map/ppermute | solution.py:268
  34.7 8.4 %collective-permute-start.5 = (bf16[24,9216]{1,0:T(8,128)(2,1)S(1)}, bf16[24,9216]{1,0:T(8,128)(2,1)S(1)}, u32[]{:S(2)}, u32[]{:S(2)}) collective-permute-start(bf16[24,9216]{1,0:T(8,128)(2,1)S(1)} %get-tuple-element.11), channel_id=1, source_target_pairs={{0,16},{128,152},{1,17},{129,153},{2,18},{130,154},{3,19},{131,155... | collective-permute-start | bytes 1327112 | tf_op jit(solution)/shard_map/ppermute | solution.py:268
  36.0 11.1 %collective-permute-start.7 = (bf16[24,9216]{1,0:T(8,128)(2,1)S(1)}, bf16[24,9216]{1,0:T(8,128)(2,1)S(1)}, u32[]{:S(2)}, u32[]{:S(2)}) collective-permute-start(bf16[24,9216]{1,0:T(8,128)(2,1)S(1)} %get-tuple-element.12), channel_id=1, source_target_pairs={{0,48},{128,184},{1,49},{129,185},{2,50},{130,186},{3,51},{131,187... | collective-permute-start | bytes 1327112 | tf_op jit(solution)/shard_map/ppermute | solution.py:268
  38.3 14.6 %collective-permute-start.6 = (bf16[24,9216]{1,0:T(8,128)(2,1)}, bf16[24,9216]{1,0:T(8,128)(2,1)}, u32[]{:S(2)}, u32[]{:S(2)}) collective-permute-start(bf16[24,9216]{1,0:T(8,128)(2,1)} %get-tuple-element.13), channel_id=1, source_target_pairs={{0,32},{128,168},{1,33},{129,169},{2,34},{130,170},{3,35},{131,171... | collective-permute-start | bytes 1327112 | tf_op jit(solution)/shard_map/ppermute | solution.py:268
  42.9 20.7 %collective-permute-start.14 = (bf16[24,9216]{1,0:T(8,128)(2,1)S(1)}, bf16[24,9216]{1,0:T(8,128)(2,1)S(1)}, u32[]{:S(2)}, u32[]{:S(2)}) collective-permute-start(bf16[24,9216]{1,0:T(8,128)(2,1)S(1)} %maximum_add_fusion.refs_0_), channel_id=1, source_target_pairs={{0,48},{8,56},{16,32},{24,40},{32,16},{40,24},{48,0},{56,8},{64,11... | collective-permute-start | bytes 1327112 | tf_op jit(solution)/shard_map/ppermute | solution.py:268
  43.0 20.6 %collective-permute-start.13 = (bf16[24,9216]{1,0:T(8,128)(2,1)S(1)}, bf16[24,9216]{1,0:T(8,128)(2,1)S(1)}, u32[]{:S(2)}, u32[]{:S(2)}) collective-permute-start(bf16[24,9216]{1,0:T(8,128)(2,1)S(1)} %maximum_add_fusion.refs_0_), channel_id=1, source_target_pairs={{0,32},{8,40},{16,48},{24,56},{32,0},{40,8},{48,16},{56,24},{64,96... | collective-permute-start | bytes 1327112 | tf_op jit(solution)/shard_map/ppermute | solution.py:268
  43.1 23.9 %collective-permute-start.12 = (bf16[24,9216]{1,0:T(8,128)(2,1)S(1)}, bf16[24,9216]{1,0:T(8,128)(2,1)S(1)}, u32[]{:S(2)}, u32[]{:S(2)}) collective-permute-start(bf16[24,9216]{1,0:T(8,128)(2,1)S(1)} %maximum_add_fusion.refs_0_), channel_id=1, source_target_pairs={{0,16},{8,24},{16,0},{24,8},{32,48},{40,56},{48,32},{56,40},{64,80... | collective-permute-start | bytes 1327112 | tf_op jit(solution)/shard_map/ppermute | solution.py:268
  47.9 19.2 %collective-permute-start.4 = (bf16[24,9216]{1,0:T(8,128)(2,1)}, bf16[24,9216]{1,0:T(8,128)(2,1)}, u32[]{:S(2)}, u32[]{:S(2)}) collective-permute-start(bf16[24,9216]{1,0:T(8,128)(2,1)} %get-tuple-element.14), channel_id=1, source_target_pairs={{0,0},{128,136},{1,1},{129,137},{2,2},{130,138},{3,3},{131,139},{4... | collective-permute-start | bytes 1327112 | tf_op jit(solution)/shard_map/ppermute | solution.py:268
  52.9 16.6 %collective-permute-start.15 = (bf16[24,9216]{1,0:T(8,128)(2,1)S(1)}, bf16[24,9216]{1,0:T(8,128)(2,1)S(1)}, u32[]{:S(2)}, u32[]{:S(2)}) collective-permute-start(bf16[24,9216]{1,0:T(8,128)(2,1)S(1)} %maximum_add_fusion.refs_0_), channel_id=1, source_target_pairs={{0,8},{8,0},{16,24},{24,16},{32,40},{40,32},{48,56},{56,48},{64,72... | collective-permute-start | bytes 1327112 | tf_op jit(solution)/shard_map/ppermute | solution.py:268
  77.7 10.1 %collective-permute-start.20 = (bf16[24,9216]{1,0:T(8,128)(2,1)}, bf16[24,9216]{1,0:T(8,128)(2,1)}, u32[]{:S(2)}, u32[]{:S(2)}) collective-permute-start(bf16[24,9216]{1,0:T(8,128)(2,1)} %add_add_fusion), channel_id=1, source_target_pairs={{0,192},{16,208},{32,224},{48,240},{136,72},{152,88},{168,104},{18... | collective-permute-start | bytes 1327112 | tf_op jit(solution)/shard_map/ppermute | solution.py:268
  79.8 10.5 %collective-permute-start.19 = (bf16[24,9216]{1,0:T(8,128)(2,1)}, bf16[24,9216]{1,0:T(8,128)(2,1)}, u32[]{:S(2)}, u32[]{:S(2)}) collective-permute-start(bf16[24,9216]{1,0:T(8,128)(2,1)} %add_add_fusion), channel_id=1, source_target_pairs={{0,64},{16,80},{32,96},{48,112},{136,200},{152,216},{168,232},{184... | collective-permute-start | bytes 1327112 | tf_op jit(solution)/shard_map/ppermute | solution.py:268
  81.9 76.1 %all-to-all-start.2 = ((bf16[8,2,6,48,384]{4,3,2,1,0:T(8,128)(2,1)}), bf16[8,2,6,48,384]{4,3,2,1,0:T(8,128)(2,1)S(1)}, u32[]{:S(2)}, u32[]{:S(2)}) async-start(bf16[8,2,6,48,384]{4,3,2,1,0:T(8,128)(2,1)} %copy-done.8), calls=%async_computation.2 | async-start | bytes 7077888 | tf_op jit(solution)/shard_map/all_to_all | solution.py:260
  93.1 38.8 %collective-permute-start.25 = (bf16[24,9216]{1,0:T(8,128)(2,1)S(1)}, bf16[24,9216]{1,0:T(8,128)(2,1)S(1)}, u32[]{:S(2)}, u32[]{:S(2)}) collective-permute-start(bf16[24,9216]{1,0:T(8,128)(2,1)S(1)} %maximum_add_fusion.1.refs_0_), channel_id=1, source_target_pairs={{0,48},{8,56},{16,32},{24,40},{32,16},{40,24},{48,0},{56,8},{64,11... | collective-permute-start | bytes 1327112 | tf_op jit(solution)/shard_map/ppermute | solution.py:268
  94.5 46.9 %collective-permute-start.24 = (bf16[24,9216]{1,0:T(8,128)(2,1)S(1)}, bf16[24,9216]{1,0:T(8,128)(2,1)S(1)}, u32[]{:S(2)}, u32[]{:S(2)}) collective-permute-start(bf16[24,9216]{1,0:T(8,128)(2,1)S(1)} %maximum_add_fusion.1.refs_0_), channel_id=1, source_target_pairs={{0,32},{8,40},{16,48},{24,56},{32,0},{40,8},{48,16},{56,24},{64,96... | collective-permute-start | bytes 1327112 | tf_op jit(solution)/shard_map/ppermute | solution.py:268
  97.1 44.2 %collective-permute-start.23 = (bf16[24,9216]{1,0:T(8,128)(2,1)S(1)}, bf16[24,9216]{1,0:T(8,128)(2,1)S(1)}, u32[]{:S(2)}, u32[]{:S(2)}) collective-permute-start(bf16[24,9216]{1,0:T(8,128)(2,1)S(1)} %maximum_add_fusion.1.refs_0_), channel_id=1, source_target_pairs={{0,16},{8,24},{16,0},{24,8},{32,48},{40,56},{48,32},{56,40},{64,80... | collective-permute-start | bytes 1327112 | tf_op jit(solution)/shard_map/ppermute | solution.py:268
  97.3 44.6 %collective-permute-start.26 = (bf16[24,9216]{1,0:T(8,128)(2,1)S(1)}, bf16[24,9216]{1,0:T(8,128)(2,1)S(1)}, u32[]{:S(2)}, u32[]{:S(2)}) collective-permute-start(bf16[24,9216]{1,0:T(8,128)(2,1)S(1)} %maximum_add_fusion.1.refs_0_), channel_id=1, source_target_pairs={{0,8},{8,0},{16,24},{24,16},{32,40},{40,32},{48,56},{56,48},{64,72... | collective-permute-start | bytes 1327112 | tf_op jit(solution)/shard_map/ppermute | solution.py:268
  131.9 10.8 %collective-permute-start.29 = (bf16[24,9216]{1,0:T(8,128)(2,1)S(1)}, bf16[24,9216]{1,0:T(8,128)(2,1)S(1)}, u32[]{:S(2)}, u32[]{:S(2)}) collective-permute-start(bf16[24,9216]{1,0:T(8,128)(2,1)S(1)} %collective-permute-done.25.refs_3_), channel_id=1, source_target_pairs={{0,8},{8,0},{16,24},{24,16},{32,40},{40,32},{48,56},{56,48},{64,72... | collective-permute-start | bytes 1327112 | tf_op jit(solution)/shard_map/ppermute | solution.py:268
  159.8 48.0 %all-to-all-start = ((bf16[8,2,6,48,384]{4,3,2,1,0:T(8,128)(2,1)}), bf16[8,2,6,48,384]{4,3,2,1,0:T(8,128)(2,1)}, u32[]{:S(2)}, u32[]{:S(2)}) async-start(bf16[8,2,6,48,384]{4,3,2,1,0:T(8,128)(2,1)} %copy-done.9), calls=%async_computation | async-start | bytes 7077888 | tf_op jit(solution)/shard_map/all_to_all | solution.py:260
  207.8 46.9 %all-to-all-start.3 = ((bf16[8,2,6,48,384]{4,3,2,1,0:T(8,128)(2,1)}), bf16[8,2,6,48,384]{4,3,2,1,0:T(8,128)(2,1)}, u32[]{:S(2)}, u32[]{:S(2)}) async-start(bf16[8,2,6,48,384]{4,3,2,1,0:T(8,128)(2,1)} %copy-done.5), calls=%async_computation.3 | async-start | bytes 7077888 | tf_op jit(solution)/shard_map/all_to_all | solution.py:260
  254.8 45.3 %all-to-all-start.1 = ((bf16[8,2,6,48,384]{4,3,2,1,0:T(8,128)(2,1)}), bf16[8,2,6,48,384]{4,3,2,1,0:T(8,128)(2,1)S(1)}, u32[]{:S(2)}, u32[]{:S(2)}) async-start(bf16[8,2,6,48,384]{4,3,2,1,0:T(8,128)(2,1)} %copy-done.4), calls=%async_computation.1 | async-start | bytes 7077888 | tf_op jit(solution)/shard_map/all_to_all | solution.py:260
  (66 other events, 437.1 us)

commit v3 on v2

--- a/solution.py
+++ b/solution.py
@@ -17,7 +17,7 @@
 PER_CUT = DUOS // 4
 PIECE = (QUADS, 2 * ROWS, 384)
 VECTOR = pl.BlockSpec(memory_space=pltpu.VMEM)
-FAR = pl.BlockSpec(memory_space=pl.ANY)
+FAR = pl.BlockSpec(memory_space=pltpu.HBM)
 SCALAR = pl.BlockSpec(memory_space=pltpu.SMEM)
 F32 = jnp.float32
 BF16 = jnp.bfloat16
@@ -75,11 +75,25 @@
     return jnp.concatenate([lot[rows, :] for lot in lots], axis=1)
 
 
-def forward_body(column, target, *refs):
-    sources, (z_tables, y_table, out), lots = refs[:-6], refs[-6:-3], refs[-3:]
-    for which in range(len(sources) // 4):
+def started(pairs, semaphores):
+    copies = [pltpu.make_async_copy(a, b, semaphores.at[i]) for i, (a, b) in enumerate(pairs)]
+    for copy in copies:
+        copy.start()
+    return copies
+
+
+def forward_body(column, far_target, *refs):
+    pairs = (len(refs) - 9) // 9
+    far_sources, (z_tables, y_table, far_out), refs = refs[: 4 * pairs], refs[4 * pairs : 4 * pairs + 3], refs[4 * pairs + 3 :]
+    lots, (arrived, left, target), sources, outs = refs[:3], refs[3:6], refs[6 : 6 + 4 * pairs], refs[6 + 4 * pairs :]
+    copies = started([(far_target, target), *zip(far_sources, sources)], arrived)
+    copies[0].wait()
+    results = []
+    for which in range(pairs):
+        out = outs[which]
         for slot in range(4):
             source = sources[which * 4 + slot]
+            copies[1 + which * 4 + slot].wait()
 
             def form(part, carry, source=source, slot=slot):
                 duo = (column[0] ^ slot) * PER_CUT + part
@@ -92,7 +106,7 @@
 
             lax.fori_loop(0, PER_CUT, form, 0, unroll=12)
 
-        def planes(quad, carry, which=which):
+        def planes(quad, carry, out=out):
             along_z = []
             for pair in range(2):
                 halves = []
@@ -107,10 +121,14 @@
             along_y = dot(y_table[...], jnp.concatenate(along_z, axis=1).astype(BF16))
             for part in range(PARTS):
                 rows = slice(part * ROWS, (part + 1) * ROWS)
-                out[part, which, quad] = jnp.concatenate([along_y[rows, :384], along_y[rows, 384:]], axis=0).astype(BF16)
+                out[part, quad] = jnp.concatenate([along_y[rows, :384], along_y[rows, 384:]], axis=0).astype(BF16)
             return carry
 
         lax.fori_loop(0, QUADS, planes, 0, unroll=6)
+        results.append(pltpu.make_async_copy(out, far_out.at[:, which], left.at[which]))
+        results[-1].start()
+    for copy in results:
+        copy.wait()
 
 
 def cost(pairs):
@@ -119,20 +137,30 @@
 
 def forward(column, target, sources):
     cuts = [cut for source in sources for cut in source]
+    pairs = len(sources)
     return pl.pallas_call(
         forward_body,
-        in_specs=[SCALAR] + [VECTOR] * (len(cuts) + 3),
-        out_specs=VECTOR,
-        out_shape=jax.ShapeDtypeStruct((PARTS, len(sources), *PIECE), BF16),
-        scratch_shapes=[pltpu.VMEM((ROWS * PITCH, 128), F32)] * 3,
-        compiler_params=pltpu.CompilerParams(vmem_limit_bytes=16 * 2**20),
-        cost_estimate=cost(len(sources)),
+        in_specs=[SCALAR] + [FAR] * (1 + len(cuts)) + [VECTOR] * 2,
+        out_specs=FAR,
+        out_shape=jax.ShapeDtypeStruct((PARTS, pairs, *PIECE), BF16),
+        scratch_shapes=[pltpu.VMEM((ROWS * PITCH, 128), F32)] * 3
+        + [pltpu.SemaphoreType.DMA((1 + len(cuts),)), pltpu.SemaphoreType.DMA((pairs,)), pltpu.VMEM(target.shape, BF16)]
+        + [pltpu.VMEM(cut.shape, BF16) for cut in cuts]
+        + [pltpu.VMEM((PARTS, *PIECE), BF16)] * pairs,
+        compiler_params=pltpu.CompilerParams(vmem_limit_bytes=32 * 2**20),
+        cost_estimate=cost(pairs),
         name="forward_zy",
     )(column, target, *cuts, jnp.asarray(Z_TABLES, BF16), jnp.asarray(Y_TABLE, BF16))
 
 
-def middle_body(pieces, kernel, x_table, x_back, out, head0, head1, tail):
+def middle_body(far_pieces, far_kernel, x_table, x_back, far_out, head0, head1, tail, arrived, left, kernel, *pieces):
     lots = (head0, head1, tail)
+    copies = started([(far_pieces.at[:, 0], pieces[0]), (far_kernel, kernel)], arrived)
+    copies += [
+        pltpu.make_async_copy(far_pieces.at[:, i], piece, arrived.at[1 + i]) for i, piece in enumerate(pieces) if i
+    ]
+    for copy in copies[2:]:
+        copy.start()
     block = QUADS * 2 * ROWS
     low = lax.broadcasted_iota(jnp.int32, (DUOS, 128), 1) < 64
 
@@ -160,29 +188,40 @@
         tail[there, :] = jnp.where(low, pltpu.roll(first, 64, 1), second)
         return carry
 
-    for which in range(pieces.shape[1]):
+    results = []
+    for which, piece in enumerate(pieces):
+        copies[which and 1 + which].wait()
         for part in range(PARTS):
             for tile, lot in enumerate(lots):
                 lot[part * block : (part + 1) * block] = (
-                    pieces[part, which, :, :, tile * 128 : (tile + 1) * 128].astype(F32).reshape(block, 128)
+                    piece[part, :, :, tile * 128 : (tile + 1) * 128].astype(F32).reshape(block, 128)
                 )
+        if which == 0:
+            copies[1].wait()
         lax.fori_loop(0, ROWS // 2, step, 0, unroll=6)
         for part in range(PARTS):
             for tile, lot in enumerate(lots):
-                out[part, which, :, :, tile * 128 : (tile + 1) * 128] = (
+                piece[part, :, :, tile * 128 : (tile + 1) * 128] = (
                     lot[part * block : (part + 1) * block].astype(BF16).reshape(QUADS, 2 * ROWS, 128)
                 )
+        results.append(pltpu.make_async_copy(piece, far_out.at[:, which], left.at[which]))
+        results[-1].start()
+    for copy in results:
+        copy.wait()
 
 
 def middle(pieces, kernel):
+    pairs = pieces.shape[1]
     return pl.pallas_call(
         middle_body,
-        in_specs=[VECTOR] * 4,
-        out_specs=VECTOR,
+        in_specs=[FAR, FAR, VECTOR, VECTOR],
+        out_specs=FAR,
         out_shape=jax.ShapeDtypeStruct(pieces.shape, BF16),
-        scratch_shapes=[pltpu.VMEM((DUOS * ROWS, 128), F32)] * 3,
-        compiler_params=pltpu.CompilerParams(vmem_limit_bytes=16 * 2**20),
-        cost_estimate=cost(pieces.shape[1]),
+        scratch_shapes=[pltpu.VMEM((DUOS * ROWS, 128), F32)] * 3
+        + [pltpu.SemaphoreType.DMA((1 + pairs,)), pltpu.SemaphoreType.DMA((pairs,)), pltpu.VMEM(kernel.shape, F32)]
+        + [pltpu.VMEM((PARTS, *PIECE), BF16)] * pairs,
+        compiler_params=pltpu.CompilerParams(vmem_limit_bytes=32 * 2**20),
+        cost_estimate=cost(pairs),
         name="middle_x",
     )(pieces, kernel, jnp.asarray(X_TABLE, BF16), jnp.asarray(X_BACK, BF16))
 
@@ -190,16 +229,16 @@
 def backward_body(column, far_pieces, *refs):
     pairs = far_pieces.shape[1]
     far_sources, refs = refs[: 4 * pairs], refs[4 * pairs :]
-    total = refs[0] if len(refs) == 9 + 4 * pairs else None
-    y_table, z_tables, out, *refs = refs[total is not None :]
-    lots, (pieces, arrived), sources = refs[:3], refs[3:5], refs[5:]
-    copies = [pltpu.make_async_copy(far_pieces, pieces, arrived.at[0])]
-    copies += [
-        pltpu.make_async_copy(far, near, arrived.at[1 + i]) for i, (far, near) in enumerate(zip(far_sources, sources))
-    ]
-    for copy in copies:
-        copy.start()
+    far_total = refs[0] if len(refs) == 11 + 4 * pairs else None
+    y_table, z_tables, far_out, *refs = refs[far_total is not None :]
+    lots, (pieces, out, arrived, left), sources = refs[:3], refs[3:7], refs[7:]
+    total = None if far_total is None else out
+    copies = started([(far_pieces, pieces), *zip(far_sources, sources)], arrived)
+    if total is not None:
+        copies.append(pltpu.make_async_copy(far_total, out, arrived.at[1 + 4 * pairs]))
+        copies[-1].start()
     copies[0].wait()
+    results = []
 
     for which in range(pairs):
 
@@ -227,6 +266,8 @@
         for slot in range(4):
             source = sources[which * 4 + slot]
             copies[1 + which * 4 + slot].wait()
+            if which == 0 and slot == 0 and total is not None:
+                copies[-1].wait()
 
             def gather(part, carry, source=source, slot=slot, base=base):
                 duo = (column[0] ^ slot) * PER_CUT + part
@@ -238,19 +279,26 @@
                 return carry
 
             lax.fori_loop(0, PER_CUT, gather, 0, unroll=12)
+            if which == pairs - 1:
+                here = pl.ds(pl.multiple_of((column[0] ^ slot) * (CELLS // 4), 128), CELLS // 4)
+                results.append(pltpu.make_async_copy(out.at[:, here], far_out.at[:, here], left.at[slot]))
+                results[-1].start()
+    for copy in results:
+        copy.wait()
 
 
 def backward(column, pieces, sources, total):
     cuts = [cut for source in sources for cut in source]
     return pl.pallas_call(
         backward_body,
-        in_specs=[SCALAR] + [FAR] * (1 + len(cuts)) + [VECTOR] * (2 + (total is not None)),
-        out_specs=VECTOR,
+        in_specs=[SCALAR] + [FAR] * (1 + len(cuts) + (total is not None)) + [VECTOR] * 2,
+        out_specs=FAR,
         out_shape=jax.ShapeDtypeStruct((ROWS, CELLS), F32),
         scratch_shapes=[pltpu.VMEM((ROWS * PITCH, 128), F32)] * 3
-        + [pltpu.VMEM(pieces.shape, BF16), pltpu.SemaphoreType.DMA((1 + len(cuts),))]
+        + [pltpu.VMEM(pieces.shape, BF16), pltpu.VMEM((ROWS, CELLS), F32)]
+        + [pltpu.SemaphoreType.DMA((2 + len(cuts),)), pltpu.SemaphoreType.DMA((4,))]
         + [pltpu.VMEM(cut.shape, BF16) for cut in cuts],
-        compiler_params=pltpu.CompilerParams(vmem_limit_bytes=24 * 2**20),
+        compiler_params=pltpu.CompilerParams(vmem_limit_bytes=32 * 2**20),
         cost_estimate=cost(len(sources)),
         name="backward_yz",
     )(column, pieces, *cuts, *([] if total is None else [total]), jnp.asarray(Y_BACK, BF16), jnp.asarray(Z_BACKS, BF16))
@@ -321,10 +369,12 @@
 
     cut_0 = scatter(orbitals[0])
     cut_1 = scatter(after(orbitals[1], cut_0))
-    mine_0 = gather_x(beyond(beside(cut_0, is_root)))
+    full_0 = beyond(beside(cut_0, is_root))
+    mine_0 = gather_x(full_0)
+    full_1 = beyond(beside(after(cut_1, full_0), is_root))
     batch_0 = [mine_0, other_core(mine_0)]
-    pieces_0 = forward(column, target, batch_0)
-    mine_1 = gather_x(beyond(beside(after(cut_1, pieces_0), is_root)))
+    pieces_0 = forward(column, after(target, full_1), batch_0)
+    mine_1 = gather_x(after(full_1, *mine_0))
     batch_1 = [mine_1, other_core(mine_1)]
     pieces_1 = forward(column, target, batch_1)
     back_0 = exchange(middle(exchange(pieces_0), kernel))

time: 326 us -> 311 us (0.954)
  starting transfers between devices: 107 us -> 71.2 us
  local copies, waits for them, and re-layouts: 47.8 us -> 57.3 us
  waiting for transfers between devices: 111 us -> 118 us
  Pallas kernels: 48.6 us -> 54.9 us
    ppermute x30, starting transfers between devices: 84.8 us -> 48.3 us  [move(): return lax.ppermute(array, 'band', pairs)]
    ppermute x30, waiting for transfers between devices: 34.3 us -> 43.2 us  [move(): return lax.ppermute(array, 'band', pairs)]
    unnamed x112 -> x110, local copies, waits for them, and re-layouts: 44.4 us -> 52.8 us
    pallas_call x6, Pallas kernels: 48.6 us -> 54.9 us  [the longest x2 18.7 us: backward(): pl.pallas_call(backward_body, in_specs=[SCALAR] + [FAR] * (1 + len(cuts)...]
  transfers between devices with their start and end apart: 34 -> 34, of which waited for: 14 -> 14; matrix products, arithmetic and copies ran while one was open for 2% -> 1% of each run, Pallas kernels for 10% -> 12%
where the time goes in v3:
time: 311 us; the launch traced here: 307 us
  waiting for transfers between devices  118 us (38%)
  starting transfers between devices  71.2 us (23%)
  local copies, waits for them, and re-layouts  57.3 us (18%)
  Pallas kernels  54.9 us (18%)
  other arithmetic  4.98 us (2%)
    all_to_all x4, waiting for transfers between devices, exchange(): return lax.all_to_all(pieces, 'grid', 0, 0, tiled=True)  74.8 us
    unnamed x110, local copies, waits for them, and re-layouts  52.8 us
    ppermute x30, starting transfers between devices, move(): return lax.ppermute(array, 'band', pairs)  48.3 us
    ppermute x30, waiting for transfers between devices, move(): return lax.ppermute(array, 'band', pairs)  43.2 us
    all_to_all x4, starting transfers between devices, exchange(): return lax.all_to_all(pieces, 'grid', 0, 0, tiled=True)  22.9 us
    pallas_call x2, Pallas kernels, backward(): pl.pallas_call(backward_body, in_specs=[SCALAR] + [FAR] * (1 + len(cuts)...  18.7 us
    pallas_call x2, Pallas kernels, middle(): pl.pallas_call(middle_body, in_specs=[FAR, FAR, VECTOR, VECTOR], out_spec...  18.4 us
    pallas_call x2, Pallas kernels, forward(): pl.pallas_call(forward_body, in_specs=[SCALAR] + [FAR] * (1 + len(cuts))...  17.7 us
  transfers between devices with their start and end apart: 34, of which 14 were waited for; matrix products, arithmetic and copies ran while one was open for 1% of the time, Pallas kernels for 12%

profile of v3, /device:TPU:32, one launch (start us, length us, event | category | flops | bytes accessed | tf_op | source)
XLA Modules:
  0.0 307.0 jit_solution(3458330057849874778)
XLA Ops:
  3.6 5.0 %collective-permute-start = (bf16[24,9216]{1,0:T(8,128)(2,1)}, bf16[24,9216]{1,0:T(8,128)(2,1)}, u32[]{:S(2)}, u32[]{:S(2)}) collective-permute-start(bf16[24,9216]{1,0:T(8,128)(2,1)} %get-tuple-element.22), channel_id=1, source_target_pairs={{0,0},{128,136},{1,1},{129,137},{2,2},{130,138},{3,3},{131,139},{4... | collective-permute-start | bytes 1327112 | tf_op jit(solution)/shard_map/ppermute | solution.py:316
  16.0 4.7 %collective-permute-done.2 = bf16[24,9216]{1,0:T(8,128)(2,1)} collective-permute-done((bf16[24,9216]{1,0:T(8,128)(2,1)}, bf16[24,9216]{1,0:T(8,128)(2,1)}, u32[]{:S(2)}, u32[]{:S(2)}) %collective-permute-start.2) | collective-permute-done | bytes 442400 | tf_op jit(solution)/shard_map/ppermute | solution.py:316
  27.0 5.3 %collective-permute-start.6 = (bf16[24,9216]{1,0:T(8,128)(2,1)S(1)}, bf16[24,9216]{1,0:T(8,128)(2,1)S(1)}, u32[]{:S(2)}, u32[]{:S(2)}) collective-permute-start(bf16[24,9216]{1,0:T(8,128)(2,1)S(1)} %get-tuple-element.17), channel_id=1, source_target_pairs={{0,32},{128,168},{1,33},{129,169},{2,34},{130,170},{3,35},{131,171... | collective-permute-start | bytes 1327112 | tf_op jit(solution)/shard_map/ppermute | solution.py:316
  34.1 5.0 %collective-permute-start.7 = (bf16[24,9216]{1,0:T(8,128)(2,1)S(1)}, bf16[24,9216]{1,0:T(8,128)(2,1)S(1)}, u32[]{:S(2)}, u32[]{:S(2)}) collective-permute-start(bf16[24,9216]{1,0:T(8,128)(2,1)S(1)} %get-tuple-element.16), channel_id=1, source_target_pairs={{0,48},{128,184},{1,49},{129,185},{2,50},{130,186},{3,51},{131,187... | collective-permute-start | bytes 1327112 | tf_op jit(solution)/shard_map/ppermute | solution.py:316
  40.6 4.3 %collective-permute-done.7 = bf16[24,9216]{1,0:T(8,128)(2,1)S(1)} collective-permute-done((bf16[24,9216]{1,0:T(8,128)(2,1)S(1)}, bf16[24,9216]{1,0:T(8,128)(2,1)S(1)}, u32[]{:S(2)}, u32[]{:S(2)}) %collective-permute-start.7) | collective-permute-done | bytes 442400 | tf_op jit(solution)/shard_map/ppermute | solution.py:316
  45.1 6.1 %collective-permute-start.12 = (bf16[24,9216]{1,0:T(8,128)(2,1)S(1)}, bf16[24,9216]{1,0:T(8,128)(2,1)S(1)}, u32[]{:S(2)}, u32[]{:S(2)}) collective-permute-start(bf16[24,9216]{1,0:T(8,128)(2,1)S(1)} %add_add_fusion), channel_id=1, source_target_pairs={{0,64},{16,80},{32,96},{48,112},{136,200},{152,216},{168,232},{184... | collective-permute-start | bytes 1327112 | tf_op jit(solution)/shard_map/ppermute | solution.py:316
  53.4 4.6 %collective-permute-start.18 = (bf16[24,9216]{1,0:T(8,128)(2,1)S(1)}, bf16[24,9216]{1,0:T(8,128)(2,1)S(1)}, u32[]{:S(2)}, u32[]{:S(2)}) collective-permute-start(bf16[24,9216]{1,0:T(8,128)(2,1)S(1)} %maximum_add_fusion.refs_0_), channel_id=1, source_target_pairs={{0,48},{8,56},{16,32},{24,40},{32,16},{40,24},{48,0},{56,8},{64,11... | collective-permute-start | bytes 1327112 | tf_op jit(solution)/shard_map/ppermute | solution.py:316
  63.4 6.8 %collective-permute-done.17.refs_2_ = bf16[24,9216]{1,0:T(8,128)(2,1)S(1)} collective-permute-done((bf16[24,9216]{1,0:T(8,128)(2,1)S(1)}, bf16[24,9216]{1,0:T(8,128)(2,1)S(1)}, u32[]{:S(2)}, u32[]{:S(2)}) %collective-permute-start.17) | collective-permute-done | bytes 442400 | tf_op jit(solution)/shard_map/ppermute | solution.py:316
  77.3 8.9 %forward_zy.3 = bf16[8,2,6,48,384]{4,3,2,1,0:T(8,128)(2,1)S(1)} custom-call(s32[1]{0:T(128)} %bitcast.column, bf16[24,36864]{1,0:T(8,128)(2,1)S(1)} %get-tuple-element.12.far_target, bf16[24,9216]{1,0:T(8,128)(2,1)S(1)} %maximum_add_fusion.refs_0_, bf16[24,9216]{1,0:T(8,128)(2,1)S(1)} %collective-permute-done.16.refs_1_, ...), custom_call_target="tpu_custom_call" | custom-call | flops 2800000000 | bytes 14000000 | tf_op jit(solution)/shard_map/forward_zy/pallas_call | solution.py:141
  91.0 6.8 %all-to-all-start.2 = ((bf16[8,2,6,48,384]{4,3,2,1,0:T(8,128)(2,1)}), bf16[8,2,6,48,384]{4,3,2,1,0:T(8,128)(2,1)S(1)}, u32[]{:S(2)}, u32[]{:S(2)}) async-start(bf16[8,2,6,48,384]{4,3,2,1,0:T(8,128)(2,1)} %copy-done.8), calls=%async_computation.2 | async-start | bytes 7077888 | tf_op jit(solution)/shard_map/all_to_all | solution.py:308
  99.3 3.3 %collective-permute-start.21 = (bf16[24,9216]{1,0:T(8,128)(2,1)}, bf16[24,9216]{1,0:T(8,128)(2,1)S(1)}, u32[]{:S(2)}, u32[]{:S(2)}) collective-permute-start(bf16[24,9216]{1,0:T(8,128)(2,1)} %maximum_add_fusion.1.refs_0_), channel_id=1, source_target_pairs={{0,48},{8,56},{16,32},{24,40},{32,16},{40,24},{48,0},{56,8},{64,11... | collective-permute-start | bytes 1327112 | tf_op jit(solution)/shard_map/ppermute | solution.py:316
  102.6 8.6 %collective-permute-done.19.refs_1_ = bf16[24,9216]{1,0:T(8,128)(2,1)S(1)} collective-permute-done((bf16[24,9216]{1,0:T(8,128)(2,1)}, bf16[24,9216]{1,0:T(8,128)(2,1)S(1)}, u32[]{:S(2)}, u32[]{:S(2)}) %collective-permute-start.19) | collective-permute-done | bytes 442400 | tf_op jit(solution)/shard_map/ppermute | solution.py:316
  111.2 7.5 %collective-permute-done.20.refs_2_ = bf16[24,9216]{1,0:T(8,128)(2,1)S(1)} collective-permute-done((bf16[24,9216]{1,0:T(8,128)(2,1)}, bf16[24,9216]{1,0:T(8,128)(2,1)S(1)}, u32[]{:S(2)}, u32[]{:S(2)}) %collective-permute-start.20) | collective-permute-done | bytes 442400 | tf_op jit(solution)/shard_map/ppermute | solution.py:316
  127.8 8.9 %forward_zy.2 = bf16[8,2,6,48,384]{4,3,2,1,0:T(8,128)(2,1)S(1)} custom-call(s32[1]{0:T(128)} %bitcast.column, bf16[24,36864]{1,0:T(8,128)(2,1)S(1)} %copy-done.7, bf16[24,9216]{1,0:T(8,128)(2,1)S(1)} %copy-done.14, bf16[24,9216]{1,0:T(8,128)(2,1)S(1)} %collective-permute-done.19.refs_1_, bf16[24,9216]{1,0:T(8,128)(2,1)S(1)} %collective-permute-done.20.refs_2_, ...), custom_call_target="tpu_custom_call" | custom-call | flops 2800000000 | bytes 14000000 | tf_op jit(solution)/shard_map/forward_zy/pallas_call | solution.py:141
  145.7 5.7 %all-to-all-start = ((bf16[8,2,6,48,384]{4,3,2,1,0:T(8,128)(2,1)}), bf16[8,2,6,48,384]{4,3,2,1,0:T(8,128)(2,1)}, u32[]{:S(2)}, u32[]{:S(2)}) async-start(bf16[8,2,6,48,384]{4,3,2,1,0:T(8,128)(2,1)} %copy-done.9), calls=%async_computation | async-start | bytes 7077888 | tf_op jit(solution)/shard_map/all_to_all | solution.py:308
  155.1 8.8 %middle_x.3 = bf16[8,2,6,48,384]{4,3,2,1,0:T(8,128)(2,1)S(1)} custom-call(bf16[8,2,6,48,384]{4,3,2,1,0:T(8,128)(2,1)S(1)} %copy-done.3, f32[12,192,384]{2,1,0:T(8,128)S(1)} %select_multiply_fusion.far_kernel, bf16[192,192]{1,0:T(8,128)(2,1)S(1)} %copy-done.50, bf16[192,192]{1,0:T(8,128)(2,1)S(1)} %copy-done.16), custom_call_target="tpu_custom_call" | custom-call | flops 2800000000 | bytes 14000000 | tf_op jit(solution)/shard_map/middle_x/pallas_call | solution.py:215
  165.7 27.2 %all-to-all-done.far_pieces = bf16[8,2,6,48,384]{4,3,2,1,0:T(8,128)(2,1)} async-done(((bf16[8,2,6,48,384]{4,3,2,1,0:T(8,128)(2,1)}), bf16[8,2,6,48,384]{4,3,2,1,0:T(8,128)(2,1)}, u32[]{:S(2)}, u32[]{:S(2)}) %all-to-all-start) | async-done | bytes 3538976 | tf_op jit(solution)/shard_map/all_to_all | solution.py:308
  193.0 5.6 %all-to-all-start.3 = ((bf16[8,2,6,48,384]{4,3,2,1,0:T(8,128)(2,1)}), bf16[8,2,6,48,384]{4,3,2,1,0:T(8,128)(2,1)}, u32[]{:S(2)}, u32[]{:S(2)}) async-start(bf16[8,2,6,48,384]{4,3,2,1,0:T(8,128)(2,1)} %copy-done.5), calls=%async_computation.3 | async-start | bytes 7077888 | tf_op jit(solution)/shard_map/all_to_all | solution.py:308
  200.4 9.6 %middle_x.2 = bf16[8,2,6,48,384]{4,3,2,1,0:T(8,128)(2,1)S(1)} custom-call(bf16[8,2,6,48,384]{4,3,2,1,0:T(8,128)(2,1)} %all-to-all-done.far_pieces, f32[12,192,384]{2,1,0:T(8,128)S(1)} %select_multiply_fusion.far_kernel, bf16[192,192]{1,0:T(8,128)(2,1)S(1)} %copy-done.51, bf16[192,192]{1,0:T(8,128)(2,1)S(1)} %copy-done.17), custom_call_target="tpu_custom_call" | custom-call | flops 2800000000 | bytes 14000000 | tf_op jit(solution)/shard_map/middle_x/pallas_call | solution.py:215
  211.8 27.6 %all-to-all-done.3.far_pieces = bf16[8,2,6,48,384]{4,3,2,1,0:T(8,128)(2,1)} async-done(((bf16[8,2,6,48,384]{4,3,2,1,0:T(8,128)(2,1)}), bf16[8,2,6,48,384]{4,3,2,1,0:T(8,128)(2,1)}, u32[]{:S(2)}, u32[]{:S(2)}) %all-to-all-start.3) | async-done | bytes 3538976 | tf_op jit(solution)/shard_map/all_to_all | solution.py:308
  239.3 4.8 %all-to-all-start.1 = ((bf16[8,2,6,48,384]{4,3,2,1,0:T(8,128)(2,1)}), bf16[8,2,6,48,384]{4,3,2,1,0:T(8,128)(2,1)S(1)}, u32[]{:S(2)}, u32[]{:S(2)}) async-start(bf16[8,2,6,48,384]{4,3,2,1,0:T(8,128)(2,1)} %copy-done.4), calls=%async_computation.1 | async-start | bytes 7077888 | tf_op jit(solution)/shard_map/all_to_all | solution.py:308
  254.2 8.6 %backward_yz.2.refs_8_ = f32[24,36864]{1,0:T(8,128)S(1)} custom-call(s32[1]{0:T(128)} %bitcast.column, bf16[8,2,6,48,384]{4,3,2,1,0:T(8,128)(2,1)} %all-to-all-done.3.far_pieces, bf16[24,9216]{1,0:T(8,128)(2,1)S(1)} %copy-done.13, bf16[24,9216]{1,0:T(8,128)(2,1)S(1)} %copy-done.21, bf16[24,9216]{1,0:T(8,128)(2,1)S(1)} %copy-done.23, ...), custom_call_target="tpu_custom_call" | custom-call | flops 2800000000 | bytes 14000000 | tf_op jit(solution)/shard_map/backward_yz/pallas_call | solution.py:292
  264.6 20.0 %all-to-all-done.1.far_pieces = bf16[8,2,6,48,384]{4,3,2,1,0:T(8,128)(2,1)S(1)} async-done(((bf16[8,2,6,48,384]{4,3,2,1,0:T(8,128)(2,1)}), bf16[8,2,6,48,384]{4,3,2,1,0:T(8,128)(2,1)S(1)}, u32[]{:S(2)}, u32[]{:S(2)}) %all-to-all-start.1) | async-done | bytes 3538976 | tf_op jit(solution)/shard_map/all_to_all | solution.py:308
  296.7 10.1 %backward_yz.3 = f32[24,36864]{1,0:T(8,128)} custom-call(s32[1]{0:T(128)} %bitcast.column, bf16[8,2,6,48,384]{4,3,2,1,0:T(8,128)(2,1)S(1)} %all-to-all-done.1.far_pieces, bf16[24,9216]{1,0:T(8,128)(2,1)S(1)} %copy-done.15, bf16[24,9216]{1,0:T(8,128)(2,1)S(1)} %copy-done.35, bf16[24,9216]{1,0:T(8,128)(2,1)S(1)} %copy-done.37, ...), custom_call_target="tpu_custom_call" | custom-call | flops 2800000000 | bytes 14000000 | tf_op jit(solution)/shard_map/backward_yz/pallas_call | solution.py:292
  (180 shorter events, 92.6 us)
Async XLA Ops:
  3.6 11.2 %collective-permute-start = (bf16[24,9216]{1,0:T(8,128)(2,1)}, bf16[24,9216]{1,0:T(8,128)(2,1)}, u32[]{:S(2)}, u32[]{:S(2)}) collective-permute-start(bf16[24,9216]{1,0:T(8,128)(2,1)} %get-tuple-element.22), channel_id=1, source_target_pairs={{0,0},{128,136},{1,1},{129,137},{2,2},{130,138},{3,3},{131,139},{4... | collective-permute-start | bytes 1327112 | tf_op jit(solution)/shard_map/ppermute | solution.py:316
  10.6 10.1 %collective-permute-start.2 = (bf16[24,9216]{1,0:T(8,128)(2,1)}, bf16[24,9216]{1,0:T(8,128)(2,1)}, u32[]{:S(2)}, u32[]{:S(2)}) collective-permute-start(bf16[24,9216]{1,0:T(8,128)(2,1)} %get-tuple-element.21), channel_id=1, source_target_pairs={{0,32},{128,168},{1,33},{129,169},{2,34},{130,170},{3,35},{131,171... | collective-permute-start | bytes 1327112 | tf_op jit(solution)/shard_map/ppermute | solution.py:316
  22.2 11.8 %collective-permute-start.8 = (bf16[24,9216]{1,0:T(8,128)(2,1)S(1)}, bf16[24,9216]{1,0:T(8,128)(2,1)S(1)}, u32[]{:S(2)}, u32[]{:S(2)}) collective-permute-start(bf16[24,9216]{1,0:T(8,128)(2,1)S(1)} %add_add_fusion.1), channel_id=1, source_target_pairs={{0,64},{16,80},{32,96},{48,112},{136,200},{152,216},{168,232},{184... | collective-permute-start | bytes 1327112 | tf_op jit(solution)/shard_map/ppermute | solution.py:316
  23.5 15.5 %collective-permute-start.9 = (bf16[24,9216]{1,0:T(8,128)(2,1)S(1)}, bf16[24,9216]{1,0:T(8,128)(2,1)S(1)}, u32[]{:S(2)}, u32[]{:S(2)}) collective-permute-start(bf16[24,9216]{1,0:T(8,128)(2,1)S(1)} %add_add_fusion.1), channel_id=1, source_target_pairs={{0,192},{16,208},{32,224},{48,240},{136,72},{152,88},{168,104},{18... | collective-permute-start | bytes 1327112 | tf_op jit(solution)/shard_map/ppermute | solution.py:316
  25.0 14.9 %collective-permute-start.4 = (bf16[24,9216]{1,0:T(8,128)(2,1)S(1)}, bf16[24,9216]{1,0:T(8,128)(2,1)S(1)}, u32[]{:S(2)}, u32[]{:S(2)}) collective-permute-start(bf16[24,9216]{1,0:T(8,128)(2,1)S(1)} %get-tuple-element.18), channel_id=1, source_target_pairs={{0,0},{128,136},{1,1},{129,137},{2,2},{130,138},{3,3},{131,139},{4... | collective-permute-start | bytes 1327112 | tf_op jit(solution)/shard_map/ppermute | solution.py:316
  25.7 14.9 %collective-permute-start.5 = (bf16[24,9216]{1,0:T(8,128)(2,1)S(1)}, bf16[24,9216]{1,0:T(8,128)(2,1)S(1)}, u32[]{:S(2)}, u32[]{:S(2)}) collective-permute-start(bf16[24,9216]{1,0:T(8,128)(2,1)S(1)} %get-tuple-element.15), channel_id=1, source_target_pairs={{0,16},{128,152},{1,17},{129,153},{2,18},{130,154},{3,19},{131,155... | collective-permute-start | bytes 1327112 | tf_op jit(solution)/shard_map/ppermute | solution.py:316
  27.0 13.6 %collective-permute-start.6 = (bf16[24,9216]{1,0:T(8,128)(2,1)S(1)}, bf16[24,9216]{1,0:T(8,128)(2,1)S(1)}, u32[]{:S(2)}, u32[]{:S(2)}) collective-permute-start(bf16[24,9216]{1,0:T(8,128)(2,1)S(1)} %get-tuple-element.17), channel_id=1, source_target_pairs={{0,32},{128,168},{1,33},{129,169},{2,34},{130,170},{3,35},{131,171... | collective-permute-start | bytes 1327112 | tf_op jit(solution)/shard_map/ppermute | solution.py:316
  34.1 10.8 %collective-permute-start.7 = (bf16[24,9216]{1,0:T(8,128)(2,1)S(1)}, bf16[24,9216]{1,0:T(8,128)(2,1)S(1)}, u32[]{:S(2)}, u32[]{:S(2)}) collective-permute-start(bf16[24,9216]{1,0:T(8,128)(2,1)S(1)} %get-tuple-element.16), channel_id=1, source_target_pairs={{0,48},{128,184},{1,49},{129,185},{2,50},{130,186},{3,51},{131,187... | collective-permute-start | bytes 1327112 | tf_op jit(solution)/shard_map/ppermute | solution.py:316
  45.1 12.9 %collective-permute-start.12 = (bf16[24,9216]{1,0:T(8,128)(2,1)S(1)}, bf16[24,9216]{1,0:T(8,128)(2,1)S(1)}, u32[]{:S(2)}, u32[]{:S(2)}) collective-permute-start(bf16[24,9216]{1,0:T(8,128)(2,1)S(1)} %add_add_fusion), channel_id=1, source_target_pairs={{0,64},{16,80},{32,96},{48,112},{136,200},{152,216},{168,232},{184... | collective-permute-start | bytes 1327112 | tf_op jit(solution)/shard_map/ppermute | solution.py:316
  53.2 10.2 %collective-permute-start.16 = (bf16[24,9216]{1,0:T(8,128)(2,1)S(1)}, bf16[24,9216]{1,0:T(8,128)(2,1)S(1)}, u32[]{:S(2)}, u32[]{:S(2)}) collective-permute-start(bf16[24,9216]{1,0:T(8,128)(2,1)S(1)} %maximum_add_fusion.refs_0_), channel_id=1, source_target_pairs={{0,16},{8,24},{16,0},{24,8},{32,48},{40,56},{48,32},{56,40},{64,80... | collective-permute-start | bytes 1327112 | tf_op jit(solution)/shard_map/ppermute | solution.py:316
  53.3 16.9 %collective-permute-start.17 = (bf16[24,9216]{1,0:T(8,128)(2,1)S(1)}, bf16[24,9216]{1,0:T(8,128)(2,1)S(1)}, u32[]{:S(2)}, u32[]{:S(2)}) collective-permute-start(bf16[24,9216]{1,0:T(8,128)(2,1)S(1)} %maximum_add_fusion.refs_0_), channel_id=1, source_target_pairs={{0,32},{8,40},{16,48},{24,56},{32,0},{40,8},{48,16},{56,24},{64,96... | collective-permute-start | bytes 1327112 | tf_op jit(solution)/shard_map/ppermute | solution.py:316
  53.4 19.4 %collective-permute-start.18 = (bf16[24,9216]{1,0:T(8,128)(2,1)S(1)}, bf16[24,9216]{1,0:T(8,128)(2,1)S(1)}, u32[]{:S(2)}, u32[]{:S(2)}) collective-permute-start(bf16[24,9216]{1,0:T(8,128)(2,1)S(1)} %maximum_add_fusion.refs_0_), channel_id=1, source_target_pairs={{0,48},{8,56},{16,32},{24,40},{32,16},{40,24},{48,0},{56,8},{64,11... | collective-permute-start | bytes 1327112 | tf_op jit(solution)/shard_map/ppermute | solution.py:316
  60.7 12.1 %collective-permute-start.14 = (bf16[24,4608]{1,0:T(8,128)(2,1)}, bf16[24,4608]{1,0:T(8,128)(2,1)}, u32[]{:S(2)}, u32[]{:S(2)}) collective-permute-start(bf16[24,4608]{1,0:T(8,128)(2,1)} %get-tuple-element.23), channel_id=1, source_target_pairs={{64,128},{80,144},{96,160},{112,176},{200,8},{216,24},{232,40},{24... | collective-permute-start | bytes 663560 | tf_op jit(solution)/shard_map/ppermute | solution.py:316
  62.0 11.3 %collective-permute-start.15 = (bf16[24,4608]{1,0:T(8,128)(2,1)}, bf16[24,4608]{1,0:T(8,128)(2,1)}, u32[]{:S(2)}, u32[]{:S(2)}) collective-permute-start(bf16[24,4608]{1,0:T(8,128)(2,1)} %get-tuple-element.24), channel_id=1, source_target_pairs={{192,128},{208,144},{224,160},{240,176},{72,8},{88,24},{104,40},{1... | collective-permute-start | bytes 663560 | tf_op jit(solution)/shard_map/ppermute | solution.py:316
  63.4 11.9 %collective-permute-start.26 = (bf16[24,9216]{1,0:T(8,128)(2,1)S(1)}, bf16[24,9216]{1,0:T(8,128)(2,1)S(1)}, u32[]{:S(2)}, u32[]{:S(2)}) collective-permute-start(bf16[24,9216]{1,0:T(8,128)(2,1)S(1)} %maximum_add_fusion.refs_0_), channel_id=1, source_target_pairs={{0,8},{8,0},{16,24},{24,16},{32,40},{40,32},{48,56},{56,48},{64,72... | collective-permute-start | bytes 1327112 | tf_op jit(solution)/shard_map/ppermute | solution.py:316
  91.0 52.8 %all-to-all-start.2 = ((bf16[8,2,6,48,384]{4,3,2,1,0:T(8,128)(2,1)}), bf16[8,2,6,48,384]{4,3,2,1,0:T(8,128)(2,1)S(1)}, u32[]{:S(2)}, u32[]{:S(2)}) async-start(bf16[8,2,6,48,384]{4,3,2,1,0:T(8,128)(2,1)} %copy-done.8), calls=%async_computation.2 | async-start | bytes 7077888 | tf_op jit(solution)/shard_map/all_to_all | solution.py:308
  97.9 13.3 %collective-permute-start.19 = (bf16[24,9216]{1,0:T(8,128)(2,1)}, bf16[24,9216]{1,0:T(8,128)(2,1)S(1)}, u32[]{:S(2)}, u32[]{:S(2)}) collective-permute-start(bf16[24,9216]{1,0:T(8,128)(2,1)} %maximum_add_fusion.1.refs_0_), channel_id=1, source_target_pairs={{0,16},{8,24},{16,0},{24,8},{32,48},{40,56},{48,32},{56,40},{64,80... | collective-permute-start | bytes 1327112 | tf_op jit(solution)/shard_map/ppermute | solution.py:316
  97.9 20.8 %collective-permute-start.20 = (bf16[24,9216]{1,0:T(8,128)(2,1)}, bf16[24,9216]{1,0:T(8,128)(2,1)S(1)}, u32[]{:S(2)}, u32[]{:S(2)}) collective-permute-start(bf16[24,9216]{1,0:T(8,128)(2,1)} %maximum_add_fusion.1.refs_0_), channel_id=1, source_target_pairs={{0,32},{8,40},{16,48},{24,56},{32,0},{40,8},{48,16},{56,24},{64,96... | collective-permute-start | bytes 1327112 | tf_op jit(solution)/shard_map/ppermute | solution.py:316
  99.3 22.3 %collective-permute-start.21 = (bf16[24,9216]{1,0:T(8,128)(2,1)}, bf16[24,9216]{1,0:T(8,128)(2,1)S(1)}, u32[]{:S(2)}, u32[]{:S(2)}) collective-permute-start(bf16[24,9216]{1,0:T(8,128)(2,1)} %maximum_add_fusion.1.refs_0_), channel_id=1, source_target_pairs={{0,48},{8,56},{16,32},{24,40},{32,16},{40,24},{48,0},{56,8},{64,11... | collective-permute-start | bytes 1327112 | tf_op jit(solution)/shard_map/ppermute | solution.py:316
  102.6 19.0 %collective-permute-start.22 = (bf16[24,9216]{1,0:T(8,128)(2,1)}, bf16[24,9216]{1,0:T(8,128)(2,1)S(1)}, u32[]{:S(2)}, u32[]{:S(2)}) collective-permute-start(bf16[24,9216]{1,0:T(8,128)(2,1)} %maximum_add_fusion.1.refs_0_), channel_id=1, source_target_pairs={{0,8},{8,0},{16,24},{24,16},{32,40},{40,32},{48,56},{56,48},{64,72... | collective-permute-start | bytes 1327112 | tf_op jit(solution)/shard_map/ppermute | solution.py:316
  111.2 10.4 %collective-permute-start.23 = (bf16[24,9216]{1,0:T(8,128)(2,1)S(1)}, bf16[24,9216]{1,0:T(8,128)(2,1)S(1)}, u32[]{:S(2)}, u32[]{:S(2)}) collective-permute-start(bf16[24,9216]{1,0:T(8,128)(2,1)S(1)} %collective-permute-done.19.refs_1_), channel_id=1, source_target_pairs={{0,8},{8,0},{16,24},{24,16},{32,40},{40,32},{48,56},{56,48},{64,72... | collective-permute-start | bytes 1327112 | tf_op jit(solution)/shard_map/ppermute | solution.py:316
  145.7 47.3 %all-to-all-start = ((bf16[8,2,6,48,384]{4,3,2,1,0:T(8,128)(2,1)}), bf16[8,2,6,48,384]{4,3,2,1,0:T(8,128)(2,1)}, u32[]{:S(2)}, u32[]{:S(2)}) async-start(bf16[8,2,6,48,384]{4,3,2,1,0:T(8,128)(2,1)} %copy-done.9), calls=%async_computation | async-start | bytes 7077888 | tf_op jit(solution)/shard_map/all_to_all | solution.py:308
  193.0 46.4 %all-to-all-start.3 = ((bf16[8,2,6,48,384]{4,3,2,1,0:T(8,128)(2,1)}), bf16[8,2,6,48,384]{4,3,2,1,0:T(8,128)(2,1)}, u32[]{:S(2)}, u32[]{:S(2)}) async-start(bf16[8,2,6,48,384]{4,3,2,1,0:T(8,128)(2,1)} %copy-done.5), calls=%async_computation.3 | async-start | bytes 7077888 | tf_op jit(solution)/shard_map/all_to_all | solution.py:308
  239.3 45.3 %all-to-all-start.1 = ((bf16[8,2,6,48,384]{4,3,2,1,0:T(8,128)(2,1)}), bf16[8,2,6,48,384]{4,3,2,1,0:T(8,128)(2,1)S(1)}, u32[]{:S(2)}, u32[]{:S(2)}) async-start(bf16[8,2,6,48,384]{4,3,2,1,0:T(8,128)(2,1)} %copy-done.4), calls=%async_computation.1 | async-start | bytes 7077888 | tf_op jit(solution)/shard_map/all_to_all | solution.py:308
  (65 other events, 269.6 us)

commit v4 on v3

--- a/solution.py
+++ b/solution.py
@@ -147,7 +147,7 @@
         + [pltpu.SemaphoreType.DMA((1 + len(cuts),)), pltpu.SemaphoreType.DMA((pairs,)), pltpu.VMEM(target.shape, BF16)]
         + [pltpu.VMEM(cut.shape, BF16) for cut in cuts]
         + [pltpu.VMEM((PARTS, *PIECE), BF16)] * pairs,
-        compiler_params=pltpu.CompilerParams(vmem_limit_bytes=32 * 2**20),
+        compiler_params=pltpu.CompilerParams(vmem_limit_bytes=62 * 2**20),
         cost_estimate=cost(pairs),
         name="forward_zy",
     )(column, target, *cuts, jnp.asarray(Z_TABLES, BF16), jnp.asarray(Y_TABLE, BF16))
@@ -220,7 +220,7 @@
         scratch_shapes=[pltpu.VMEM((DUOS * ROWS, 128), F32)] * 3
         + [pltpu.SemaphoreType.DMA((1 + pairs,)), pltpu.SemaphoreType.DMA((pairs,)), pltpu.VMEM(kernel.shape, F32)]
         + [pltpu.VMEM((PARTS, *PIECE), BF16)] * pairs,
-        compiler_params=pltpu.CompilerParams(vmem_limit_bytes=32 * 2**20),
+        compiler_params=pltpu.CompilerParams(vmem_limit_bytes=62 * 2**20),
         cost_estimate=cost(pairs),
         name="middle_x",
     )(pieces, kernel, jnp.asarray(X_TABLE, BF16), jnp.asarray(X_BACK, BF16))
@@ -298,7 +298,7 @@
         + [pltpu.VMEM(pieces.shape, BF16), pltpu.VMEM((ROWS, CELLS), F32)]
         + [pltpu.SemaphoreType.DMA((2 + len(cuts),)), pltpu.SemaphoreType.DMA((4,))]
         + [pltpu.VMEM(cut.shape, BF16) for cut in cuts],
-        compiler_params=pltpu.CompilerParams(vmem_limit_bytes=32 * 2**20),
+        compiler_params=pltpu.CompilerParams(vmem_limit_bytes=62 * 2**20),
         cost_estimate=cost(len(sources)),
         name="backward_yz",
     )(column, pieces, *cuts, *([] if total is None else [total]), jnp.asarray(Y_BACK, BF16), jnp.asarray(Z_BACKS, BF16))

time: 311 us -> 285 us (0.916)
  local copies, waits for them, and re-layouts: 57.3 us -> 6.88 us
  waiting for transfers between devices: 118 us -> 134 us
  Pallas kernels: 54.9 us -> 65.5 us
    unnamed x110 -> x30, local copies, waits for them, and re-layouts: 52.8 us -> 3.13 us
    all_to_all x4, waiting for transfers between devices: 74.8 us -> 89.4 us  [exchange(): return lax.all_to_all(pieces, 'grid', 0, 0, tiled=True)]
    pallas_call x2, Pallas kernels: 18.4 us -> 24.6 us  [middle(): pl.pallas_call(middle_body, in_specs=[FAR, FAR, VECTOR, VECTOR], out_spec...]
  transfers between devices with their start and end apart: 34 -> 34, of which waited for: 14 -> 17; matrix products, arithmetic and copies ran while one was open for 1% -> 1% of each run, Pallas kernels for 12% -> 16%
where the time goes in v4:
time: 285 us; the launch traced here: 284 us
  waiting for transfers between devices  134 us (47%)
  starting transfers between devices  71.4 us (25%)
  Pallas kernels  65.5 us (23%)
  local copies, waits for them, and re-layouts  6.88 us (2%)
  other arithmetic  5.4 us (2%)
    all_to_all x4, waiting for transfers between devices, exchange(): return lax.all_to_all(pieces, 'grid', 0, 0, tiled=True)  89.4 us
    ppermute x30, starting transfers between devices, move(): return lax.ppermute(array, 'band', pairs)  47.6 us
    ppermute x30, waiting for transfers between devices, move(): return lax.ppermute(array, 'band', pairs)  44.8 us
    pallas_call x2, Pallas kernels, middle(): pl.pallas_call(middle_body, in_specs=[FAR, FAR, VECTOR, VECTOR], out_spec...  24.6 us
    all_to_all x4, starting transfers between devices, exchange(): return lax.all_to_all(pieces, 'grid', 0, 0, tiled=True)  23.8 us
    pallas_call x2, Pallas kernels, backward(): pl.pallas_call(backward_body, in_specs=[SCALAR] + [FAR] * (1 + len(cuts)...  20.9 us
    pallas_call x2, Pallas kernels, forward(): pl.pallas_call(forward_body, in_specs=[SCALAR] + [FAR] * (1 + len(cuts))...  20 us
  transfers between devices with their start and end apart: 34, of which 17 were waited for; matrix products, arithmetic and copies ran while one was open for 1% of the time, Pallas kernels for 16%

profile of v4, /device:TPU:32, one launch (start us, length us, event | category | flops | bytes accessed | tf_op | source)
XLA Modules:
  0.0 284.0 jit_solution(4428693321288172986)
XLA Ops:
  3.6 5.0 %collective-permute-start = (bf16[24,9216]{1,0:T(8,128)(2,1)}, bf16[24,9216]{1,0:T(8,128)(2,1)}, u32[]{:S(2)}, u32[]{:S(2)}) collective-permute-start(bf16[24,9216]{1,0:T(8,128)(2,1)} %get-tuple-element.22), channel_id=1, source_target_pairs={{0,0},{128,136},{1,1},{129,137},{2,2},{130,138},{3,3},{131,139},{4... | collective-permute-start | bytes 1327112 | tf_op jit(solution)/shard_map/ppermute | solution.py:316
  16.0 4.7 %collective-permute-done.2 = bf16[24,9216]{1,0:T(8,128)(2,1)} collective-permute-done((bf16[24,9216]{1,0:T(8,128)(2,1)}, bf16[24,9216]{1,0:T(8,128)(2,1)}, u32[]{:S(2)}, u32[]{:S(2)}) %collective-permute-start.2) | collective-permute-done | bytes 442400 | tf_op jit(solution)/shard_map/ppermute | solution.py:316
  27.0 5.3 %collective-permute-start.6 = (bf16[24,9216]{1,0:T(8,128)(2,1)S(1)}, bf16[24,9216]{1,0:T(8,128)(2,1)S(1)}, u32[]{:S(2)}, u32[]{:S(2)}) collective-permute-start(bf16[24,9216]{1,0:T(8,128)(2,1)S(1)} %get-tuple-element.17), channel_id=1, source_target_pairs={{0,32},{128,168},{1,33},{129,169},{2,34},{130,170},{3,35},{131,171... | collective-permute-start | bytes 1327112 | tf_op jit(solution)/shard_map/ppermute | solution.py:316
  34.1 5.0 %collective-permute-start.7 = (bf16[24,9216]{1,0:T(8,128)(2,1)S(1)}, bf16[24,9216]{1,0:T(8,128)(2,1)S(1)}, u32[]{:S(2)}, u32[]{:S(2)}) collective-permute-start(bf16[24,9216]{1,0:T(8,128)(2,1)S(1)} %get-tuple-element.16), channel_id=1, source_target_pairs={{0,48},{128,184},{1,49},{129,185},{2,50},{130,186},{3,51},{131,187... | collective-permute-start | bytes 1327112 | tf_op jit(solution)/shard_map/ppermute | solution.py:316
  40.6 4.3 %collective-permute-done.7 = bf16[24,9216]{1,0:T(8,128)(2,1)S(1)} collective-permute-done((bf16[24,9216]{1,0:T(8,128)(2,1)S(1)}, bf16[24,9216]{1,0:T(8,128)(2,1)S(1)}, u32[]{:S(2)}, u32[]{:S(2)}) %collective-permute-start.7) | collective-permute-done | bytes 442400 | tf_op jit(solution)/shard_map/ppermute | solution.py:316
  45.1 6.1 %collective-permute-start.12 = (bf16[24,9216]{1,0:T(8,128)(2,1)S(1)}, bf16[24,9216]{1,0:T(8,128)(2,1)S(1)}, u32[]{:S(2)}, u32[]{:S(2)}) collective-permute-start(bf16[24,9216]{1,0:T(8,128)(2,1)S(1)} %add_add_fusion), channel_id=1, source_target_pairs={{0,64},{16,80},{32,96},{48,112},{136,200},{152,216},{168,232},{184... | collective-permute-start | bytes 1327112 | tf_op jit(solution)/shard_map/ppermute | solution.py:316
  53.4 4.6 %collective-permute-start.18 = (bf16[24,9216]{1,0:T(8,128)(2,1)S(1)}, bf16[24,9216]{1,0:T(8,128)(2,1)}, u32[]{:S(2)}, u32[]{:S(2)}) collective-permute-start(bf16[24,9216]{1,0:T(8,128)(2,1)S(1)} %maximum_add_fusion.refs_0_), channel_id=1, source_target_pairs={{0,48},{8,56},{16,32},{24,40},{32,16},{40,24},{48,0},{56,8},{64,11... | collective-permute-start | bytes 1327112 | tf_op jit(solution)/shard_map/ppermute | solution.py:316
  63.5 6.7 %collective-permute-done.17.refs_2_ = bf16[24,9216]{1,0:T(8,128)(2,1)S(1)} collective-permute-done((bf16[24,9216]{1,0:T(8,128)(2,1)S(1)}, bf16[24,9216]{1,0:T(8,128)(2,1)S(1)}, u32[]{:S(2)}, u32[]{:S(2)}) %collective-permute-start.17) | collective-permute-done | bytes 442400 | tf_op jit(solution)/shard_map/ppermute | solution.py:316
  76.8 10.0 %forward_zy.3 = bf16[8,2,6,48,384]{4,3,2,1,0:T(8,128)(2,1)} custom-call(s32[1]{0:T(128)} %bitcast.column, bf16[24,36864]{1,0:T(8,128)(2,1)} %copy-done, bf16[24,9216]{1,0:T(8,128)(2,1)} %copy-done.1, bf16[24,9216]{1,0:T(8,128)(2,1)} %copy-done.3, bf16[24,9216]{1,0:T(8,128)(2,1)} %copy-done.4, bf16[24,9216]{1,0:T(8,128)(2,1)} %collective-permute-done.18.refs_3_, ...), custom_call_target="tpu_custom_call" | custom-call | flops 2800000000 | bytes 14000000 | tf_op jit(solution)/shard_map/forward_zy/pallas_call | solution.py:141
  86.9 6.8 %all-to-all-start.2 = ((bf16[8,2,6,48,384]{4,3,2,1,0:T(8,128)(2,1)}), bf16[8,2,6,48,384]{4,3,2,1,0:T(8,128)(2,1)}, u32[]{:S(2)}, u32[]{:S(2)}) async-start(bf16[8,2,6,48,384]{4,3,2,1,0:T(8,128)(2,1)} %forward_zy.3), calls=%async_computation.2 | async-start | bytes 7077888 | tf_op jit(solution)/shard_map/all_to_all | solution.py:308
  98.4 8.4 %collective-permute-done.19.refs_1_ = bf16[24,9216]{1,0:T(8,128)(2,1)S(1)} collective-permute-done((bf16[24,9216]{1,0:T(8,128)(2,1)S(1)}, bf16[24,9216]{1,0:T(8,128)(2,1)S(1)}, u32[]{:S(2)}, u32[]{:S(2)}) %collective-permute-start.19) | collective-permute-done | bytes 442400 | tf_op jit(solution)/shard_map/ppermute | solution.py:316
  106.8 7.6 %collective-permute-done.20.refs_2_ = bf16[24,9216]{1,0:T(8,128)(2,1)S(1)} collective-permute-done((bf16[24,9216]{1,0:T(8,128)(2,1)S(1)}, bf16[24,9216]{1,0:T(8,128)(2,1)S(1)}, u32[]{:S(2)}, u32[]{:S(2)}) %collective-permute-start.20) | collective-permute-done | bytes 442400 | tf_op jit(solution)/shard_map/ppermute | solution.py:316
  119.3 10.0 %forward_zy.2 = bf16[8,2,6,48,384]{4,3,2,1,0:T(8,128)(2,1)} custom-call(s32[1]{0:T(128)} %bitcast.column, bf16[24,36864]{1,0:T(8,128)(2,1)} %copy-done, bf16[24,9216]{1,0:T(8,128)(2,1)} %copy-done.2, bf16[24,9216]{1,0:T(8,128)(2,1)} %copy-done.9, bf16[24,9216]{1,0:T(8,128)(2,1)} %copy-done.10, bf16[24,9216]{1,0:T(8,128)(2,1)} %copy-done.11, ...), custom_call_target="tpu_custom_call" | custom-call | flops 2800000000 | bytes 14000000 | tf_op jit(solution)/shard_map/forward_zy/pallas_call | solution.py:141
  129.3 6.2 %all-to-all-done.2.far_pieces = bf16[8,2,6,48,384]{4,3,2,1,0:T(8,128)(2,1)} async-done(((bf16[8,2,6,48,384]{4,3,2,1,0:T(8,128)(2,1)}), bf16[8,2,6,48,384]{4,3,2,1,0:T(8,128)(2,1)}, u32[]{:S(2)}, u32[]{:S(2)}) %all-to-all-start.2) | async-done | bytes 3538976 | tf_op jit(solution)/shard_map/all_to_all | solution.py:308
  135.5 5.6 %all-to-all-start = ((bf16[8,2,6,48,384]{4,3,2,1,0:T(8,128)(2,1)}), bf16[8,2,6,48,384]{4,3,2,1,0:T(8,128)(2,1)}, u32[]{:S(2)}, u32[]{:S(2)}) async-start(bf16[8,2,6,48,384]{4,3,2,1,0:T(8,128)(2,1)} %forward_zy.2), calls=%async_computation | async-start | bytes 7077888 | tf_op jit(solution)/shard_map/all_to_all | solution.py:308
  143.6 12.3 %middle_x.3 = bf16[8,2,6,48,384]{4,3,2,1,0:T(8,128)(2,1)} custom-call(bf16[8,2,6,48,384]{4,3,2,1,0:T(8,128)(2,1)} %all-to-all-done.2.far_pieces, f32[12,192,384]{2,1,0:T(8,128)} %select_multiply_fusion.far_kernel, bf16[192,192]{1,0:T(8,128)(2,1)} %constant.117.clone.refs_9_.x_table, bf16[192,192]{1,0:T(8,128)(2,1)} %constant.118.clone.x_back.refs_8_.refs_9_), custom_call_target="tpu_custom_call" | custom-call | flops 2800000000 | bytes 14000000 | tf_op jit(solution)/shard_map/middle_x/pallas_call | solution.py:215
  156.0 26.1 %all-to-all-done.far_pieces = bf16[8,2,6,48,384]{4,3,2,1,0:T(8,128)(2,1)} async-done(((bf16[8,2,6,48,384]{4,3,2,1,0:T(8,128)(2,1)}), bf16[8,2,6,48,384]{4,3,2,1,0:T(8,128)(2,1)}, u32[]{:S(2)}, u32[]{:S(2)}) %all-to-all-start) | async-done | bytes 3538976 | tf_op jit(solution)/shard_map/all_to_all | solution.py:308
  182.1 5.9 %all-to-all-start.3 = ((bf16[8,2,6,48,384]{4,3,2,1,0:T(8,128)(2,1)}), bf16[8,2,6,48,384]{4,3,2,1,0:T(8,128)(2,1)}, u32[]{:S(2)}, u32[]{:S(2)}) async-start(bf16[8,2,6,48,384]{4,3,2,1,0:T(8,128)(2,1)} %middle_x.3), calls=%async_computation.3 | async-start | bytes 7077888 | tf_op jit(solution)/shard_map/all_to_all | solution.py:308
  187.9 12.2 %middle_x.2 = bf16[8,2,6,48,384]{4,3,2,1,0:T(8,128)(2,1)} custom-call(bf16[8,2,6,48,384]{4,3,2,1,0:T(8,128)(2,1)} %all-to-all-done.far_pieces, f32[12,192,384]{2,1,0:T(8,128)} %select_multiply_fusion.far_kernel, bf16[192,192]{1,0:T(8,128)(2,1)} %constant.117.clone.refs_9_.x_table, bf16[192,192]{1,0:T(8,128)(2,1)} %constant.118.clone.x_back.refs_8_.refs_9_), custom_call_target="tpu_custom_call" | custom-call | flops 2800000000 | bytes 14000000 | tf_op jit(solution)/shard_map/middle_x/pallas_call | solution.py:215
  200.1 27.8 %all-to-all-done.3.far_pieces = bf16[8,2,6,48,384]{4,3,2,1,0:T(8,128)(2,1)} async-done(((bf16[8,2,6,48,384]{4,3,2,1,0:T(8,128)(2,1)}), bf16[8,2,6,48,384]{4,3,2,1,0:T(8,128)(2,1)}, u32[]{:S(2)}, u32[]{:S(2)}) %all-to-all-start.3) | async-done | bytes 3538976 | tf_op jit(solution)/shard_map/all_to_all | solution.py:308
  228.0 5.6 %all-to-all-start.1 = ((bf16[8,2,6,48,384]{4,3,2,1,0:T(8,128)(2,1)}), bf16[8,2,6,48,384]{4,3,2,1,0:T(8,128)(2,1)}, u32[]{:S(2)}, u32[]{:S(2)}) async-start(bf16[8,2,6,48,384]{4,3,2,1,0:T(8,128)(2,1)} %middle_x.2), calls=%async_computation.1 | async-start | bytes 7077888 | tf_op jit(solution)/shard_map/all_to_all | solution.py:308
  233.6 10.4 %backward_yz.2.refs_8_ = f32[24,36864]{1,0:T(8,128)} custom-call(s32[1]{0:T(128)} %bitcast.column, bf16[8,2,6,48,384]{4,3,2,1,0:T(8,128)(2,1)} %all-to-all-done.3.far_pieces, bf16[24,9216]{1,0:T(8,128)(2,1)} %copy-done.1, bf16[24,9216]{1,0:T(8,128)(2,1)} %copy-done.3, bf16[24,9216]{1,0:T(8,128)(2,1)} %copy-done.4, ...), custom_call_target="tpu_custom_call" | custom-call | flops 2800000000 | bytes 14000000 | tf_op jit(solution)/shard_map/backward_yz/pallas_call | solution.py:292
  244.0 29.4 %all-to-all-done.1.far_pieces = bf16[8,2,6,48,384]{4,3,2,1,0:T(8,128)(2,1)} async-done(((bf16[8,2,6,48,384]{4,3,2,1,0:T(8,128)(2,1)}), bf16[8,2,6,48,384]{4,3,2,1,0:T(8,128)(2,1)}, u32[]{:S(2)}, u32[]{:S(2)}) %all-to-all-start.1) | async-done | bytes 3538976 | tf_op jit(solution)/shard_map/all_to_all | solution.py:308
  273.4 10.4 %backward_yz.3 = f32[24,36864]{1,0:T(8,128)} custom-call(s32[1]{0:T(128)} %bitcast.column, bf16[8,2,6,48,384]{4,3,2,1,0:T(8,128)(2,1)} %all-to-all-done.1.far_pieces, bf16[24,9216]{1,0:T(8,128)(2,1)} %copy-done.2, bf16[24,9216]{1,0:T(8,128)(2,1)} %copy-done.9, bf16[24,9216]{1,0:T(8,128)(2,1)} %copy-done.10, bf16[24,9216]{1,0:T(8,128)(2,1)} %copy-done.11, ...), custom_call_target="tpu_custom_call" | custom-call | flops 2800000000 | bytes 14000000 | tf_op jit(solution)/shard_map/backward_yz/pallas_call | solution.py:292
  (100 shorter events, 47.1 us)
Async XLA Ops:
  3.6 11.2 %collective-permute-start = (bf16[24,9216]{1,0:T(8,128)(2,1)}, bf16[24,9216]{1,0:T(8,128)(2,1)}, u32[]{:S(2)}, u32[]{:S(2)}) collective-permute-start(bf16[24,9216]{1,0:T(8,128)(2,1)} %get-tuple-element.22), channel_id=1, source_target_pairs={{0,0},{128,136},{1,1},{129,137},{2,2},{130,138},{3,3},{131,139},{4... | collective-permute-start | bytes 1327112 | tf_op jit(solution)/shard_map/ppermute | solution.py:316
  22.2 11.8 %collective-permute-start.8 = (bf16[24,9216]{1,0:T(8,128)(2,1)S(1)}, bf16[24,9216]{1,0:T(8,128)(2,1)S(1)}, u32[]{:S(2)}, u32[]{:S(2)}) collective-permute-start(bf16[24,9216]{1,0:T(8,128)(2,1)S(1)} %add_add_fusion.1), channel_id=1, source_target_pairs={{0,64},{16,80},{32,96},{48,112},{136,200},{152,216},{168,232},{184... | collective-permute-start | bytes 1327112 | tf_op jit(solution)/shard_map/ppermute | solution.py:316
  23.6 15.5 %collective-permute-start.9 = (bf16[24,9216]{1,0:T(8,128)(2,1)S(1)}, bf16[24,9216]{1,0:T(8,128)(2,1)S(1)}, u32[]{:S(2)}, u32[]{:S(2)}) collective-permute-start(bf16[24,9216]{1,0:T(8,128)(2,1)S(1)} %add_add_fusion.1), channel_id=1, source_target_pairs={{0,192},{16,208},{32,224},{48,240},{136,72},{152,88},{168,104},{18... | collective-permute-start | bytes 1327112 | tf_op jit(solution)/shard_map/ppermute | solution.py:316
  25.0 14.9 %collective-permute-start.4 = (bf16[24,9216]{1,0:T(8,128)(2,1)S(1)}, bf16[24,9216]{1,0:T(8,128)(2,1)S(1)}, u32[]{:S(2)}, u32[]{:S(2)}) collective-permute-start(bf16[24,9216]{1,0:T(8,128)(2,1)S(1)} %get-tuple-element.18), channel_id=1, source_target_pairs={{0,0},{128,136},{1,1},{129,137},{2,2},{130,138},{3,3},{131,139},{4... | collective-permute-start | bytes 1327112 | tf_op jit(solution)/shard_map/ppermute | solution.py:316
  25.7 14.9 %collective-permute-start.5 = (bf16[24,9216]{1,0:T(8,128)(2,1)S(1)}, bf16[24,9216]{1,0:T(8,128)(2,1)S(1)}, u32[]{:S(2)}, u32[]{:S(2)}) collective-permute-start(bf16[24,9216]{1,0:T(8,128)(2,1)S(1)} %get-tuple-element.15), channel_id=1, source_target_pairs={{0,16},{128,152},{1,17},{129,153},{2,18},{130,154},{3,19},{131,155... | collective-permute-start | bytes 1327112 | tf_op jit(solution)/shard_map/ppermute | solution.py:316
  27.0 13.5 %collective-permute-start.6 = (bf16[24,9216]{1,0:T(8,128)(2,1)S(1)}, bf16[24,9216]{1,0:T(8,128)(2,1)S(1)}, u32[]{:S(2)}, u32[]{:S(2)}) collective-permute-start(bf16[24,9216]{1,0:T(8,128)(2,1)S(1)} %get-tuple-element.17), channel_id=1, source_target_pairs={{0,32},{128,168},{1,33},{129,169},{2,34},{130,170},{3,35},{131,171... | collective-permute-start | bytes 1327112 | tf_op jit(solution)/shard_map/ppermute | solution.py:316
  34.1 10.8 %collective-permute-start.7 = (bf16[24,9216]{1,0:T(8,128)(2,1)S(1)}, bf16[24,9216]{1,0:T(8,128)(2,1)S(1)}, u32[]{:S(2)}, u32[]{:S(2)}) collective-permute-start(bf16[24,9216]{1,0:T(8,128)(2,1)S(1)} %get-tuple-element.16), channel_id=1, source_target_pairs={{0,48},{128,184},{1,49},{129,185},{2,50},{130,186},{3,51},{131,187... | collective-permute-start | bytes 1327112 | tf_op jit(solution)/shard_map/ppermute | solution.py:316
  45.1 12.9 %collective-permute-start.12 = (bf16[24,9216]{1,0:T(8,128)(2,1)S(1)}, bf16[24,9216]{1,0:T(8,128)(2,1)S(1)}, u32[]{:S(2)}, u32[]{:S(2)}) collective-permute-start(bf16[24,9216]{1,0:T(8,128)(2,1)S(1)} %add_add_fusion), channel_id=1, source_target_pairs={{0,64},{16,80},{32,96},{48,112},{136,200},{152,216},{168,232},{184... | collective-permute-start | bytes 1327112 | tf_op jit(solution)/shard_map/ppermute | solution.py:316
  51.2 10.1 %collective-permute-start.13 = (bf16[24,9216]{1,0:T(8,128)(2,1)S(1)}, bf16[24,9216]{1,0:T(8,128)(2,1)S(1)}, u32[]{:S(2)}, u32[]{:S(2)}) collective-permute-start(bf16[24,9216]{1,0:T(8,128)(2,1)S(1)} %add_add_fusion), channel_id=1, source_target_pairs={{0,192},{16,208},{32,224},{48,240},{136,72},{152,88},{168,104},{18... | collective-permute-start | bytes 1327112 | tf_op jit(solution)/shard_map/ppermute | solution.py:316
  53.2 10.3 %collective-permute-start.16 = (bf16[24,9216]{1,0:T(8,128)(2,1)S(1)}, bf16[24,9216]{1,0:T(8,128)(2,1)S(1)}, u32[]{:S(2)}, u32[]{:S(2)}) collective-permute-start(bf16[24,9216]{1,0:T(8,128)(2,1)S(1)} %maximum_add_fusion.refs_0_), channel_id=1, source_target_pairs={{0,16},{8,24},{16,0},{24,8},{32,48},{40,56},{48,32},{56,40},{64,80... | collective-permute-start | bytes 1327112 | tf_op jit(solution)/shard_map/ppermute | solution.py:316
  53.3 16.9 %collective-permute-start.17 = (bf16[24,9216]{1,0:T(8,128)(2,1)S(1)}, bf16[24,9216]{1,0:T(8,128)(2,1)S(1)}, u32[]{:S(2)}, u32[]{:S(2)}) collective-permute-start(bf16[24,9216]{1,0:T(8,128)(2,1)S(1)} %maximum_add_fusion.refs_0_), channel_id=1, source_target_pairs={{0,32},{8,40},{16,48},{24,56},{32,0},{40,8},{48,16},{56,24},{64,96... | collective-permute-start | bytes 1327112 | tf_op jit(solution)/shard_map/ppermute | solution.py:316
  53.4 19.5 %collective-permute-start.18 = (bf16[24,9216]{1,0:T(8,128)(2,1)S(1)}, bf16[24,9216]{1,0:T(8,128)(2,1)}, u32[]{:S(2)}, u32[]{:S(2)}) collective-permute-start(bf16[24,9216]{1,0:T(8,128)(2,1)S(1)} %maximum_add_fusion.refs_0_), channel_id=1, source_target_pairs={{0,48},{8,56},{16,32},{24,40},{32,16},{40,24},{48,0},{56,8},{64,11... | collective-permute-start | bytes 1327112 | tf_op jit(solution)/shard_map/ppermute | solution.py:316
  61.4 11.4 %collective-permute-start.14 = (bf16[24,4608]{1,0:T(8,128)(2,1)S(1)}, bf16[24,4608]{1,0:T(8,128)(2,1)S(1)}, u32[]{:S(2)}, u32[]{:S(2)}) collective-permute-start(bf16[24,4608]{1,0:T(8,128)(2,1)S(1)} %get-tuple-element.23), channel_id=1, source_target_pairs={{64,128},{80,144},{96,160},{112,176},{200,8},{216,24},{232,40},{24... | collective-permute-start | bytes 663560 | tf_op jit(solution)/shard_map/ppermute | solution.py:316
  62.1 11.2 %collective-permute-start.15 = (bf16[24,4608]{1,0:T(8,128)(2,1)S(1)}, bf16[24,4608]{1,0:T(8,128)(2,1)}, u32[]{:S(2)}, u32[]{:S(2)}) collective-permute-start(bf16[24,4608]{1,0:T(8,128)(2,1)S(1)} %get-tuple-element.24), channel_id=1, source_target_pairs={{192,128},{208,144},{224,160},{240,176},{72,8},{88,24},{104,40},{1... | collective-permute-start | bytes 663560 | tf_op jit(solution)/shard_map/ppermute | solution.py:316
  63.5 10.9 %collective-permute-start.26 = (bf16[24,9216]{1,0:T(8,128)(2,1)S(1)}, bf16[24,9216]{1,0:T(8,128)(2,1)S(1)}, u32[]{:S(2)}, u32[]{:S(2)}) collective-permute-start(bf16[24,9216]{1,0:T(8,128)(2,1)S(1)} %maximum_add_fusion.refs_0_), channel_id=1, source_target_pairs={{0,8},{8,0},{16,24},{24,16},{32,40},{40,32},{48,56},{56,48},{64,72... | collective-permute-start | bytes 1327112 | tf_op jit(solution)/shard_map/ppermute | solution.py:316
  86.9 48.6 %all-to-all-start.2 = ((bf16[8,2,6,48,384]{4,3,2,1,0:T(8,128)(2,1)}), bf16[8,2,6,48,384]{4,3,2,1,0:T(8,128)(2,1)}, u32[]{:S(2)}, u32[]{:S(2)}) async-start(bf16[8,2,6,48,384]{4,3,2,1,0:T(8,128)(2,1)} %forward_zy.3), calls=%async_computation.2 | async-start | bytes 7077888 | tf_op jit(solution)/shard_map/all_to_all | solution.py:308
  93.7 13.1 %collective-permute-start.19 = (bf16[24,9216]{1,0:T(8,128)(2,1)S(1)}, bf16[24,9216]{1,0:T(8,128)(2,1)S(1)}, u32[]{:S(2)}, u32[]{:S(2)}) collective-permute-start(bf16[24,9216]{1,0:T(8,128)(2,1)S(1)} %maximum_add_fusion.1.refs_0_), channel_id=1, source_target_pairs={{0,16},{8,24},{16,0},{24,8},{32,48},{40,56},{48,32},{56,40},{64,80... | collective-permute-start | bytes 1327112 | tf_op jit(solution)/shard_map/ppermute | solution.py:316
  93.7 20.6 %collective-permute-start.20 = (bf16[24,9216]{1,0:T(8,128)(2,1)S(1)}, bf16[24,9216]{1,0:T(8,128)(2,1)S(1)}, u32[]{:S(2)}, u32[]{:S(2)}) collective-permute-start(bf16[24,9216]{1,0:T(8,128)(2,1)S(1)} %maximum_add_fusion.1.refs_0_), channel_id=1, source_target_pairs={{0,32},{8,40},{16,48},{24,56},{32,0},{40,8},{48,16},{56,24},{64,96... | collective-permute-start | bytes 1327112 | tf_op jit(solution)/shard_map/ppermute | solution.py:316
  95.1 22.2 %collective-permute-start.21 = (bf16[24,9216]{1,0:T(8,128)(2,1)S(1)}, bf16[24,9216]{1,0:T(8,128)(2,1)S(1)}, u32[]{:S(2)}, u32[]{:S(2)}) collective-permute-start(bf16[24,9216]{1,0:T(8,128)(2,1)S(1)} %maximum_add_fusion.1.refs_0_), channel_id=1, source_target_pairs={{0,48},{8,56},{16,32},{24,40},{32,16},{40,24},{48,0},{56,8},{64,11... | collective-permute-start | bytes 1327112 | tf_op jit(solution)/shard_map/ppermute | solution.py:316
  98.4 19.0 %collective-permute-start.22 = (bf16[24,9216]{1,0:T(8,128)(2,1)S(1)}, bf16[24,9216]{1,0:T(8,128)(2,1)S(1)}, u32[]{:S(2)}, u32[]{:S(2)}) collective-permute-start(bf16[24,9216]{1,0:T(8,128)(2,1)S(1)} %maximum_add_fusion.1.refs_0_), channel_id=1, source_target_pairs={{0,8},{8,0},{16,24},{24,16},{32,40},{40,32},{48,56},{56,48},{64,72... | collective-permute-start | bytes 1327112 | tf_op jit(solution)/shard_map/ppermute | solution.py:316
  106.8 10.6 %collective-permute-start.23 = (bf16[24,9216]{1,0:T(8,128)(2,1)S(1)}, bf16[24,9216]{1,0:T(8,128)(2,1)S(1)}, u32[]{:S(2)}, u32[]{:S(2)}) collective-permute-start(bf16[24,9216]{1,0:T(8,128)(2,1)S(1)} %collective-permute-done.19.refs_1_), channel_id=1, source_target_pairs={{0,8},{8,0},{16,24},{24,16},{32,40},{40,32},{48,56},{56,48},{64,72... | collective-permute-start | bytes 1327112 | tf_op jit(solution)/shard_map/ppermute | solution.py:316
  135.5 46.6 %all-to-all-start = ((bf16[8,2,6,48,384]{4,3,2,1,0:T(8,128)(2,1)}), bf16[8,2,6,48,384]{4,3,2,1,0:T(8,128)(2,1)}, u32[]{:S(2)}, u32[]{:S(2)}) async-start(bf16[8,2,6,48,384]{4,3,2,1,0:T(8,128)(2,1)} %forward_zy.2), calls=%async_computation | async-start | bytes 7077888 | tf_op jit(solution)/shard_map/all_to_all | solution.py:308
  182.1 45.9 %all-to-all-start.3 = ((bf16[8,2,6,48,384]{4,3,2,1,0:T(8,128)(2,1)}), bf16[8,2,6,48,384]{4,3,2,1,0:T(8,128)(2,1)}, u32[]{:S(2)}, u32[]{:S(2)}) async-start(bf16[8,2,6,48,384]{4,3,2,1,0:T(8,128)(2,1)} %middle_x.3), calls=%async_computation.3 | async-start | bytes 7077888 | tf_op jit(solution)/shard_map/all_to_all | solution.py:308
  228.0 45.4 %all-to-all-start.1 = ((bf16[8,2,6,48,384]{4,3,2,1,0:T(8,128)(2,1)}), bf16[8,2,6,48,384]{4,3,2,1,0:T(8,128)(2,1)}, u32[]{:S(2)}, u32[]{:S(2)}) async-start(bf16[8,2,6,48,384]{4,3,2,1,0:T(8,128)(2,1)} %middle_x.2), calls=%async_computation.1 | async-start | bytes 7077888 | tf_op jit(solution)/shard_map/all_to_all | solution.py:308
  (25 other events, 174.5 us)

commit v5 on v4

--- a/solution.py
+++ b/solution.py
@@ -229,21 +229,19 @@
 def backward_body(column, far_pieces, *refs):
     pairs = far_pieces.shape[1]
     far_sources, refs = refs[: 4 * pairs], refs[4 * pairs :]
-    far_total = refs[0] if len(refs) == 11 + 4 * pairs else None
+    far_total = refs[0] if len(refs) == 10 + 5 * pairs else None
     y_table, z_tables, far_out, *refs = refs[far_total is not None :]
-    lots, (pieces, out, arrived, left), sources = refs[:3], refs[3:7], refs[7:]
+    lots, (out, arrived, left), pieces, sources = refs[:3], refs[3:6], refs[6 : 6 + pairs], refs[6 + pairs :]
     total = None if far_total is None else out
-    copies = started([(far_pieces, pieces), *zip(far_sources, sources)], arrived)
-    if total is not None:
-        copies.append(pltpu.make_async_copy(far_total, out, arrived.at[1 + 4 * pairs]))
-        copies[-1].start()
-    copies[0].wait()
+    brought = [(far_pieces.at[:, i], piece) for i, piece in enumerate(pieces)] + list(zip(far_sources, sources))
+    copies = started(brought + ([] if total is None else [(far_total, out)]), arrived)
     results = []
 
     for which in range(pairs):
+        copies[which].wait()
 
         def planes(quad, carry, which=which):
-            parts = [pieces[part, which, quad].astype(F32) for part in range(PARTS)]
+            parts = [pieces[which][part, quad].astype(F32) for part in range(PARTS)]
             stacks = [
                 jnp.concatenate([part[pair * ROWS : (pair + 1) * ROWS] for part in parts], axis=0) for pair in range(2)
             ]
@@ -260,12 +258,12 @@
                     lots[2][rows, :] = odd[:, 128:]
             return carry
 
-        lax.fori_loop(0, QUADS, planes, 0, unroll=3)
+        lax.fori_loop(0, QUADS, planes, 0, unroll=6)
         base = total if which == 0 else out
 
         for slot in range(4):
             source = sources[which * 4 + slot]
-            copies[1 + which * 4 + slot].wait()
+            copies[pairs + which * 4 + slot].wait()
             if which == 0 and slot == 0 and total is not None:
                 copies[-1].wait()
 
@@ -295,8 +293,8 @@
         out_specs=FAR,
         out_shape=jax.ShapeDtypeStruct((ROWS, CELLS), F32),
         scratch_shapes=[pltpu.VMEM((ROWS * PITCH, 128), F32)] * 3
-        + [pltpu.VMEM(pieces.shape, BF16), pltpu.VMEM((ROWS, CELLS), F32)]
-        + [pltpu.SemaphoreType.DMA((2 + len(cuts),)), pltpu.SemaphoreType.DMA((4,))]
+        + [pltpu.VMEM((ROWS, CELLS), F32), pltpu.SemaphoreType.DMA((6 * len(sources),)), pltpu.SemaphoreType.DMA((4,))]
+        + [pltpu.VMEM((PARTS, *PIECE), BF16)] * len(sources)
         + [pltpu.VMEM(cut.shape, BF16) for cut in cuts],
         compiler_params=pltpu.CompilerParams(vmem_limit_bytes=62 * 2**20),
         cost_estimate=cost(len(sources)),
@@ -369,11 +367,11 @@
 
     cut_0 = scatter(orbitals[0])
     cut_1 = scatter(after(orbitals[1], cut_0))
-    full_0 = beyond(beside(cut_0, is_root))
+    full_0 = beyond(after(beside(cut_0, is_root), cut_1))
     mine_0 = gather_x(full_0)
-    full_1 = beyond(beside(after(cut_1, full_0), is_root))
     batch_0 = [mine_0, other_core(mine_0)]
-    pieces_0 = forward(column, after(target, full_1), batch_0)
+    full_1 = beyond(beside(after(cut_1, batch_0[1][0]), is_root))
+    pieces_0 = after(forward(column, target, batch_0), full_1)
     mine_1 = gather_x(after(full_1, *mine_0))
     batch_1 = [mine_1, other_core(mine_1)]
     pieces_1 = forward(column, target, batch_1)

time: 285 us -> 306 us (1.074)
  the two profiles are of different devices: /device:TPU:32 before, /device:TPU:134 now
where the time goes in v5:
time: 306 us; the launch traced here: 301 us
  waiting for transfers between devices  161 us (53%)
  Pallas kernels  64.6 us (21%)
  starting transfers between devices  60.7 us (20%)
  local copies, waits for them, and re-layouts  8.51 us (3%)
  other arithmetic  5.52 us (2%)
    all_to_all x4, waiting for transfers between devices, exchange(): return lax.all_to_all(pieces, 'grid', 0, 0, tiled=True)  94.8 us
    ppermute x30, waiting for transfers between devices, move(): return lax.ppermute(array, 'band', pairs)  66 us
    all_to_all x4, starting transfers between devices, exchange(): return lax.all_to_all(pieces, 'grid', 0, 0, tiled=True)  32.2 us
    ppermute x30, starting transfers between devices, move(): return lax.ppermute(array, 'band', pairs)  28.5 us
    pallas_call x2, Pallas kernels, middle(): pl.pallas_call(middle_body, in_specs=[FAR, FAR, VECTOR, VECTOR], out_spec...  24.5 us
    pallas_call x2, Pallas kernels, forward(): pl.pallas_call(forward_body, in_specs=[SCALAR] + [FAR] * (1 + len(cuts))...  20.1 us
    pallas_call x2, Pallas kernels, backward(): pl.pallas_call(backward_body, in_specs=[SCALAR] + [FAR] * (1 + len(cuts)...  20 us
  transfers between devices with their start and end apart: 34, of which 13 were waited for; matrix products, arithmetic and copies ran while one was open for 1% of the time, Pallas kernels for 18%

profile of v5, /device:TPU:134, one launch (start us, length us, event | category | flops | bytes accessed | tf_op | source)
XLA Modules:
  0.0 300.8 jit_solution(10367233854646633958)
XLA Ops:
  18.0 19.4 %collective-permute-done.10 = bf16[24,4608]{1,0:T(8,128)(2,1)S(1)} collective-permute-done((bf16[24,4608]{1,0:T(8,128)(2,1)S(1)}, bf16[24,4608]{1,0:T(8,128)(2,1)S(1)}, u32[]{:S(2)}, u32[]{:S(2)}) %collective-permute-start.10) | collective-permute-done | bytes 221216 | tf_op jit(solution)/shard_map/ppermute | solution.py:314
  37.4 5.6 %collective-permute-done.11 = bf16[24,4608]{1,0:T(8,128)(2,1)S(1)} collective-permute-done((bf16[24,4608]{1,0:T(8,128)(2,1)S(1)}, bf16[24,4608]{1,0:T(8,128)(2,1)S(1)}, u32[]{:S(2)}, u32[]{:S(2)}) %collective-permute-start.11) | collective-permute-done | bytes 221216 | tf_op jit(solution)/shard_map/ppermute | solution.py:314
  44.8 5.5 %collective-permute-start.18 = (bf16[24,9216]{1,0:T(8,128)(2,1)S(1)}, bf16[24,9216]{1,0:T(8,128)(2,1)}, u32[]{:S(2)}, u32[]{:S(2)}) collective-permute-start(bf16[24,9216]{1,0:T(8,128)(2,1)S(1)} %maximum_add_fusion.refs_0_), channel_id=1, source_target_pairs={{0,32},{8,40},{16,48},{24,56},{32,0},{40,8},{48,16},{56,24},{64,96... | collective-permute-start | bytes 1327112 | tf_op jit(solution)/shard_map/ppermute | solution.py:314
  51.7 4.6 %collective-permute-done.17.refs_1_ = bf16[24,9216]{1,0:T(8,128)(2,1)S(1)} collective-permute-done((bf16[24,9216]{1,0:T(8,128)(2,1)S(1)}, bf16[24,9216]{1,0:T(8,128)(2,1)S(1)}, u32[]{:S(2)}, u32[]{:S(2)}) %collective-permute-start.17) | collective-permute-done | bytes 442400 | tf_op jit(solution)/shard_map/ppermute | solution.py:314
  56.3 14.2 %collective-permute-done.18.refs_2_ = bf16[24,9216]{1,0:T(8,128)(2,1)} collective-permute-done((bf16[24,9216]{1,0:T(8,128)(2,1)S(1)}, bf16[24,9216]{1,0:T(8,128)(2,1)}, u32[]{:S(2)}, u32[]{:S(2)}) %collective-permute-start.18) | collective-permute-done | bytes 442400 | tf_op jit(solution)/shard_map/ppermute | solution.py:314
  70.5 2.6 collective-permute-done.19.refs_3_
  78.7 10.0 %forward_zy.3 = bf16[8,2,6,48,384]{4,3,2,1,0:T(8,128)(2,1)} custom-call(s32[1]{0:T(128)} %bitcast.column, bf16[24,36864]{1,0:T(8,128)(2,1)} %copy-done, bf16[24,9216]{1,0:T(8,128)(2,1)} %copy-done.1, bf16[24,9216]{1,0:T(8,128)(2,1)} %copy-done.4, bf16[24,9216]{1,0:T(8,128)(2,1)} %collective-permute-done.18.refs_2_, ...), custom_call_target="tpu_custom_call" | custom-call | flops 2800000000 | bytes 14000000 | tf_op jit(solution)/shard_map/forward_zy/pallas_call | solution.py:141
  90.0 9.6 %all-to-all-start.2 = ((bf16[8,2,6,48,384]{4,3,2,1,0:T(8,128)(2,1)}), bf16[8,2,6,48,384]{4,3,2,1,0:T(8,128)(2,1)}, u32[]{:S(2)}, u32[]{:S(2)}) async-start(bf16[8,2,6,48,384]{4,3,2,1,0:T(8,128)(2,1)} %forward_zy.3), calls=%async_computation.2 | async-start | bytes 7077888 | tf_op jit(solution)/shard_map/all_to_all | solution.py:306
  101.6 3.0 collective-permute-start.22
  104.6 8.3 %collective-permute-done.20.refs_1_ = bf16[24,9216]{1,0:T(8,128)(2,1)S(1)} collective-permute-done((bf16[24,9216]{1,0:T(8,128)(2,1)S(1)}, bf16[24,9216]{1,0:T(8,128)(2,1)S(1)}, u32[]{:S(2)}, u32[]{:S(2)}) %collective-permute-start.20) | collective-permute-done | bytes 442400 | tf_op jit(solution)/shard_map/ppermute | solution.py:314
  112.8 8.7 %collective-permute-done.21.refs_2_ = bf16[24,9216]{1,0:T(8,128)(2,1)S(1)} collective-permute-done((bf16[24,9216]{1,0:T(8,128)(2,1)S(1)}, bf16[24,9216]{1,0:T(8,128)(2,1)S(1)}, u32[]{:S(2)}, u32[]{:S(2)}) %collective-permute-start.21) | collective-permute-done | bytes 442400 | tf_op jit(solution)/shard_map/ppermute | solution.py:314
  121.5 2.6 collective-permute-done.22.refs_3_
  126.0 10.0 %forward_zy.2 = bf16[8,2,6,48,384]{4,3,2,1,0:T(8,128)(2,1)} custom-call(s32[1]{0:T(128)} %bitcast.column, bf16[24,36864]{1,0:T(8,128)(2,1)} %copy-done, bf16[24,9216]{1,0:T(8,128)(2,1)} %copy-done.2, bf16[24,9216]{1,0:T(8,128)(2,1)} %copy-done.8, bf16[24,9216]{1,0:T(8,128)(2,1)} %copy-done.9, bf16[24,9216]{1,0:T(8,128)(2,1)} %copy-done.10, ...), custom_call_target="tpu_custom_call" | custom-call | flops 2800000000 | bytes 14000000 | tf_op jit(solution)/shard_map/forward_zy/pallas_call | solution.py:141
  136.1 6.8 %all-to-all-done.2.far_pieces = bf16[8,2,6,48,384]{4,3,2,1,0:T(8,128)(2,1)} async-done(((bf16[8,2,6,48,384]{4,3,2,1,0:T(8,128)(2,1)}), bf16[8,2,6,48,384]{4,3,2,1,0:T(8,128)(2,1)}, u32[]{:S(2)}, u32[]{:S(2)}) %all-to-all-start.2) | async-done | bytes 3538976 | tf_op jit(solution)/shard_map/all_to_all | solution.py:306
  142.9 4.5 %all-to-all-start = ((bf16[8,2,6,48,384]{4,3,2,1,0:T(8,128)(2,1)}), bf16[8,2,6,48,384]{4,3,2,1,0:T(8,128)(2,1)}, u32[]{:S(2)}, u32[]{:S(2)}) async-start(bf16[8,2,6,48,384]{4,3,2,1,0:T(8,128)(2,1)} %forward_zy.2), calls=%async_computation | async-start | bytes 7077888 | tf_op jit(solution)/shard_map/all_to_all | solution.py:306
  150.0 12.3 %middle_x.3 = bf16[8,2,6,48,384]{4,3,2,1,0:T(8,128)(2,1)} custom-call(bf16[8,2,6,48,384]{4,3,2,1,0:T(8,128)(2,1)} %all-to-all-done.2.far_pieces, f32[12,192,384]{2,1,0:T(8,128)} %select_multiply_fusion.far_kernel, bf16[192,192]{1,0:T(8,128)(2,1)} %constant.117.clone.refs_9_.x_table, bf16[192,192]{1,0:T(8,128)(2,1)} %constant.118.clone.x_back.refs_8_.refs_9_), custom_call_target="tpu_custom_call" | custom-call | flops 2800000000 | bytes 14000000 | tf_op jit(solution)/shard_map/middle_x/pallas_call | solution.py:215
  162.3 27.5 %all-to-all-done.far_pieces = bf16[8,2,6,48,384]{4,3,2,1,0:T(8,128)(2,1)} async-done(((bf16[8,2,6,48,384]{4,3,2,1,0:T(8,128)(2,1)}), bf16[8,2,6,48,384]{4,3,2,1,0:T(8,128)(2,1)}, u32[]{:S(2)}, u32[]{:S(2)}) %all-to-all-start) | async-done | bytes 3538976 | tf_op jit(solution)/shard_map/all_to_all | solution.py:306
  189.8 13.6 %all-to-all-start.3 = ((bf16[8,2,6,48,384]{4,3,2,1,0:T(8,128)(2,1)}), bf16[8,2,6,48,384]{4,3,2,1,0:T(8,128)(2,1)}, u32[]{:S(2)}, u32[]{:S(2)}) async-start(bf16[8,2,6,48,384]{4,3,2,1,0:T(8,128)(2,1)} %middle_x.3), calls=%async_computation.3 | async-start | bytes 7077888 | tf_op jit(solution)/shard_map/all_to_all | solution.py:306
  203.4 12.2 %middle_x.2 = bf16[8,2,6,48,384]{4,3,2,1,0:T(8,128)(2,1)} custom-call(bf16[8,2,6,48,384]{4,3,2,1,0:T(8,128)(2,1)} %all-to-all-done.far_pieces, f32[12,192,384]{2,1,0:T(8,128)} %select_multiply_fusion.far_kernel, bf16[192,192]{1,0:T(8,128)(2,1)} %constant.117.clone.refs_9_.x_table, bf16[192,192]{1,0:T(8,128)(2,1)} %constant.118.clone.x_back.refs_8_.refs_9_), custom_call_target="tpu_custom_call" | custom-call | flops 2800000000 | bytes 14000000 | tf_op jit(solution)/shard_map/middle_x/pallas_call | solution.py:215
  215.6 29.2 %all-to-all-done.3.far_pieces = bf16[8,2,6,48,384]{4,3,2,1,0:T(8,128)(2,1)} async-done(((bf16[8,2,6,48,384]{4,3,2,1,0:T(8,128)(2,1)}), bf16[8,2,6,48,384]{4,3,2,1,0:T(8,128)(2,1)}, u32[]{:S(2)}, u32[]{:S(2)}) %all-to-all-start.3) | async-done | bytes 3538976 | tf_op jit(solution)/shard_map/all_to_all | solution.py:306
  244.8 4.5 %all-to-all-start.1 = ((bf16[8,2,6,48,384]{4,3,2,1,0:T(8,128)(2,1)}), bf16[8,2,6,48,384]{4,3,2,1,0:T(8,128)(2,1)}, u32[]{:S(2)}, u32[]{:S(2)}) async-start(bf16[8,2,6,48,384]{4,3,2,1,0:T(8,128)(2,1)} %middle_x.2), calls=%async_computation.1 | async-start | bytes 7077888 | tf_op jit(solution)/shard_map/all_to_all | solution.py:306
  249.3 9.7 %backward_yz.2.refs_8_ = f32[24,36864]{1,0:T(8,128)} custom-call(s32[1]{0:T(128)} %bitcast.column, bf16[8,2,6,48,384]{4,3,2,1,0:T(8,128)(2,1)} %all-to-all-done.3.far_pieces, bf16[24,9216]{1,0:T(8,128)(2,1)} %copy-done.1, bf16[24,9216]{1,0:T(8,128)(2,1)} %copy-done.4, bf16[24,9216]{1,0:T(8,128)(2,1)} %collective-permute-done.18.refs_2_, ...), custom_call_target="tpu_custom_call" | custom-call | flops 2800000000 | bytes 14000000 | tf_op jit(solution)/shard_map/backward_yz/pallas_call | solution.py:290
  259.0 31.2 %all-to-all-done.1.far_pieces = bf16[8,2,6,48,384]{4,3,2,1,0:T(8,128)(2,1)} async-done(((bf16[8,2,6,48,384]{4,3,2,1,0:T(8,128)(2,1)}), bf16[8,2,6,48,384]{4,3,2,1,0:T(8,128)(2,1)}, u32[]{:S(2)}, u32[]{:S(2)}) %all-to-all-start.1) | async-done | bytes 3538976 | tf_op jit(solution)/shard_map/all_to_all | solution.py:306
  290.2 10.3 %backward_yz.3 = f32[24,36864]{1,0:T(8,128)} custom-call(s32[1]{0:T(128)} %bitcast.column, bf16[8,2,6,48,384]{4,3,2,1,0:T(8,128)(2,1)} %all-to-all-done.1.far_pieces, bf16[24,9216]{1,0:T(8,128)(2,1)} %copy-done.2, bf16[24,9216]{1,0:T(8,128)(2,1)} %copy-done.8, bf16[24,9216]{1,0:T(8,128)(2,1)} %copy-done.9, bf16[24,9216]{1,0:T(8,128)(2,1)} %copy-done.10, ...), custom_call_target="tpu_custom_call" | custom-call | flops 2800000000 | bytes 14000000 | tf_op jit(solution)/shard_map/backward_yz/pallas_call | solution.py:290
  (98 shorter events, 34.2 us)
Async XLA Ops:
  3.6 5.7 %collective-permute-start = (bf16[24,9216]{1,0:T(8,128)(2,1)}, bf16[24,9216]{1,0:T(8,128)(2,1)}, u32[]{:S(2)}, u32[]{:S(2)}) collective-permute-start(bf16[24,9216]{1,0:T(8,128)(2,1)} %get-tuple-element.24), channel_id=1, source_target_pairs={{0,0},{128,136},{1,1},{129,137},{2,2},{130,138},{3,3},{131,139},{4... | collective-permute-start | bytes 1327112 | tf_op jit(solution)/shard_map/ppermute | solution.py:314
  5.0 4.3 %collective-permute-start.1 = (bf16[24,9216]{1,0:T(8,128)(2,1)}, bf16[24,9216]{1,0:T(8,128)(2,1)}, u32[]{:S(2)}, u32[]{:S(2)}) collective-permute-start(bf16[24,9216]{1,0:T(8,128)(2,1)} %get-tuple-element.21), channel_id=1, source_target_pairs={{0,16},{128,152},{1,17},{129,153},{2,18},{130,154},{3,19},{131,155... | collective-permute-start | bytes 1327112 | tf_op jit(solution)/shard_map/ppermute | solution.py:314
  15.4 22.0 %collective-permute-start.10 = (bf16[24,4608]{1,0:T(8,128)(2,1)S(1)}, bf16[24,4608]{1,0:T(8,128)(2,1)S(1)}, u32[]{:S(2)}, u32[]{:S(2)}) collective-permute-start(bf16[24,4608]{1,0:T(8,128)(2,1)S(1)} %get-tuple-element.27), channel_id=1, source_target_pairs={{64,128},{80,144},{96,160},{112,176},{200,8},{216,24},{232,40},{24... | collective-permute-start | bytes 663560 | tf_op jit(solution)/shard_map/ppermute | solution.py:314
  16.7 26.3 %collective-permute-start.11 = (bf16[24,4608]{1,0:T(8,128)(2,1)S(1)}, bf16[24,4608]{1,0:T(8,128)(2,1)S(1)}, u32[]{:S(2)}, u32[]{:S(2)}) collective-permute-start(bf16[24,4608]{1,0:T(8,128)(2,1)S(1)} %get-tuple-element.28), channel_id=1, source_target_pairs={{192,128},{208,144},{224,160},{240,176},{72,8},{88,24},{104,40},{1... | collective-permute-start | bytes 663560 | tf_op jit(solution)/shard_map/ppermute | solution.py:314
  43.1 7.2 %collective-permute-start.12 = (bf16[24,9216]{1,0:T(8,128)(2,1)S(1)}, bf16[24,9216]{1,0:T(8,128)(2,1)S(1)}, u32[]{:S(2)}, u32[]{:S(2)}) collective-permute-start(bf16[24,9216]{1,0:T(8,128)(2,1)S(1)} %maximum_add_fusion.refs_0_), channel_id=1, source_target_pairs={{0,8},{8,0},{16,24},{24,16},{32,40},{40,32},{48,56},{56,48},{64,72... | collective-permute-start | bytes 1327112 | tf_op jit(solution)/shard_map/ppermute | solution.py:314
  43.2 13.1 %collective-permute-start.17 = (bf16[24,9216]{1,0:T(8,128)(2,1)S(1)}, bf16[24,9216]{1,0:T(8,128)(2,1)S(1)}, u32[]{:S(2)}, u32[]{:S(2)}) collective-permute-start(bf16[24,9216]{1,0:T(8,128)(2,1)S(1)} %maximum_add_fusion.refs_0_), channel_id=1, source_target_pairs={{0,16},{8,24},{16,0},{24,8},{32,48},{40,56},{48,32},{56,40},{64,80... | collective-permute-start | bytes 1327112 | tf_op jit(solution)/shard_map/ppermute | solution.py:314
  44.8 25.6 %collective-permute-start.18 = (bf16[24,9216]{1,0:T(8,128)(2,1)S(1)}, bf16[24,9216]{1,0:T(8,128)(2,1)}, u32[]{:S(2)}, u32[]{:S(2)}) collective-permute-start(bf16[24,9216]{1,0:T(8,128)(2,1)S(1)} %maximum_add_fusion.refs_0_), channel_id=1, source_target_pairs={{0,32},{8,40},{16,48},{24,56},{32,0},{40,8},{48,16},{56,24},{64,96... | collective-permute-start | bytes 1327112 | tf_op jit(solution)/shard_map/ppermute | solution.py:314
  50.3 22.7 %collective-permute-start.19 = (bf16[24,9216]{1,0:T(8,128)(2,1)S(1)}, bf16[24,9216]{1,0:T(8,128)(2,1)}, u32[]{:S(2)}, u32[]{:S(2)}) collective-permute-start(bf16[24,9216]{1,0:T(8,128)(2,1)S(1)} %maximum_add_fusion.refs_0_), channel_id=1, source_target_pairs={{0,48},{8,56},{16,32},{24,40},{32,16},{40,24},{48,0},{56,8},{64,11... | collective-permute-start | bytes 1327112 | tf_op jit(solution)/shard_map/ppermute | solution.py:314
  50.3 22.7 %collective-permute-start.13 = (bf16[24,9216]{1,0:T(8,128)(2,1)S(1)}, bf16[24,9216]{1,0:T(8,128)(2,1)S(1)}, u32[]{:S(2)}, u32[]{:S(2)}) collective-permute-start(bf16[24,9216]{1,0:T(8,128)(2,1)S(1)} %add_add_fusion), channel_id=1, source_target_pairs={{0,64},{16,80},{32,96},{48,112},{136,200},{152,216},{168,232},{184... | collective-permute-start | bytes 1327112 | tf_op jit(solution)/shard_map/ppermute | solution.py:314
  51.0 22.0 %collective-permute-start.14 = (bf16[24,9216]{1,0:T(8,128)(2,1)S(1)}, bf16[24,9216]{1,0:T(8,128)(2,1)S(1)}, u32[]{:S(2)}, u32[]{:S(2)}) collective-permute-start(bf16[24,9216]{1,0:T(8,128)(2,1)S(1)} %add_add_fusion), channel_id=1, source_target_pairs={{0,192},{16,208},{32,224},{48,240},{136,72},{152,88},{168,104},{18... | collective-permute-start | bytes 1327112 | tf_op jit(solution)/shard_map/ppermute | solution.py:314
  56.3 20.1 %collective-permute-start.27 = (bf16[24,9216]{1,0:T(8,128)(2,1)S(1)}, bf16[24,9216]{1,0:T(8,128)(2,1)S(1)}, u32[]{:S(2)}, u32[]{:S(2)}) collective-permute-start(bf16[24,9216]{1,0:T(8,128)(2,1)S(1)} %collective-permute-done.17.refs_1_), channel_id=1, source_target_pairs={{0,8},{8,0},{16,24},{24,16},{32,40},{40,32},{48,56},{56,48},{64,72... | collective-permute-start | bytes 1327112 | tf_op jit(solution)/shard_map/ppermute | solution.py:314
  70.4 6.7 %collective-permute-start.28 = (bf16[24,9216]{1,0:T(8,128)(2,1)}, bf16[24,9216]{1,0:T(8,128)(2,1)S(1)}, u32[]{:S(2)}, u32[]{:S(2)}) collective-permute-start(bf16[24,9216]{1,0:T(8,128)(2,1)} %collective-permute-done.18.refs_2_), channel_id=1, source_target_pairs={{0,8},{8,0},{16,24},{24,16},{32,40},{40,32},{48,56},{56,48},{64,72... | collective-permute-start | bytes 1327112 | tf_op jit(solution)/shard_map/ppermute | solution.py:314
  73.0 4.9 %collective-permute-start.29 = (bf16[24,9216]{1,0:T(8,128)(2,1)}, bf16[24,9216]{1,0:T(8,128)(2,1)S(1)}, u32[]{:S(2)}, u32[]{:S(2)}) collective-permute-start(bf16[24,9216]{1,0:T(8,128)(2,1)} %collective-permute-done.19.refs_3_), channel_id=1, source_target_pairs={{0,8},{8,0},{16,24},{24,16},{32,40},{40,32},{48,56},{56,48},{64,72... | collective-permute-start | bytes 1327112 | tf_op jit(solution)/shard_map/ppermute | solution.py:314
  73.8 15.0 %collective-permute-start.15 = (bf16[24,4608]{1,0:T(8,128)(2,1)}, bf16[24,4608]{1,0:T(8,128)(2,1)}, u32[]{:S(2)}, u32[]{:S(2)}) collective-permute-start(bf16[24,4608]{1,0:T(8,128)(2,1)} %get-tuple-element.25), channel_id=1, source_target_pairs={{64,128},{80,144},{96,160},{112,176},{200,8},{216,24},{232,40},{24... | collective-permute-start | bytes 663560 | tf_op jit(solution)/shard_map/ppermute | solution.py:314
  75.1 13.7 %collective-permute-start.16 = (bf16[24,4608]{1,0:T(8,128)(2,1)S(1)}, bf16[24,4608]{1,0:T(8,128)(2,1)}, u32[]{:S(2)}, u32[]{:S(2)}) collective-permute-start(bf16[24,4608]{1,0:T(8,128)(2,1)S(1)} %get-tuple-element.26), channel_id=1, source_target_pairs={{192,128},{208,144},{224,160},{240,176},{72,8},{88,24},{104,40},{1... | collective-permute-start | bytes 663560 | tf_op jit(solution)/shard_map/ppermute | solution.py:314
  90.0 52.9 %all-to-all-start.2 = ((bf16[8,2,6,48,384]{4,3,2,1,0:T(8,128)(2,1)}), bf16[8,2,6,48,384]{4,3,2,1,0:T(8,128)(2,1)}, u32[]{:S(2)}, u32[]{:S(2)}) async-start(bf16[8,2,6,48,384]{4,3,2,1,0:T(8,128)(2,1)} %forward_zy.3), calls=%async_computation.2 | async-start | bytes 7077888 | tf_op jit(solution)/shard_map/all_to_all | solution.py:306
  99.6 13.2 %collective-permute-start.20 = (bf16[24,9216]{1,0:T(8,128)(2,1)S(1)}, bf16[24,9216]{1,0:T(8,128)(2,1)S(1)}, u32[]{:S(2)}, u32[]{:S(2)}) collective-permute-start(bf16[24,9216]{1,0:T(8,128)(2,1)S(1)} %maximum_add_fusion.1.refs_0_), channel_id=1, source_target_pairs={{0,16},{8,24},{16,0},{24,8},{32,48},{40,56},{48,32},{56,40},{64,80... | collective-permute-start | bytes 1327112 | tf_op jit(solution)/shard_map/ppermute | solution.py:314
  99.9 21.7 %collective-permute-start.21 = (bf16[24,9216]{1,0:T(8,128)(2,1)S(1)}, bf16[24,9216]{1,0:T(8,128)(2,1)S(1)}, u32[]{:S(2)}, u32[]{:S(2)}) collective-permute-start(bf16[24,9216]{1,0:T(8,128)(2,1)S(1)} %maximum_add_fusion.1.refs_0_), channel_id=1, source_target_pairs={{0,32},{8,40},{16,48},{24,56},{32,0},{40,8},{48,16},{56,24},{64,96... | collective-permute-start | bytes 1327112 | tf_op jit(solution)/shard_map/ppermute | solution.py:314
  101.6 22.5 %collective-permute-start.22 = (bf16[24,9216]{1,0:T(8,128)(2,1)S(1)}, bf16[24,9216]{1,0:T(8,128)(2,1)S(1)}, u32[]{:S(2)}, u32[]{:S(2)}) collective-permute-start(bf16[24,9216]{1,0:T(8,128)(2,1)S(1)} %maximum_add_fusion.1.refs_0_), channel_id=1, source_target_pairs={{0,48},{8,56},{16,32},{24,40},{32,16},{40,24},{48,0},{56,8},{64,11... | collective-permute-start | bytes 1327112 | tf_op jit(solution)/shard_map/ppermute | solution.py:314
  104.5 19.6 %collective-permute-start.23 = (bf16[24,9216]{1,0:T(8,128)(2,1)S(1)}, bf16[24,9216]{1,0:T(8,128)(2,1)S(1)}, u32[]{:S(2)}, u32[]{:S(2)}) collective-permute-start(bf16[24,9216]{1,0:T(8,128)(2,1)S(1)} %maximum_add_fusion.1.refs_0_), channel_id=1, source_target_pairs={{0,8},{8,0},{16,24},{24,16},{32,40},{40,32},{48,56},{56,48},{64,72... | collective-permute-start | bytes 1327112 | tf_op jit(solution)/shard_map/ppermute | solution.py:314
  112.8 11.3 %collective-permute-start.24 = (bf16[24,9216]{1,0:T(8,128)(2,1)S(1)}, bf16[24,9216]{1,0:T(8,128)(2,1)S(1)}, u32[]{:S(2)}, u32[]{:S(2)}) collective-permute-start(bf16[24,9216]{1,0:T(8,128)(2,1)S(1)} %collective-permute-done.20.refs_1_), channel_id=1, source_target_pairs={{0,8},{8,0},{16,24},{24,16},{32,40},{40,32},{48,56},{56,48},{64,72... | collective-permute-start | bytes 1327112 | tf_op jit(solution)/shard_map/ppermute | solution.py:314
  142.9 46.9 %all-to-all-start = ((bf16[8,2,6,48,384]{4,3,2,1,0:T(8,128)(2,1)}), bf16[8,2,6,48,384]{4,3,2,1,0:T(8,128)(2,1)}, u32[]{:S(2)}, u32[]{:S(2)}) async-start(bf16[8,2,6,48,384]{4,3,2,1,0:T(8,128)(2,1)} %forward_zy.2), calls=%async_computation | async-start | bytes 7077888 | tf_op jit(solution)/shard_map/all_to_all | solution.py:306
  189.8 55.1 %all-to-all-start.3 = ((bf16[8,2,6,48,384]{4,3,2,1,0:T(8,128)(2,1)}), bf16[8,2,6,48,384]{4,3,2,1,0:T(8,128)(2,1)}, u32[]{:S(2)}, u32[]{:S(2)}) async-start(bf16[8,2,6,48,384]{4,3,2,1,0:T(8,128)(2,1)} %middle_x.3), calls=%async_computation.3 | async-start | bytes 7077888 | tf_op jit(solution)/shard_map/all_to_all | solution.py:306
  244.8 45.4 %all-to-all-start.1 = ((bf16[8,2,6,48,384]{4,3,2,1,0:T(8,128)(2,1)}), bf16[8,2,6,48,384]{4,3,2,1,0:T(8,128)(2,1)}, u32[]{:S(2)}, u32[]{:S(2)}) async-start(bf16[8,2,6,48,384]{4,3,2,1,0:T(8,128)(2,1)} %middle_x.2), calls=%async_computation.1 | async-start | bytes 7077888 | tf_op jit(solution)/shard_map/all_to_all | solution.py:306
  (24 other events, 159.2 us)

commit v6 on v5

--- a/solution.py
+++ b/solution.py
@@ -1,3 +1,5 @@
+import functools
+
 import jax
 import jax.numpy as jnp
 import numpy as np
@@ -14,6 +16,7 @@
 CELLS = SIDE * SIDE
 COUL = 160.0
 PITCH = 104
+CUT = CELLS // 4
 PER_CUT = DUOS // 4
 PIECE = (QUADS, 2 * ROWS, 384)
 VECTOR = pl.BlockSpec(memory_space=pltpu.VMEM)
@@ -82,50 +85,47 @@
     return copies
 
 
-def forward_body(column, far_target, *refs):
-    pairs = (len(refs) - 9) // 9
-    far_sources, (z_tables, y_table, far_out), refs = refs[: 4 * pairs], refs[4 * pairs : 4 * pairs + 3], refs[4 * pairs + 3 :]
-    lots, (arrived, left, target), sources, outs = refs[:3], refs[3:6], refs[6 : 6 + 4 * pairs], refs[6 + 4 * pairs :]
-    copies = started([(far_target, target), *zip(far_sources, sources)], arrived)
-    copies[0].wait()
+def forward_body(which, column, far_orbitals, *refs):
+    far_sources, (z_tables, y_table), far_out, refs = refs[:4], refs[4:6], refs[-15], refs[-14:]
+    lots, (arrived, left), targets, sources, out = refs[:3], refs[3:5], refs[5:9], refs[9:13], refs[13]
+    brought = []
+    for slot in range(4):
+        here = pl.ds(pl.multiple_of((column[0] ^ slot) * CUT, 128), CUT)
+        brought += [(far_orbitals.at[0, :, here], targets[slot]), (far_sources[slot], sources[slot])]
+    copies = started(brought, arrived)
+    for slot in range(4):
+        target, source = targets[slot], sources[slot]
+        copies[2 * slot].wait()
+        copies[2 * slot + 1].wait()
+
+        def form(part, carry, target=target, source=source, slot=slot):
+            duo = (column[0] ^ slot) * PER_CUT + part
+            here = pl.ds(pl.multiple_of(part * 384, 128), 384)
+            density = target[:, here].astype(F32) * source[:, here].astype(F32)
+            for tile, lot in enumerate(lots):
+                lot[pl.ds(duo, ROWS, stride=PITCH), :] = density[:, tile * 128 : (tile + 1) * 128]
+            return carry
+
+        lax.fori_loop(0, PER_CUT, form, 0, unroll=12)
+
     results = []
-    for which in range(pairs):
-        out = outs[which]
-        for slot in range(4):
-            source = sources[which * 4 + slot]
-            copies[1 + which * 4 + slot].wait()
-
-            def form(part, carry, source=source, slot=slot):
-                duo = (column[0] ^ slot) * PER_CUT + part
-                left = target[:, pl.ds(pl.multiple_of(duo * 384, 128), 384)].astype(F32)
-                right = source[:, pl.ds(pl.multiple_of(part * 384, 128), 384)].astype(F32)
-                density = left * right
-                for tile, lot in enumerate(lots):
-                    lot[pl.ds(duo, ROWS, stride=PITCH), :] = density[:, tile * 128 : (tile + 1) * 128]
-                return carry
-
-            lax.fori_loop(0, PER_CUT, form, 0, unroll=12)
-
-        def planes(quad, carry, out=out):
-            along_z = []
-            for pair in range(2):
-                halves = []
-                for plane in range(2):
-                    rows = pl.ds(pl.multiple_of((quad * 4 + pair * 2 + plane) * PITCH, 8), DUOS)
-                    density = tiles(lots, rows).astype(BF16)
-                    even = dot(density[:, :256], z_tables[2 * plane])
-                    odd = dot(density[:, 128:], z_tables[2 * plane + 1])
-                    halves.append(jnp.concatenate([even, odd], axis=0))
-                low, high = halves
-                along_z += [low[:, :128], high[:, :128], low[:, 128:] + high[:, 128:]]
-            along_y = dot(y_table[...], jnp.concatenate(along_z, axis=1).astype(BF16))
-            for part in range(PARTS):
-                rows = slice(part * ROWS, (part + 1) * ROWS)
-                out[part, quad] = jnp.concatenate([along_y[rows, :384], along_y[rows, 384:]], axis=0).astype(BF16)
-            return carry
-
-        lax.fori_loop(0, QUADS, planes, 0, unroll=6)
-        results.append(pltpu.make_async_copy(out, far_out.at[:, which], left.at[which]))
+    for quad in range(QUADS):
+        along_z = []
+        for pair in range(2):
+            halves = []
+            for plane in range(2):
+                row = (quad * 4 + pair * 2 + plane) * PITCH
+                density = tiles(lots, slice(row, row + DUOS)).astype(BF16)
+                even = dot(density[:, :256], z_tables[2 * plane])
+                odd = dot(density[:, 128:], z_tables[2 * plane + 1])
+                halves.append(jnp.concatenate([even, odd], axis=0))
+            low, high = halves
+            along_z += [low[:, :128], high[:, :128], low[:, 128:] + high[:, 128:]]
+        along_y = dot(y_table[...], jnp.concatenate(along_z, axis=1).astype(BF16))
+        for part in range(PARTS):
+            rows = slice(part * ROWS, (part + 1) * ROWS)
+            out[part, quad] = jnp.concatenate([along_y[rows, :384], along_y[rows, 384:]], axis=0).astype(BF16)
+        results.append(pltpu.make_async_copy(out.at[:, quad], far_out.at[:, which, quad], left.at[quad]))
         results[-1].start()
     for copy in results:
         copy.wait()
@@ -135,22 +135,28 @@
     return pl.CostEstimate(flops=pairs * 1400 * 10**6, bytes_accessed=pairs * 7 * 10**6, transcendentals=0)
 
 
-def forward(column, target, sources):
-    cuts = [cut for source in sources for cut in source]
-    pairs = len(sources)
+def forward(column, orbitals, source, which, pieces):
     return pl.pallas_call(
-        forward_body,
-        in_specs=[SCALAR] + [FAR] * (1 + len(cuts)) + [VECTOR] * 2,
+        functools.partial(forward_body, which),
+        in_specs=[SCALAR] + [FAR] * 5 + [VECTOR] * 2 + [FAR] * (pieces is not None),
         out_specs=FAR,
-        out_shape=jax.ShapeDtypeStruct((PARTS, pairs, *PIECE), BF16),
+        out_shape=jax.ShapeDtypeStruct((PARTS, 2, *PIECE), BF16),
+        input_output_aliases={} if pieces is None else {8: 0},
         scratch_shapes=[pltpu.VMEM((ROWS * PITCH, 128), F32)] * 3
-        + [pltpu.SemaphoreType.DMA((1 + len(cuts),)), pltpu.SemaphoreType.DMA((pairs,)), pltpu.VMEM(target.shape, BF16)]
-        + [pltpu.VMEM(cut.shape, BF16) for cut in cuts]
-        + [pltpu.VMEM((PARTS, *PIECE), BF16)] * pairs,
+        + [pltpu.SemaphoreType.DMA((8,)), pltpu.SemaphoreType.DMA((QUADS,))]
+        + [pltpu.VMEM((ROWS, CUT), BF16)] * 8
+        + [pltpu.VMEM((PARTS, *PIECE), BF16)],
         compiler_params=pltpu.CompilerParams(vmem_limit_bytes=62 * 2**20),
-        cost_estimate=cost(pairs),
+        cost_estimate=cost(1),
         name="forward_zy",
-    )(column, target, *cuts, jnp.asarray(Z_TABLES, BF16), jnp.asarray(Y_TABLE, BF16))
+    )(
+        column,
+        orbitals,
+        *source,
+        jnp.asarray(Z_TABLES, BF16),
+        jnp.asarray(Y_TABLE, BF16),
+        *([] if pieces is None else [pieces]),
+    )
 
 
 def middle_body(far_pieces, far_kernel, x_table, x_back, far_out, head0, head1, tail, arrived, left, kernel, *pieces):
@@ -229,13 +235,13 @@
 def backward_body(column, far_pieces, *refs):
     pairs = far_pieces.shape[1]
     far_sources, refs = refs[: 4 * pairs], refs[4 * pairs :]
-    far_total = refs[0] if len(refs) == 10 + 5 * pairs else None
+    far_total = refs[0] if len(refs) == 7 + 8 * pairs else None
     y_table, z_tables, far_out, *refs = refs[far_total is not None :]
-    lots, (out, arrived, left), pieces, sources = refs[:3], refs[3:6], refs[6 : 6 + pairs], refs[6 + pairs :]
-    total = None if far_total is None else out
+    (out, arrived, left), refs = refs[:3], refs[3:]
+    lots = [refs[3 * i : 3 * i + 3] for i in range(pairs)]
+    pieces, sources = refs[3 * pairs : 4 * pairs], refs[4 * pairs :]
     brought = [(far_pieces.at[:, i], piece) for i, piece in enumerate(pieces)] + list(zip(far_sources, sources))
-    copies = started(brought + ([] if total is None else [(far_total, out)]), arrived)
-    results = []
+    copies = started(brought + ([] if far_total is None else [(far_total, out)]), arrived)
 
     for which in range(pairs):
         copies[which].wait()
@@ -253,34 +259,33 @@
                     even = dot(lanes[:DUOS], z_tables[2 * plane])
                     odd = dot(lanes[DUOS:], z_tables[2 * plane + 1])
                     rows = pl.ds(pl.multiple_of((quad * 4 + pair * 2 + plane) * PITCH, 8), DUOS)
-                    lots[0][rows, :] = even[:, :128]
-                    lots[1][rows, :] = even[:, 128:] + odd[:, :128]
-                    lots[2][rows, :] = odd[:, 128:]
+                    lots[which][0][rows, :] = even[:, :128]
+                    lots[which][1][rows, :] = even[:, 128:] + odd[:, :128]
+                    lots[which][2][rows, :] = odd[:, 128:]
             return carry
 
         lax.fori_loop(0, QUADS, planes, 0, unroll=6)
-        base = total if which == 0 else out
-
-        for slot in range(4):
-            source = sources[which * 4 + slot]
-            copies[pairs + which * 4 + slot].wait()
-            if which == 0 and slot == 0 and total is not None:
-                copies[-1].wait()
-
-            def gather(part, carry, source=source, slot=slot, base=base):
-                duo = (column[0] ^ slot) * PER_CUT + part
-                potential = tiles(lots, pl.ds(duo, ROWS, stride=PITCH))
-                here = pl.ds(pl.multiple_of(duo * 384, 128), 384)
-                right = source[:, pl.ds(pl.multiple_of(part * 384, 128), 384)].astype(F32)
-                term = potential * right
-                out[:, here] = -term if base is None else base[:, here] - term
-                return carry
-
-            lax.fori_loop(0, PER_CUT, gather, 0, unroll=12)
-            if which == pairs - 1:
-                here = pl.ds(pl.multiple_of((column[0] ^ slot) * (CELLS // 4), 128), CELLS // 4)
-                results.append(pltpu.make_async_copy(out.at[:, here], far_out.at[:, here], left.at[slot]))
-                results[-1].start()
+
+    for copy in copies[pairs:]:
+        copy.wait()
+    results = []
+    for slot in range(4):
+
+        def gather(part, carry, slot=slot):
+            duo = (column[0] ^ slot) * PER_CUT + part
+            here = pl.ds(pl.multiple_of(duo * 384, 128), 384)
+            there = pl.ds(pl.multiple_of(part * 384, 128), 384)
+            term = 0.0 if far_total is None else out[:, here]
+            for which in range(pairs):
+                potential = tiles(lots[which], pl.ds(duo, ROWS, stride=PITCH))
+                term = term - potential * sources[which * 4 + slot][:, there].astype(F32)
+            out[:, here] = term
+            return carry
+
+        lax.fori_loop(0, PER_CUT, gather, 0, unroll=12)
+        here = pl.ds(pl.multiple_of((column[0] ^ slot) * CUT, 128), CUT)
+        results.append(pltpu.make_async_copy(out.at[:, here], far_out.at[:, here], left.at[slot]))
+        results[-1].start()
     for copy in results:
         copy.wait()
 
@@ -292,8 +297,9 @@
         in_specs=[SCALAR] + [FAR] * (1 + len(cuts) + (total is not None)) + [VECTOR] * 2,
         out_specs=FAR,
         out_shape=jax.ShapeDtypeStruct((ROWS, CELLS), F32),
-        scratch_shapes=[pltpu.VMEM((ROWS * PITCH, 128), F32)] * 3
-        + [pltpu.VMEM((ROWS, CELLS), F32), pltpu.SemaphoreType.DMA((6 * len(sources),)), pltpu.SemaphoreType.DMA((4,))]
+        scratch_shapes=[pltpu.VMEM((ROWS, CELLS), F32)]
+        + [pltpu.SemaphoreType.DMA((6 * len(sources),)), pltpu.SemaphoreType.DMA((4,))]
+        + [pltpu.VMEM((ROWS * PITCH, 128), F32)] * (3 * len(sources))
         + [pltpu.VMEM((PARTS, *PIECE), BF16)] * len(sources)
         + [pltpu.VMEM(cut.shape, BF16) for cut in cuts],
         compiler_params=pltpu.CompilerParams(vmem_limit_bytes=62 * 2**20),
@@ -318,11 +324,10 @@
     return lax.optimization_barrier((array, *others))[0]
 
 
-def scatter(orbital):
-    cut = CELLS // 4
+def scatter(orbitals, which):
     return sum(
         move(
-            orbital[:, step * cut : (step + 1) * cut],
+            orbitals[which, :, step * CUT : (step + 1) * CUT],
             [(band_of(2 * root, 0, 0), band_of(2 * root, step, root)) for root in range(2)],
         )
         for step in range(4)
@@ -362,19 +367,20 @@
     z_hi, x, core = band // 8, (band // 2) % 4, band % 2
     column = x[None].astype(jnp.int32)
     kernel = coulomb(lax.axis_index("grid"))
-    target = orbitals[0]
     is_root = z_hi == 2 * core
 
-    cut_0 = scatter(orbitals[0])
-    cut_1 = scatter(after(orbitals[1], cut_0))
-    full_0 = beyond(after(beside(cut_0, is_root), cut_1))
+    cut_0 = scatter(orbitals, 0)
+    cut_1 = scatter(after(orbitals, cut_0), 1)
+    full_0 = beyond(beside(cut_0, is_root))
     mine_0 = gather_x(full_0)
+    full_1 = beyond(beside(after(cut_1, full_0), is_root))
     batch_0 = [mine_0, other_core(mine_0)]
-    full_1 = beyond(beside(after(cut_1, batch_0[1][0]), is_root))
-    pieces_0 = after(forward(column, target, batch_0), full_1)
+    pieces_0 = forward(column, orbitals, mine_0, 0, None)
+    pieces_0 = after(forward(column, orbitals, batch_0[1], 1, pieces_0), full_1)
     mine_1 = gather_x(after(full_1, *mine_0))
     batch_1 = [mine_1, other_core(mine_1)]
-    pieces_1 = forward(column, target, batch_1)
+    pieces_1 = forward(column, orbitals, mine_1, 0, None)
+    pieces_1 = forward(column, orbitals, batch_1[1], 1, pieces_1)
     back_0 = exchange(middle(exchange(pieces_0), kernel))
     back_1 = exchange(middle(exchange(pieces_1), kernel))
     total = backward(column, back_0, batch_0, None)

time: 306 us -> 297 us (0.971)
  the two profiles are of different devices: /device:TPU:134 before, /device:TPU:32 now
where the time goes in v6:
time: 297 us; the launch traced here: 292 us
  waiting for transfers between devices  132 us (44%)
  starting transfers between devices  80.4 us (27%)
  Pallas kernels  67.8 us (23%)
  other arithmetic  5.55 us (2%)
  local copies, waits for them, and re-layouts  5.24 us (2%)
    all_to_all x4, waiting for transfers between devices, exchange(): return lax.all_to_all(pieces, 'grid', 0, 0, tiled=True)  89.2 us
    ppermute x30, starting transfers between devices, move(): return lax.ppermute(array, 'band', pairs)  48 us
    ppermute x30, waiting for transfers between devices, move(): return lax.ppermute(array, 'band', pairs)  43.2 us
    all_to_all x4, starting transfers between devices, exchange(): return lax.all_to_all(pieces, 'grid', 0, 0, tiled=True)  32.3 us
    pallas_call x4, Pallas kernels, forward(): pl.pallas_call(functools.partial(forward_body, which), in_specs=[SCALAR]...  24.5 us
    pallas_call x2, Pallas kernels, middle(): pl.pallas_call(middle_body, in_specs=[FAR, FAR, VECTOR, VECTOR], out_spec...  24.5 us
    pallas_call x2, Pallas kernels, backward(): pl.pallas_call(backward_body, in_specs=[SCALAR] + [FAR] * (1 + len(cuts)...  18.9 us
  transfers between devices with their start and end apart: 34, of which 15 were waited for; matrix products, arithmetic and copies ran while one was open for 2% of the time, Pallas kernels for 18%

profile of v6, /device:TPU:32, one launch (start us, length us, event | category | flops | bytes accessed | tf_op | source)
XLA Modules:
  0.0 292.0 jit_solution(18003422540072778527)
XLA Ops:
  2.8 5.0 %collective-permute-start = (bf16[24,9216]{1,0:T(8,128)(2,1)}, bf16[24,9216]{1,0:T(8,128)(2,1)}, u32[]{:S(2)}, u32[]{:S(2)}) collective-permute-start(bf16[24,9216]{1,0:T(8,128)(2,1)} %get-tuple-element.20), channel_id=1, source_target_pairs={{0,0},{128,136},{1,1},{129,137},{2,2},{130,138},{3,3},{131,139},{4... | collective-permute-start | bytes 1327112 | tf_op jit(solution)/shard_map/ppermute | solution.py:320
  15.2 4.7 %collective-permute-done.2 = bf16[24,9216]{1,0:T(8,128)(2,1)} collective-permute-done((bf16[24,9216]{1,0:T(8,128)(2,1)}, bf16[24,9216]{1,0:T(8,128)(2,1)}, u32[]{:S(2)}, u32[]{:S(2)}) %collective-permute-start.2) | collective-permute-done | bytes 442400 | tf_op jit(solution)/shard_map/ppermute | solution.py:320
  26.3 5.3 %collective-permute-start.6 = (bf16[24,9216]{1,0:T(8,128)(2,1)S(1)}, bf16[24,9216]{1,0:T(8,128)(2,1)S(1)}, u32[]{:S(2)}, u32[]{:S(2)}) collective-permute-start(bf16[24,9216]{1,0:T(8,128)(2,1)S(1)} %get-tuple-element.15), channel_id=1, source_target_pairs={{0,32},{128,168},{1,33},{129,169},{2,34},{130,170},{3,35},{131,171... | collective-permute-start | bytes 1327112 | tf_op jit(solution)/shard_map/ppermute | solution.py:320
  33.3 5.0 %collective-permute-start.7 = (bf16[24,9216]{1,0:T(8,128)(2,1)S(1)}, bf16[24,9216]{1,0:T(8,128)(2,1)S(1)}, u32[]{:S(2)}, u32[]{:S(2)}) collective-permute-start(bf16[24,9216]{1,0:T(8,128)(2,1)S(1)} %get-tuple-element.14), channel_id=1, source_target_pairs={{0,48},{128,184},{1,49},{129,185},{2,50},{130,186},{3,51},{131,187... | collective-permute-start | bytes 1327112 | tf_op jit(solution)/shard_map/ppermute | solution.py:320
  44.3 6.1 %collective-permute-start.12 = (bf16[24,9216]{1,0:T(8,128)(2,1)S(1)}, bf16[24,9216]{1,0:T(8,128)(2,1)S(1)}, u32[]{:S(2)}, u32[]{:S(2)}) collective-permute-start(bf16[24,9216]{1,0:T(8,128)(2,1)S(1)} %add_add_fusion), channel_id=1, source_target_pairs={{0,64},{16,80},{32,96},{48,112},{136,200},{152,216},{168,232},{184... | collective-permute-start | bytes 1327112 | tf_op jit(solution)/shard_map/ppermute | solution.py:320
  61.8 7.7 %collective-permute-done.17.refs_2_ = bf16[24,9216]{1,0:T(8,128)(2,1)} collective-permute-done((bf16[24,9216]{1,0:T(8,128)(2,1)S(1)}, bf16[24,9216]{1,0:T(8,128)(2,1)}, u32[]{:S(2)}, u32[]{:S(2)}) %collective-permute-start.17) | collective-permute-done | bytes 442400 | tf_op jit(solution)/shard_map/ppermute | solution.py:320
  72.7 6.1 %forward_zy.6.refs_6_ = bf16[8,2,6,48,384]{4,3,2,1,0:T(8,128)(2,1)} custom-call(s32[1]{0:T(128)} %bitcast.column, bf16[2,24,36864]{2,1,0:T(8,128)(2,1)} %far_orbitals.7, bf16[24,9216]{1,0:T(8,128)(2,1)} %copy-done.1, bf16[24,9216]{1,0:T(8,128)(2,1)} %copy-done.3, bf16[24,9216]{1,0:T(8,128)(2,1)} %collective-permute-done.17.refs_2_, ...), custom_call_target="tpu_custom_call" | custom-call | flops 1400000000 | bytes 7000000 | tf_op jit(solution)/shard_map/forward_zy/pallas_call | solution.py:139
  81.1 6.1 %forward_zy.7 = bf16[8,2,6,48,384]{4,3,2,1,0:T(8,128)(2,1)} custom-call(s32[1]{0:T(128)} %bitcast.column, bf16[2,24,36864]{2,1,0:T(8,128)(2,1)} %far_orbitals.7, bf16[24,9216]{1,0:T(8,128)(2,1)} %collective-permute-done.26.refs_0_.refs_4_, bf16[24,9216]{1,0:T(8,128)(2,1)} %collective-permute-done.27.refs_1_.refs_5_, ...), custom_call_target="tpu_custom_call", output_to_operand_aliasing={{}: (8, {})} | custom-call | flops 1400000000 | bytes 7000000 | tf_op jit(solution)/shard_map/forward_zy/pallas_call | solution.py:139
  87.2 6.8 %all-to-all-start.2 = ((bf16[8,2,6,48,384]{4,3,2,1,0:T(8,128)(2,1)}), bf16[8,2,6,48,384]{4,3,2,1,0:T(8,128)(2,1)}, u32[]{:S(2)}, u32[]{:S(2)}) async-start(bf16[8,2,6,48,384]{4,3,2,1,0:T(8,128)(2,1)} %forward_zy.7), calls=%async_computation.2 | async-start | bytes 7077888 | tf_op jit(solution)/shard_map/all_to_all | solution.py:312
  99.0 8.1 %collective-permute-done.20.refs_1_ = bf16[24,9216]{1,0:T(8,128)(2,1)S(1)} collective-permute-done((bf16[24,9216]{1,0:T(8,128)(2,1)S(1)}, bf16[24,9216]{1,0:T(8,128)(2,1)S(1)}, u32[]{:S(2)}, u32[]{:S(2)}) %collective-permute-start.20) | collective-permute-done | bytes 442400 | tf_op jit(solution)/shard_map/ppermute | solution.py:320
  107.1 7.6 %collective-permute-done.22.refs_2_ = bf16[24,9216]{1,0:T(8,128)(2,1)S(1)} collective-permute-done((bf16[24,9216]{1,0:T(8,128)(2,1)S(1)}, bf16[24,9216]{1,0:T(8,128)(2,1)S(1)}, u32[]{:S(2)}, u32[]{:S(2)}) %collective-permute-start.22) | collective-permute-done | bytes 442400 | tf_op jit(solution)/shard_map/ppermute | solution.py:320
  118.8 6.1 %forward_zy.4.refs_6_ = bf16[8,2,6,48,384]{4,3,2,1,0:T(8,128)(2,1)} custom-call(s32[1]{0:T(128)} %bitcast.column, bf16[2,24,36864]{2,1,0:T(8,128)(2,1)} %far_orbitals.7, bf16[24,9216]{1,0:T(8,128)(2,1)} %copy-done.2, bf16[24,9216]{1,0:T(8,128)(2,1)} %copy-done.5, bf16[24,9216]{1,0:T(8,128)(2,1)} %copy-done.6, bf16[24,9216]{1,0:T(8,128)(2,1)} %copy-done.7, ...), custom_call_target="tpu_custom_call" | custom-call | flops 1400000000 | bytes 7000000 | tf_op jit(solution)/shard_map/forward_zy/pallas_call | solution.py:139
  125.0 6.1 %forward_zy.5 = bf16[8,2,6,48,384]{4,3,2,1,0:T(8,128)(2,1)} custom-call(s32[1]{0:T(128)} %bitcast.column, bf16[2,24,36864]{2,1,0:T(8,128)(2,1)} %far_orbitals.7, bf16[24,9216]{1,0:T(8,128)(2,1)} %collective-permute-done.19.refs_0_.refs_4_, bf16[24,9216]{1,0:T(8,128)(2,1)} %collective-permute-done.21.refs_1_.refs_5_, ...), custom_call_target="tpu_custom_call", output_to_operand_aliasing={{}: (8, {})} | custom-call | flops 1400000000 | bytes 7000000 | tf_op jit(solution)/shard_map/forward_zy/pallas_call | solution.py:139
  131.1 4.8 %all-to-all-done.2.far_pieces = bf16[8,2,6,48,384]{4,3,2,1,0:T(8,128)(2,1)} async-done(((bf16[8,2,6,48,384]{4,3,2,1,0:T(8,128)(2,1)}), bf16[8,2,6,48,384]{4,3,2,1,0:T(8,128)(2,1)}, u32[]{:S(2)}, u32[]{:S(2)}) %all-to-all-start.2) | async-done | bytes 3538976 | tf_op jit(solution)/shard_map/all_to_all | solution.py:312
  135.9 5.6 %all-to-all-start = ((bf16[8,2,6,48,384]{4,3,2,1,0:T(8,128)(2,1)}), bf16[8,2,6,48,384]{4,3,2,1,0:T(8,128)(2,1)}, u32[]{:S(2)}, u32[]{:S(2)}) async-start(bf16[8,2,6,48,384]{4,3,2,1,0:T(8,128)(2,1)} %forward_zy.5), calls=%async_computation | async-start | bytes 7077888 | tf_op jit(solution)/shard_map/all_to_all | solution.py:312
  144.1 12.2 %middle_x.3 = bf16[8,2,6,48,384]{4,3,2,1,0:T(8,128)(2,1)} custom-call(bf16[8,2,6,48,384]{4,3,2,1,0:T(8,128)(2,1)} %all-to-all-done.2.far_pieces, f32[12,192,384]{2,1,0:T(8,128)} %select_multiply_fusion.far_kernel, bf16[192,192]{1,0:T(8,128)(2,1)} %constant.117.clone.refs_5_.x_table, bf16[192,192]{1,0:T(8,128)(2,1)} %constant.118.clone.x_back.refs_8_.refs_9_), custom_call_target="tpu_custom_call" | custom-call | flops 2800000000 | bytes 14000000 | tf_op jit(solution)/shard_map/middle_x/pallas_call | solution.py:221
  156.4 26.2 %all-to-all-done.far_pieces = bf16[8,2,6,48,384]{4,3,2,1,0:T(8,128)(2,1)} async-done(((bf16[8,2,6,48,384]{4,3,2,1,0:T(8,128)(2,1)}), bf16[8,2,6,48,384]{4,3,2,1,0:T(8,128)(2,1)}, u32[]{:S(2)}, u32[]{:S(2)}) %all-to-all-start) | async-done | bytes 3538976 | tf_op jit(solution)/shard_map/all_to_all | solution.py:312
  182.5 14.3 %all-to-all-start.3 = ((bf16[8,2,6,48,384]{4,3,2,1,0:T(8,128)(2,1)}), bf16[8,2,6,48,384]{4,3,2,1,0:T(8,128)(2,1)}, u32[]{:S(2)}, u32[]{:S(2)}) async-start(bf16[8,2,6,48,384]{4,3,2,1,0:T(8,128)(2,1)} %middle_x.3), calls=%async_computation.3 | async-start | bytes 7077888 | tf_op jit(solution)/shard_map/all_to_all | solution.py:312
  196.9 12.2 %middle_x.2 = bf16[8,2,6,48,384]{4,3,2,1,0:T(8,128)(2,1)} custom-call(bf16[8,2,6,48,384]{4,3,2,1,0:T(8,128)(2,1)} %all-to-all-done.far_pieces, f32[12,192,384]{2,1,0:T(8,128)} %select_multiply_fusion.far_kernel, bf16[192,192]{1,0:T(8,128)(2,1)} %constant.117.clone.refs_5_.x_table, bf16[192,192]{1,0:T(8,128)(2,1)} %constant.118.clone.x_back.refs_8_.refs_9_), custom_call_target="tpu_custom_call" | custom-call | flops 2800000000 | bytes 14000000 | tf_op jit(solution)/shard_map/middle_x/pallas_call | solution.py:221
  209.1 27.8 %all-to-all-done.3.far_pieces = bf16[8,2,6,48,384]{4,3,2,1,0:T(8,128)(2,1)} async-done(((bf16[8,2,6,48,384]{4,3,2,1,0:T(8,128)(2,1)}), bf16[8,2,6,48,384]{4,3,2,1,0:T(8,128)(2,1)}, u32[]{:S(2)}, u32[]{:S(2)}) %all-to-all-start.3) | async-done | bytes 3538976 | tf_op jit(solution)/shard_map/all_to_all | solution.py:312
  236.9 5.6 %all-to-all-start.1 = ((bf16[8,2,6,48,384]{4,3,2,1,0:T(8,128)(2,1)}), bf16[8,2,6,48,384]{4,3,2,1,0:T(8,128)(2,1)}, u32[]{:S(2)}, u32[]{:S(2)}) async-start(bf16[8,2,6,48,384]{4,3,2,1,0:T(8,128)(2,1)} %middle_x.2), calls=%async_computation.1 | async-start | bytes 7077888 | tf_op jit(solution)/shard_map/all_to_all | solution.py:312
  242.5 9.4 %backward_yz.2.refs_8_ = f32[24,36864]{1,0:T(8,128)} custom-call(s32[1]{0:T(128)} %bitcast.column, bf16[8,2,6,48,384]{4,3,2,1,0:T(8,128)(2,1)} %all-to-all-done.3.far_pieces, bf16[24,9216]{1,0:T(8,128)(2,1)} %copy-done.1, bf16[24,9216]{1,0:T(8,128)(2,1)} %copy-done.3, bf16[24,9216]{1,0:T(8,128)(2,1)} %collective-permute-done.17.refs_2_, ...), custom_call_target="tpu_custom_call" | custom-call | flops 2800000000 | bytes 14000000 | tf_op jit(solution)/shard_map/backward_yz/pallas_call | solution.py:295
  251.9 30.4 %all-to-all-done.1.far_pieces = bf16[8,2,6,48,384]{4,3,2,1,0:T(8,128)(2,1)} async-done(((bf16[8,2,6,48,384]{4,3,2,1,0:T(8,128)(2,1)}), bf16[8,2,6,48,384]{4,3,2,1,0:T(8,128)(2,1)}, u32[]{:S(2)}, u32[]{:S(2)}) %all-to-all-start.1) | async-done | bytes 3538976 | tf_op jit(solution)/shard_map/all_to_all | solution.py:312
  282.3 9.5 %backward_yz.3 = f32[24,36864]{1,0:T(8,128)} custom-call(s32[1]{0:T(128)} %bitcast.column, bf16[8,2,6,48,384]{4,3,2,1,0:T(8,128)(2,1)} %all-to-all-done.1.far_pieces, bf16[24,9216]{1,0:T(8,128)(2,1)} %copy-done.2, bf16[24,9216]{1,0:T(8,128)(2,1)} %copy-done.5, bf16[24,9216]{1,0:T(8,128)(2,1)} %copy-done.6, bf16[24,9216]{1,0:T(8,128)(2,1)} %copy-done.7, ...), custom_call_target="tpu_custom_call" | custom-call | flops 2800000000 | bytes 14000000 | tf_op jit(solution)/shard_map/backward_yz/pallas_call | solution.py:295
  (87 shorter events, 52.5 us)
Async XLA Ops:
  2.8 11.2 %collective-permute-start = (bf16[24,9216]{1,0:T(8,128)(2,1)}, bf16[24,9216]{1,0:T(8,128)(2,1)}, u32[]{:S(2)}, u32[]{:S(2)}) collective-permute-start(bf16[24,9216]{1,0:T(8,128)(2,1)} %get-tuple-element.20), channel_id=1, source_target_pairs={{0,0},{128,136},{1,1},{129,137},{2,2},{130,138},{3,3},{131,139},{4... | collective-permute-start | bytes 1327112 | tf_op jit(solution)/shard_map/ppermute | solution.py:320
  21.4 11.8 %collective-permute-start.8 = (bf16[24,9216]{1,0:T(8,128)(2,1)S(1)}, bf16[24,9216]{1,0:T(8,128)(2,1)S(1)}, u32[]{:S(2)}, u32[]{:S(2)}) collective-permute-start(bf16[24,9216]{1,0:T(8,128)(2,1)S(1)} %add_add_fusion.1), channel_id=1, source_target_pairs={{0,64},{16,80},{32,96},{48,112},{136,200},{152,216},{168,232},{184... | collective-permute-start | bytes 1327112 | tf_op jit(solution)/shard_map/ppermute | solution.py:320
  22.8 15.5 %collective-permute-start.9 = (bf16[24,9216]{1,0:T(8,128)(2,1)S(1)}, bf16[24,9216]{1,0:T(8,128)(2,1)S(1)}, u32[]{:S(2)}, u32[]{:S(2)}) collective-permute-start(bf16[24,9216]{1,0:T(8,128)(2,1)S(1)} %add_add_fusion.1), channel_id=1, source_target_pairs={{0,192},{16,208},{32,224},{48,240},{136,72},{152,88},{168,104},{18... | collective-permute-start | bytes 1327112 | tf_op jit(solution)/shard_map/ppermute | solution.py:320
  24.2 14.9 %collective-permute-start.4 = (bf16[24,9216]{1,0:T(8,128)(2,1)S(1)}, bf16[24,9216]{1,0:T(8,128)(2,1)S(1)}, u32[]{:S(2)}, u32[]{:S(2)}) collective-permute-start(bf16[24,9216]{1,0:T(8,128)(2,1)S(1)} %get-tuple-element.16), channel_id=1, source_target_pairs={{0,0},{128,136},{1,1},{129,137},{2,2},{130,138},{3,3},{131,139},{4... | collective-permute-start | bytes 1327112 | tf_op jit(solution)/shard_map/ppermute | solution.py:320
  24.9 14.8 %collective-permute-start.5 = (bf16[24,9216]{1,0:T(8,128)(2,1)S(1)}, bf16[24,9216]{1,0:T(8,128)(2,1)S(1)}, u32[]{:S(2)}, u32[]{:S(2)}) collective-permute-start(bf16[24,9216]{1,0:T(8,128)(2,1)S(1)} %get-tuple-element.13), channel_id=1, source_target_pairs={{0,16},{128,152},{1,17},{129,153},{2,18},{130,154},{3,19},{131,155... | collective-permute-start | bytes 1327112 | tf_op jit(solution)/shard_map/ppermute | solution.py:320
  26.3 13.5 %collective-permute-start.6 = (bf16[24,9216]{1,0:T(8,128)(2,1)S(1)}, bf16[24,9216]{1,0:T(8,128)(2,1)S(1)}, u32[]{:S(2)}, u32[]{:S(2)}) collective-permute-start(bf16[24,9216]{1,0:T(8,128)(2,1)S(1)} %get-tuple-element.15), channel_id=1, source_target_pairs={{0,32},{128,168},{1,33},{129,169},{2,34},{130,170},{3,35},{131,171... | collective-permute-start | bytes 1327112 | tf_op jit(solution)/shard_map/ppermute | solution.py:320
  33.3 10.8 %collective-permute-start.7 = (bf16[24,9216]{1,0:T(8,128)(2,1)S(1)}, bf16[24,9216]{1,0:T(8,128)(2,1)S(1)}, u32[]{:S(2)}, u32[]{:S(2)}) collective-permute-start(bf16[24,9216]{1,0:T(8,128)(2,1)S(1)} %get-tuple-element.14), channel_id=1, source_target_pairs={{0,48},{128,184},{1,49},{129,185},{2,50},{130,186},{3,51},{131,187... | collective-permute-start | bytes 1327112 | tf_op jit(solution)/shard_map/ppermute | solution.py:320
  44.3 12.9 %collective-permute-start.12 = (bf16[24,9216]{1,0:T(8,128)(2,1)S(1)}, bf16[24,9216]{1,0:T(8,128)(2,1)S(1)}, u32[]{:S(2)}, u32[]{:S(2)}) collective-permute-start(bf16[24,9216]{1,0:T(8,128)(2,1)S(1)} %add_add_fusion), channel_id=1, source_target_pairs={{0,64},{16,80},{32,96},{48,112},{136,200},{152,216},{168,232},{184... | collective-permute-start | bytes 1327112 | tf_op jit(solution)/shard_map/ppermute | solution.py:320
  52.5 17.0 %collective-permute-start.17 = (bf16[24,9216]{1,0:T(8,128)(2,1)S(1)}, bf16[24,9216]{1,0:T(8,128)(2,1)}, u32[]{:S(2)}, u32[]{:S(2)}) collective-permute-start(bf16[24,9216]{1,0:T(8,128)(2,1)S(1)} %maximum_add_fusion.refs_0_), channel_id=1, source_target_pairs={{0,32},{8,40},{16,48},{24,56},{32,0},{40,8},{48,16},{56,24},{64,96... | collective-permute-start | bytes 1327112 | tf_op jit(solution)/shard_map/ppermute | solution.py:320
  52.6 19.4 %collective-permute-start.18 = (bf16[24,9216]{1,0:T(8,128)(2,1)S(1)}, bf16[24,9216]{1,0:T(8,128)(2,1)S(1)}, u32[]{:S(2)}, u32[]{:S(2)}) collective-permute-start(bf16[24,9216]{1,0:T(8,128)(2,1)S(1)} %maximum_add_fusion.refs_0_), channel_id=1, source_target_pairs={{0,48},{8,56},{16,32},{24,40},{32,16},{40,24},{48,0},{56,8},{64,11... | collective-permute-start | bytes 1327112 | tf_op jit(solution)/shard_map/ppermute | solution.py:320
  59.1 19.8 %collective-permute-start.14 = (bf16[24,4608]{1,0:T(8,128)(2,1)}, bf16[24,4608]{1,0:T(8,128)(2,1)}, u32[]{:S(2)}, u32[]{:S(2)}) collective-permute-start(bf16[24,4608]{1,0:T(8,128)(2,1)} %get-tuple-element.21), channel_id=1, source_target_pairs={{64,128},{80,144},{96,160},{112,176},{200,8},{216,24},{232,40},{24... | collective-permute-start | bytes 663560 | tf_op jit(solution)/shard_map/ppermute | solution.py:320
  60.4 18.5 %collective-permute-start.15 = (bf16[24,4608]{1,0:T(8,128)(2,1)S(1)}, bf16[24,4608]{1,0:T(8,128)(2,1)}, u32[]{:S(2)}, u32[]{:S(2)}) collective-permute-start(bf16[24,4608]{1,0:T(8,128)(2,1)S(1)} %get-tuple-element.22), channel_id=1, source_target_pairs={{192,128},{208,144},{224,160},{240,176},{72,8},{88,24},{104,40},{1... | collective-permute-start | bytes 663560 | tf_op jit(solution)/shard_map/ppermute | solution.py:320
  61.8 18.3 %collective-permute-start.26 = (bf16[24,9216]{1,0:T(8,128)(2,1)S(1)}, bf16[24,9216]{1,0:T(8,128)(2,1)}, u32[]{:S(2)}, u32[]{:S(2)}) collective-permute-start(bf16[24,9216]{1,0:T(8,128)(2,1)S(1)} %maximum_add_fusion.refs_0_), channel_id=1, source_target_pairs={{0,8},{8,0},{16,24},{24,16},{32,40},{40,32},{48,56},{56,48},{64,72... | collective-permute-start | bytes 1327112 | tf_op jit(solution)/shard_map/ppermute | solution.py:320
  69.5 10.7 %collective-permute-start.27 = (bf16[24,9216]{1,0:T(8,128)(2,1)S(1)}, bf16[24,9216]{1,0:T(8,128)(2,1)}, u32[]{:S(2)}, u32[]{:S(2)}) collective-permute-start(bf16[24,9216]{1,0:T(8,128)(2,1)S(1)} %collective-permute-done.16.refs_1_), channel_id=1, source_target_pairs={{0,8},{8,0},{16,24},{24,16},{32,40},{40,32},{48,56},{56,48},{64,72... | collective-permute-start | bytes 1327112 | tf_op jit(solution)/shard_map/ppermute | solution.py:320
  87.2 48.7 %all-to-all-start.2 = ((bf16[8,2,6,48,384]{4,3,2,1,0:T(8,128)(2,1)}), bf16[8,2,6,48,384]{4,3,2,1,0:T(8,128)(2,1)}, u32[]{:S(2)}, u32[]{:S(2)}) async-start(bf16[8,2,6,48,384]{4,3,2,1,0:T(8,128)(2,1)} %forward_zy.7), calls=%async_computation.2 | async-start | bytes 7077888 | tf_op jit(solution)/shard_map/all_to_all | solution.py:312
  94.1 13.1 %collective-permute-start.20 = (bf16[24,9216]{1,0:T(8,128)(2,1)S(1)}, bf16[24,9216]{1,0:T(8,128)(2,1)S(1)}, u32[]{:S(2)}, u32[]{:S(2)}) collective-permute-start(bf16[24,9216]{1,0:T(8,128)(2,1)S(1)} %maximum_add_fusion.1.refs_0_), channel_id=1, source_target_pairs={{0,16},{8,24},{16,0},{24,8},{32,48},{40,56},{48,32},{56,40},{64,80... | collective-permute-start | bytes 1327112 | tf_op jit(solution)/shard_map/ppermute | solution.py:320
  94.1 20.7 %collective-permute-start.22 = (bf16[24,9216]{1,0:T(8,128)(2,1)S(1)}, bf16[24,9216]{1,0:T(8,128)(2,1)S(1)}, u32[]{:S(2)}, u32[]{:S(2)}) collective-permute-start(bf16[24,9216]{1,0:T(8,128)(2,1)S(1)} %maximum_add_fusion.1.refs_0_), channel_id=1, source_target_pairs={{0,32},{8,40},{16,48},{24,56},{32,0},{40,8},{48,16},{56,24},{64,96... | collective-permute-start | bytes 1327112 | tf_op jit(solution)/shard_map/ppermute | solution.py:320
  95.7 22.3 %collective-permute-start.24 = (bf16[24,9216]{1,0:T(8,128)(2,1)S(1)}, bf16[24,9216]{1,0:T(8,128)(2,1)S(1)}, u32[]{:S(2)}, u32[]{:S(2)}) collective-permute-start(bf16[24,9216]{1,0:T(8,128)(2,1)S(1)} %maximum_add_fusion.1.refs_0_), channel_id=1, source_target_pairs={{0,48},{8,56},{16,32},{24,40},{32,16},{40,24},{48,0},{56,8},{64,11... | collective-permute-start | bytes 1327112 | tf_op jit(solution)/shard_map/ppermute | solution.py:320
  99.0 26.0 %collective-permute-start.19 = (bf16[24,9216]{1,0:T(8,128)(2,1)S(1)}, bf16[24,9216]{1,0:T(8,128)(2,1)}, u32[]{:S(2)}, u32[]{:S(2)}) collective-permute-start(bf16[24,9216]{1,0:T(8,128)(2,1)S(1)} %maximum_add_fusion.1.refs_0_), channel_id=1, source_target_pairs={{0,8},{8,0},{16,24},{24,16},{32,40},{40,32},{48,56},{56,48},{64,72... | collective-permute-start | bytes 1327112 | tf_op jit(solution)/shard_map/ppermute | solution.py:320
  107.1 17.9 %collective-permute-start.21 = (bf16[24,9216]{1,0:T(8,128)(2,1)S(1)}, bf16[24,9216]{1,0:T(8,128)(2,1)}, u32[]{:S(2)}, u32[]{:S(2)}) collective-permute-start(bf16[24,9216]{1,0:T(8,128)(2,1)S(1)} %collective-permute-done.20.refs_1_), channel_id=1, source_target_pairs={{0,8},{8,0},{16,24},{24,16},{32,40},{40,32},{48,56},{56,48},{64,72... | collective-permute-start | bytes 1327112 | tf_op jit(solution)/shard_map/ppermute | solution.py:320
  114.8 10.2 %collective-permute-start.23 = (bf16[24,9216]{1,0:T(8,128)(2,1)S(1)}, bf16[24,9216]{1,0:T(8,128)(2,1)}, u32[]{:S(2)}, u32[]{:S(2)}) collective-permute-start(bf16[24,9216]{1,0:T(8,128)(2,1)S(1)} %collective-permute-done.22.refs_2_), channel_id=1, source_target_pairs={{0,8},{8,0},{16,24},{24,16},{32,40},{40,32},{48,56},{56,48},{64,72... | collective-permute-start | bytes 1327112 | tf_op jit(solution)/shard_map/ppermute | solution.py:320
  135.9 46.6 %all-to-all-start = ((bf16[8,2,6,48,384]{4,3,2,1,0:T(8,128)(2,1)}), bf16[8,2,6,48,384]{4,3,2,1,0:T(8,128)(2,1)}, u32[]{:S(2)}, u32[]{:S(2)}) async-start(bf16[8,2,6,48,384]{4,3,2,1,0:T(8,128)(2,1)} %forward_zy.5), calls=%async_computation | async-start | bytes 7077888 | tf_op jit(solution)/shard_map/all_to_all | solution.py:312
  182.5 54.4 %all-to-all-start.3 = ((bf16[8,2,6,48,384]{4,3,2,1,0:T(8,128)(2,1)}), bf16[8,2,6,48,384]{4,3,2,1,0:T(8,128)(2,1)}, u32[]{:S(2)}, u32[]{:S(2)}) async-start(bf16[8,2,6,48,384]{4,3,2,1,0:T(8,128)(2,1)} %middle_x.3), calls=%async_computation.3 | async-start | bytes 7077888 | tf_op jit(solution)/shard_map/all_to_all | solution.py:312
  236.9 45.4 %all-to-all-start.1 = ((bf16[8,2,6,48,384]{4,3,2,1,0:T(8,128)(2,1)}), bf16[8,2,6,48,384]{4,3,2,1,0:T(8,128)(2,1)}, u32[]{:S(2)}, u32[]{:S(2)}) async-start(bf16[8,2,6,48,384]{4,3,2,1,0:T(8,128)(2,1)} %middle_x.2), calls=%async_computation.1 | async-start | bytes 7077888 | tf_op jit(solution)/shard_map/all_to_all | solution.py:312
  (18 other events, 167.7 us)

commit v7 on v6

--- a/solution.py
+++ b/solution.py
@@ -1,5 +1,3 @@
-import functools
-
 import jax
 import jax.numpy as jnp
 import numpy as np
@@ -85,48 +83,57 @@
     return copies
 
 
-def forward_body(which, column, far_orbitals, *refs):
-    far_sources, (z_tables, y_table), far_out, refs = refs[:4], refs[4:6], refs[-15], refs[-14:]
-    lots, (arrived, left), targets, sources, out = refs[:3], refs[3:5], refs[5:9], refs[9:13], refs[13]
+def forward_body(column, far_orbitals, *refs):
+    pairs = (len(refs) - 12) // 9
+    far_sources, (z_tables, y_table, far_out), refs = refs[: 4 * pairs], refs[4 * pairs : 4 * pairs + 3], refs[4 * pairs + 3 :]
+    lots, (arrived, left), targets, refs = refs[:3], refs[3:5], refs[5:9], refs[9:]
+    sources, outs = refs[: 4 * pairs], refs[4 * pairs :]
     brought = []
     for slot in range(4):
         here = pl.ds(pl.multiple_of((column[0] ^ slot) * CUT, 128), CUT)
         brought += [(far_orbitals.at[0, :, here], targets[slot]), (far_sources[slot], sources[slot])]
-    copies = started(brought, arrived)
-    for slot in range(4):
-        target, source = targets[slot], sources[slot]
-        copies[2 * slot].wait()
-        copies[2 * slot + 1].wait()
-
-        def form(part, carry, target=target, source=source, slot=slot):
-            duo = (column[0] ^ slot) * PER_CUT + part
-            here = pl.ds(pl.multiple_of(part * 384, 128), 384)
-            density = target[:, here].astype(F32) * source[:, here].astype(F32)
-            for tile, lot in enumerate(lots):
-                lot[pl.ds(duo, ROWS, stride=PITCH), :] = density[:, tile * 128 : (tile + 1) * 128]
+    copies = started(brought + list(zip(far_sources[4:], sources[4:])), arrived)
+    results = []
+    for which, out in enumerate(outs):
+        for slot in range(4):
+            target, source = targets[slot], sources[4 * which + slot]
+            for copy in copies[2 * slot : 2 * slot + 2] if which == 0 else copies[4 + 4 * which + slot :][:1]:
+                copy.wait()
+
+            def form(part, carry, target=target, source=source, slot=slot):
+                duo = (column[0] ^ slot) * PER_CUT + part
+                here = pl.ds(pl.multiple_of(part * 384, 128), 384)
+                density = target[:, here].astype(F32) * source[:, here].astype(F32)
+                for tile, lot in enumerate(lots):
+                    lot[pl.ds(duo, ROWS, stride=PITCH), :] = density[:, tile * 128 : (tile + 1) * 128]
+                return carry
+
+            lax.fori_loop(0, PER_CUT, form, 0, unroll=12)
+
+        def result(quad, which=which, out=out):
+            return pltpu.make_async_copy(out.at[:, quad], far_out.at[:, which, quad], left.at[which, quad])
+
+        def planes(quad, carry, out=out, result=result):
+            along_z = []
+            for pair in range(2):
+                halves = []
+                for plane in range(2):
+                    rows = pl.ds(pl.multiple_of((quad * 4 + pair * 2 + plane) * PITCH, 8), DUOS)
+                    density = tiles(lots, rows).astype(BF16)
+                    even = dot(density[:, :256], z_tables[2 * plane])
+                    odd = dot(density[:, 128:], z_tables[2 * plane + 1])
+                    halves.append(jnp.concatenate([even, odd], axis=0))
+                low, high = halves
+                along_z += [low[:, :128], high[:, :128], low[:, 128:] + high[:, 128:]]
+            along_y = dot(y_table[...], jnp.concatenate(along_z, axis=1).astype(BF16))
+            for part in range(PARTS):
+                rows = slice(part * ROWS, (part + 1) * ROWS)
+                out[part, quad] = jnp.concatenate([along_y[rows, :384], along_y[rows, 384:]], axis=0).astype(BF16)
+            result(quad).start()
             return carry
 
-        lax.fori_loop(0, PER_CUT, form, 0, unroll=12)
-
-    results = []
-    for quad in range(QUADS):
-        along_z = []
-        for pair in range(2):
-            halves = []
-            for plane in range(2):
-                row = (quad * 4 + pair * 2 + plane) * PITCH
-                density = tiles(lots, slice(row, row + DUOS)).astype(BF16)
-                even = dot(density[:, :256], z_tables[2 * plane])
-                odd = dot(density[:, 128:], z_tables[2 * plane + 1])
-                halves.append(jnp.concatenate([even, odd], axis=0))
-            low, high = halves
-            along_z += [low[:, :128], high[:, :128], low[:, 128:] + high[:, 128:]]
-        along_y = dot(y_table[...], jnp.concatenate(along_z, axis=1).astype(BF16))
-        for part in range(PARTS):
-            rows = slice(part * ROWS, (part + 1) * ROWS)
-            out[part, quad] = jnp.concatenate([along_y[rows, :384], along_y[rows, 384:]], axis=0).astype(BF16)
-        results.append(pltpu.make_async_copy(out.at[:, quad], far_out.at[:, which, quad], left.at[quad]))
-        results[-1].start()
+        lax.fori_loop(0, QUADS, planes, 0, unroll=3)
+        results += [result(quad) for quad in range(QUADS)]
     for copy in results:
         copy.wait()
 
@@ -135,28 +142,22 @@
     return pl.CostEstimate(flops=pairs * 1400 * 10**6, bytes_accessed=pairs * 7 * 10**6, transcendentals=0)
 
 
-def forward(column, orbitals, source, which, pieces):
+def forward(column, orbitals, sources):
+    cuts = [cut for source in sources for cut in source]
+    pairs = len(sources)
     return pl.pallas_call(
-        functools.partial(forward_body, which),
-        in_specs=[SCALAR] + [FAR] * 5 + [VECTOR] * 2 + [FAR] * (pieces is not None),
+        forward_body,
+        in_specs=[SCALAR] + [FAR] * (1 + len(cuts)) + [VECTOR] * 2,
         out_specs=FAR,
-        out_shape=jax.ShapeDtypeStruct((PARTS, 2, *PIECE), BF16),
-        input_output_aliases={} if pieces is None else {8: 0},
+        out_shape=jax.ShapeDtypeStruct((PARTS, pairs, *PIECE), BF16),
         scratch_shapes=[pltpu.VMEM((ROWS * PITCH, 128), F32)] * 3
-        + [pltpu.SemaphoreType.DMA((8,)), pltpu.SemaphoreType.DMA((QUADS,))]
-        + [pltpu.VMEM((ROWS, CUT), BF16)] * 8
-        + [pltpu.VMEM((PARTS, *PIECE), BF16)],
+        + [pltpu.SemaphoreType.DMA((4 + len(cuts),)), pltpu.SemaphoreType.DMA((pairs, QUADS))]
+        + [pltpu.VMEM((ROWS, CUT), BF16)] * (4 + len(cuts))
+        + [pltpu.VMEM((PARTS, *PIECE), BF16)] * pairs,
         compiler_params=pltpu.CompilerParams(vmem_limit_bytes=62 * 2**20),
-        cost_estimate=cost(1),
+        cost_estimate=cost(pairs),
         name="forward_zy",
-    )(
-        column,
-        orbitals,
-        *source,
-        jnp.asarray(Z_TABLES, BF16),
-        jnp.asarray(Y_TABLE, BF16),
-        *([] if pieces is None else [pieces]),
-    )
+    )(column, orbitals, *cuts, jnp.asarray(Z_TABLES, BF16), jnp.asarray(Y_TABLE, BF16))
 
 
 def middle_body(far_pieces, far_kernel, x_table, x_back, far_out, head0, head1, tail, arrived, left, kernel, *pieces):
@@ -264,7 +265,7 @@
                     lots[which][2][rows, :] = odd[:, 128:]
             return carry
 
-        lax.fori_loop(0, QUADS, planes, 0, unroll=6)
+        lax.fori_loop(0, QUADS, planes, 0, unroll=3)
 
     for copy in copies[pairs:]:
         copy.wait()
@@ -341,6 +342,14 @@
     return jnp.where(is_root, mine, away)
 
 
+def along_z(mine, is_root, *others):
+    away = sum(
+        move(mine, [(band_of(2 * c, x, c), band_of(2 * c + up, x, c)) for c in range(2) for x in range(4)])
+        for up in (1, 3, 2)
+    )
+    return jnp.where(is_root, mine, away)
+
+
 def beyond(mine):
     half = mine.shape[1] // 2
     parts = [
@@ -371,16 +380,16 @@
 
     cut_0 = scatter(orbitals, 0)
     cut_1 = scatter(after(orbitals, cut_0), 1)
-    full_0 = beyond(beside(cut_0, is_root))
+    near_0 = beside(cut_0, is_root)
+    full_0 = beyond(near_0)
     mine_0 = gather_x(full_0)
-    full_1 = beyond(beside(after(cut_1, full_0), is_root))
     batch_0 = [mine_0, other_core(mine_0)]
-    pieces_0 = forward(column, orbitals, mine_0, 0, None)
-    pieces_0 = after(forward(column, orbitals, batch_0[1], 1, pieces_0), full_1)
-    mine_1 = gather_x(after(full_1, *mine_0))
+    pieces_0 = forward(column, orbitals, batch_0)
+    full_1 = along_z(after(cut_1, full_0), is_root, pieces_0)
+    pieces_0 = after(pieces_0, full_1)
+    mine_1 = gather_x(full_1)
     batch_1 = [mine_1, other_core(mine_1)]
-    pieces_1 = forward(column, orbitals, mine_1, 0, None)
-    pieces_1 = forward(column, orbitals, batch_1[1], 1, pieces_1)
+    pieces_1 = forward(column, orbitals, batch_1)
     back_0 = exchange(middle(exchange(pieces_0), kernel))
     back_1 = exchange(middle(exchange(pieces_1), kernel))
     total = backward(column, back_0, batch_0, None)

time: 297 us -> 284 us (0.956)
  starting transfers between devices: 80.4 us -> 60.2 us
  waiting for transfers between devices: 132 us -> 146 us
  Pallas kernels: 67.8 us -> 62.9 us
    ppermute x30 -> x29, waiting for transfers between devices: 43.2 us -> 57.3 us  [move(): return lax.ppermute(array, 'band', pairs)]
    ppermute x30 -> x29, starting transfers between devices: 48 us -> 36.6 us  [move(): return lax.ppermute(array, 'band', pairs)]
    all_to_all x4, starting transfers between devices: 32.3 us -> 23.6 us  [exchange(): return lax.all_to_all(pieces, 'grid', 0, 0, tiled=True)]
    pallas_call x4 -> x2, Pallas kernels: 24.5 us -> 19 us  [forward(): pl.pallas_call(forward_body, in_specs=[SCALAR] + [FAR] * (1 + len(cuts))...]
  transfers between devices with their start and end apart: 34 -> 33, of which waited for: 15 -> 17; matrix products, arithmetic and copies ran while one was open for 2% -> 2% of each run, Pallas kernels for 18% -> 16%
where the time goes in v7:
time: 284 us; the launch traced here: 281 us
  waiting for transfers between devices  146 us (51%)
  Pallas kernels  62.9 us (22%)
  starting transfers between devices  60.2 us (21%)
  other arithmetic  6.3 us (2%)
  local copies, waits for them, and re-layouts  5.49 us (2%)
    all_to_all x4, waiting for transfers between devices, exchange(): return lax.all_to_all(pieces, 'grid', 0, 0, tiled=True)  88.6 us
    ppermute x29, waiting for transfers between devices, move(): return lax.ppermute(array, 'band', pairs)  57.3 us
    ppermute x29, starting transfers between devices, move(): return lax.ppermute(array, 'band', pairs)  36.6 us
    pallas_call x2, Pallas kernels, middle(): pl.pallas_call(middle_body, in_specs=[FAR, FAR, VECTOR, VECTOR], out_spec...  24.5 us
    all_to_all x4, starting transfers between devices, exchange(): return lax.all_to_all(pieces, 'grid', 0, 0, tiled=True)  23.6 us
    pallas_call x2, Pallas kernels, backward(): pl.pallas_call(backward_body, in_specs=[SCALAR] + [FAR] * (1 + len(cuts)...  19.4 us
    pallas_call x2, Pallas kernels, forward(): pl.pallas_call(forward_body, in_specs=[SCALAR] + [FAR] * (1 + len(cuts))...  19 us
  transfers between devices with their start and end apart: 33, of which 17 were waited for; matrix products, arithmetic and copies ran while one was open for 2% of the time, Pallas kernels for 16%

profile of v7, /device:TPU:32, one launch (start us, length us, event | category | flops | bytes accessed | tf_op | source)
XLA Modules:
  0.0 281.3 jit_solution(18302432295798299657)
XLA Ops:
  2.4 3.4 %collective-permute-start.1 = (bf16[24,9216]{1,0:T(8,128)(2,1)S(1)}, bf16[24,9216]{1,0:T(8,128)(2,1)S(1)}, u32[]{:S(2)}, u32[]{:S(2)}) collective-permute-start(bf16[24,9216]{1,0:T(8,128)(2,1)S(1)} %get-tuple-element.15), channel_id=1, source_target_pairs={{0,16},{128,152},{1,17},{129,153},{2,18},{130,154},{3,19},{131,155... | collective-permute-start | bytes 1327112 | tf_op jit(solution)/shard_map/ppermute | solution.py:321
  11.6 4.7 %collective-permute-done.2 = bf16[24,9216]{1,0:T(8,128)(2,1)S(1)} collective-permute-done((bf16[24,9216]{1,0:T(8,128)(2,1)S(1)}, bf16[24,9216]{1,0:T(8,128)(2,1)S(1)}, u32[]{:S(2)}, u32[]{:S(2)}) %collective-permute-start.2) | collective-permute-done | bytes 442400 | tf_op jit(solution)/shard_map/ppermute | solution.py:321
  21.3 7.6 %collective-permute-done.8 = bf16[24,9216]{1,0:T(8,128)(2,1)} collective-permute-done((bf16[24,9216]{1,0:T(8,128)(2,1)}, bf16[24,9216]{1,0:T(8,128)(2,1)}, u32[]{:S(2)}, u32[]{:S(2)}) %collective-permute-start.8) | collective-permute-done | bytes 442400 | tf_op jit(solution)/shard_map/ppermute | solution.py:321
  33.8 5.3 %collective-permute-start.6 = (bf16[24,9216]{1,0:T(8,128)(2,1)S(1)}, bf16[24,9216]{1,0:T(8,128)(2,1)S(1)}, u32[]{:S(2)}, u32[]{:S(2)}) collective-permute-start(bf16[24,9216]{1,0:T(8,128)(2,1)S(1)} %get-tuple-element.13), channel_id=1, source_target_pairs={{0,32},{128,168},{1,33},{129,169},{2,34},{130,170},{3,35},{131,171... | collective-permute-start | bytes 1327112 | tf_op jit(solution)/shard_map/ppermute | solution.py:321
  40.7 8.9 %collective-permute-done.6 = bf16[24,9216]{1,0:T(8,128)(2,1)S(1)} collective-permute-done((bf16[24,9216]{1,0:T(8,128)(2,1)S(1)}, bf16[24,9216]{1,0:T(8,128)(2,1)S(1)}, u32[]{:S(2)}, u32[]{:S(2)}) %collective-permute-start.6) | collective-permute-done | bytes 442400 | tf_op jit(solution)/shard_map/ppermute | solution.py:321
  49.7 4.1 %collective-permute-start.23 = (bf16[24,9216]{1,0:T(8,128)(2,1)S(1)}, bf16[24,9216]{1,0:T(8,128)(2,1)S(1)}, u32[]{:S(2)}, u32[]{:S(2)}) collective-permute-start(bf16[24,9216]{1,0:T(8,128)(2,1)S(1)} %maximum_add_fusion.refs_0_), channel_id=1, source_target_pairs={{0,32},{8,40},{16,48},{24,56},{32,0},{40,8},{48,16},{56,24},{64,96... | collective-permute-start | bytes 1327112 | tf_op jit(solution)/shard_map/ppermute | solution.py:321
  63.4 4.9 %collective-permute-done.24.refs_3_ = bf16[24,9216]{1,0:T(8,128)(2,1)S(1)} collective-permute-done((bf16[24,9216]{1,0:T(8,128)(2,1)S(1)}, bf16[24,9216]{1,0:T(8,128)(2,1)S(1)}, u32[]{:S(2)}, u32[]{:S(2)}) %collective-permute-start.24) | collective-permute-done | bytes 442400 | tf_op jit(solution)/shard_map/ppermute | solution.py:321
  74.5 9.5 %forward_zy.3 = bf16[8,2,6,48,384]{4,3,2,1,0:T(8,128)(2,1)} custom-call(s32[1]{0:T(128)} %bitcast.column, bf16[2,24,36864]{2,1,0:T(8,128)(2,1)} %far_orbitals.3, bf16[24,9216]{1,0:T(8,128)(2,1)} %copy-done.2, bf16[24,9216]{1,0:T(8,128)(2,1)} %copy-done.3, bf16[24,9216]{1,0:T(8,128)(2,1)} %copy-done.4, bf16[24,9216]{1,0:T(8,128)(2,1)} %copy-done.5, ...), custom_call_target="tpu_custom_call" | custom-call | flops 2800000000 | bytes 14000000 | tf_op jit(solution)/shard_map/forward_zy/pallas_call | solution.py:148
  84.0 6.5 %all-to-all-start.2 = ((bf16[8,2,6,48,384]{4,3,2,1,0:T(8,128)(2,1)}), bf16[8,2,6,48,384]{4,3,2,1,0:T(8,128)(2,1)}, u32[]{:S(2)}, u32[]{:S(2)}) async-start(bf16[8,2,6,48,384]{4,3,2,1,0:T(8,128)(2,1)} %forward_zy.3), calls=%async_computation.2 | async-start | bytes 7077888 | tf_op jit(solution)/shard_map/all_to_all | solution.py:313
  90.6 4.6 %collective-permute-start.16 = (bf16[24,9216]{1,0:T(8,128)(2,1)S(1)}, bf16[24,9216]{1,0:T(8,128)(2,1)S(1)}, u32[]{:S(2)}, u32[]{:S(2)}) collective-permute-start(bf16[24,9216]{1,0:T(8,128)(2,1)S(1)} %add_select_fusion.refs_0_), channel_id=1, source_target_pairs={{0,32},{8,40},{16,48},{24,56},{32,0},{40,8},{48,16},{56,24},{64,96... | collective-permute-start | bytes 1327112 | tf_op jit(solution)/shard_map/ppermute | solution.py:321
  95.2 8.3 %collective-permute-done.15.refs_1_ = bf16[24,9216]{1,0:T(8,128)(2,1)S(1)} collective-permute-done((bf16[24,9216]{1,0:T(8,128)(2,1)S(1)}, bf16[24,9216]{1,0:T(8,128)(2,1)S(1)}, u32[]{:S(2)}, u32[]{:S(2)}) %collective-permute-start.15) | collective-permute-done | bytes 442400 | tf_op jit(solution)/shard_map/ppermute | solution.py:321
  103.5 11.5 %collective-permute-done.16.refs_2_ = bf16[24,9216]{1,0:T(8,128)(2,1)S(1)} collective-permute-done((bf16[24,9216]{1,0:T(8,128)(2,1)S(1)}, bf16[24,9216]{1,0:T(8,128)(2,1)S(1)}, u32[]{:S(2)}, u32[]{:S(2)}) %collective-permute-start.16) | collective-permute-done | bytes 442400 | tf_op jit(solution)/shard_map/ppermute | solution.py:321
  119.5 9.5 %forward_zy.2 = bf16[8,2,6,48,384]{4,3,2,1,0:T(8,128)(2,1)} custom-call(s32[1]{0:T(128)} %bitcast.column, bf16[2,24,36864]{2,1,0:T(8,128)(2,1)} %far_orbitals.3, bf16[24,9216]{1,0:T(8,128)(2,1)} %copy-done.1, bf16[24,9216]{1,0:T(8,128)(2,1)} %copy-done.10, bf16[24,9216]{1,0:T(8,128)(2,1)} %copy-done.11, bf16[24,9216]{1,0:T(8,128)(2,1)} %copy-done.12, ...), custom_call_target="tpu_custom_call" | custom-call | flops 2800000000 | bytes 14000000 | tf_op jit(solution)/shard_map/forward_zy/pallas_call | solution.py:148
  129.0 3.7 %all-to-all-done.2.far_pieces = bf16[8,2,6,48,384]{4,3,2,1,0:T(8,128)(2,1)} async-done(((bf16[8,2,6,48,384]{4,3,2,1,0:T(8,128)(2,1)}), bf16[8,2,6,48,384]{4,3,2,1,0:T(8,128)(2,1)}, u32[]{:S(2)}, u32[]{:S(2)}) %all-to-all-start.2) | async-done | bytes 3538976 | tf_op jit(solution)/shard_map/all_to_all | solution.py:313
  132.7 5.6 %all-to-all-start = ((bf16[8,2,6,48,384]{4,3,2,1,0:T(8,128)(2,1)}), bf16[8,2,6,48,384]{4,3,2,1,0:T(8,128)(2,1)}, u32[]{:S(2)}, u32[]{:S(2)}) async-start(bf16[8,2,6,48,384]{4,3,2,1,0:T(8,128)(2,1)} %forward_zy.2), calls=%async_computation | async-start | bytes 7077888 | tf_op jit(solution)/shard_map/all_to_all | solution.py:313
  140.9 12.3 %middle_x.3 = bf16[8,2,6,48,384]{4,3,2,1,0:T(8,128)(2,1)} custom-call(bf16[8,2,6,48,384]{4,3,2,1,0:T(8,128)(2,1)} %all-to-all-done.2.far_pieces, f32[12,192,384]{2,1,0:T(8,128)} %select_multiply_fusion.far_kernel, bf16[192,192]{1,0:T(8,128)(2,1)} %constant.117.clone.refs_9_.x_table, bf16[192,192]{1,0:T(8,128)(2,1)} %constant.118.clone.x_back.refs_8_.refs_9_), custom_call_target="tpu_custom_call" | custom-call | flops 2800000000 | bytes 14000000 | tf_op jit(solution)/shard_map/middle_x/pallas_call | solution.py:222
  153.1 26.6 %all-to-all-done.far_pieces = bf16[8,2,6,48,384]{4,3,2,1,0:T(8,128)(2,1)} async-done(((bf16[8,2,6,48,384]{4,3,2,1,0:T(8,128)(2,1)}), bf16[8,2,6,48,384]{4,3,2,1,0:T(8,128)(2,1)}, u32[]{:S(2)}, u32[]{:S(2)}) %all-to-all-start) | async-done | bytes 3538976 | tf_op jit(solution)/shard_map/all_to_all | solution.py:313
  179.7 5.6 %all-to-all-start.3 = ((bf16[8,2,6,48,384]{4,3,2,1,0:T(8,128)(2,1)}), bf16[8,2,6,48,384]{4,3,2,1,0:T(8,128)(2,1)}, u32[]{:S(2)}, u32[]{:S(2)}) async-start(bf16[8,2,6,48,384]{4,3,2,1,0:T(8,128)(2,1)} %middle_x.3), calls=%async_computation.3 | async-start | bytes 7077888 | tf_op jit(solution)/shard_map/all_to_all | solution.py:313
  185.4 12.2 %middle_x.2 = bf16[8,2,6,48,384]{4,3,2,1,0:T(8,128)(2,1)} custom-call(bf16[8,2,6,48,384]{4,3,2,1,0:T(8,128)(2,1)} %all-to-all-done.far_pieces, f32[12,192,384]{2,1,0:T(8,128)} %select_multiply_fusion.far_kernel, bf16[192,192]{1,0:T(8,128)(2,1)} %constant.117.clone.refs_9_.x_table, bf16[192,192]{1,0:T(8,128)(2,1)} %constant.118.clone.x_back.refs_8_.refs_9_), custom_call_target="tpu_custom_call" | custom-call | flops 2800000000 | bytes 14000000 | tf_op jit(solution)/shard_map/middle_x/pallas_call | solution.py:222
  197.6 28.3 %all-to-all-done.3.far_pieces = bf16[8,2,6,48,384]{4,3,2,1,0:T(8,128)(2,1)} async-done(((bf16[8,2,6,48,384]{4,3,2,1,0:T(8,128)(2,1)}), bf16[8,2,6,48,384]{4,3,2,1,0:T(8,128)(2,1)}, u32[]{:S(2)}, u32[]{:S(2)}) %all-to-all-start.3) | async-done | bytes 3538976 | tf_op jit(solution)/shard_map/all_to_all | solution.py:313
  225.9 5.8 %all-to-all-start.1 = ((bf16[8,2,6,48,384]{4,3,2,1,0:T(8,128)(2,1)}), bf16[8,2,6,48,384]{4,3,2,1,0:T(8,128)(2,1)}, u32[]{:S(2)}, u32[]{:S(2)}) async-start(bf16[8,2,6,48,384]{4,3,2,1,0:T(8,128)(2,1)} %middle_x.2), calls=%async_computation.1 | async-start | bytes 7077888 | tf_op jit(solution)/shard_map/all_to_all | solution.py:313
  231.7 9.7 %backward_yz.2.refs_8_ = f32[24,36864]{1,0:T(8,128)} custom-call(s32[1]{0:T(128)} %bitcast.column, bf16[8,2,6,48,384]{4,3,2,1,0:T(8,128)(2,1)} %all-to-all-done.3.far_pieces, bf16[24,9216]{1,0:T(8,128)(2,1)} %copy-done.2, bf16[24,9216]{1,0:T(8,128)(2,1)} %copy-done.3, bf16[24,9216]{1,0:T(8,128)(2,1)} %copy-done.4, bf16[24,9216]{1,0:T(8,128)(2,1)} %copy-done.5, ...), custom_call_target="tpu_custom_call" | custom-call | flops 2800000000 | bytes 14000000 | tf_op jit(solution)/shard_map/backward_yz/pallas_call | solution.py:296
  241.4 29.9 %all-to-all-done.1.far_pieces = bf16[8,2,6,48,384]{4,3,2,1,0:T(8,128)(2,1)} async-done(((bf16[8,2,6,48,384]{4,3,2,1,0:T(8,128)(2,1)}), bf16[8,2,6,48,384]{4,3,2,1,0:T(8,128)(2,1)}, u32[]{:S(2)}, u32[]{:S(2)}) %all-to-all-start.1) | async-done | bytes 3538976 | tf_op jit(solution)/shard_map/all_to_all | solution.py:313
  271.4 9.7 %backward_yz.3 = f32[24,36864]{1,0:T(8,128)} custom-call(s32[1]{0:T(128)} %bitcast.column, bf16[8,2,6,48,384]{4,3,2,1,0:T(8,128)(2,1)} %all-to-all-done.1.far_pieces, bf16[24,9216]{1,0:T(8,128)(2,1)} %copy-done.1, bf16[24,9216]{1,0:T(8,128)(2,1)} %copy-done.10, bf16[24,9216]{1,0:T(8,128)(2,1)} %copy-done.11, bf16[24,9216]{1,0:T(8,128)(2,1)} %copy-done.12, ...), custom_call_target="tpu_custom_call" | custom-call | flops 2800000000 | bytes 14000000 | tf_op jit(solution)/shard_map/backward_yz/pallas_call | solution.py:296
  (99 shorter events, 42.3 us)
Async XLA Ops:
  2.4 9.2 %collective-permute-start.1 = (bf16[24,9216]{1,0:T(8,128)(2,1)S(1)}, bf16[24,9216]{1,0:T(8,128)(2,1)S(1)}, u32[]{:S(2)}, u32[]{:S(2)}) collective-permute-start(bf16[24,9216]{1,0:T(8,128)(2,1)S(1)} %get-tuple-element.15), channel_id=1, source_target_pairs={{0,16},{128,152},{1,17},{129,153},{2,18},{130,154},{3,19},{131,155... | collective-permute-start | bytes 1327112 | tf_op jit(solution)/shard_map/ppermute | solution.py:321
  5.8 10.5 %collective-permute-start.2 = (bf16[24,9216]{1,0:T(8,128)(2,1)S(1)}, bf16[24,9216]{1,0:T(8,128)(2,1)S(1)}, u32[]{:S(2)}, u32[]{:S(2)}) collective-permute-start(bf16[24,9216]{1,0:T(8,128)(2,1)S(1)} %get-tuple-element.17), channel_id=1, source_target_pairs={{0,32},{128,168},{1,33},{129,169},{2,34},{130,170},{3,35},{131,171... | collective-permute-start | bytes 1327112 | tf_op jit(solution)/shard_map/ppermute | solution.py:321
  17.2 11.7 %collective-permute-start.8 = (bf16[24,9216]{1,0:T(8,128)(2,1)}, bf16[24,9216]{1,0:T(8,128)(2,1)}, u32[]{:S(2)}, u32[]{:S(2)}) collective-permute-start(bf16[24,9216]{1,0:T(8,128)(2,1)} %add_add_fusion.1), channel_id=1, source_target_pairs={{0,64},{16,80},{32,96},{48,112},{136,200},{152,216},{168,232},{184... | collective-permute-start | bytes 1327112 | tf_op jit(solution)/shard_map/ppermute | solution.py:321
  19.2 9.6 %collective-permute-start.9 = (bf16[24,9216]{1,0:T(8,128)(2,1)}, bf16[24,9216]{1,0:T(8,128)(2,1)}, u32[]{:S(2)}, u32[]{:S(2)}) collective-permute-start(bf16[24,9216]{1,0:T(8,128)(2,1)} %add_add_fusion.1), channel_id=1, source_target_pairs={{0,192},{16,208},{32,224},{48,240},{136,72},{152,88},{168,104},{18... | collective-permute-start | bytes 1327112 | tf_op jit(solution)/shard_map/ppermute | solution.py:321
  30.9 9.5 %collective-permute-start.11 = (bf16[24,4608]{1,0:T(8,128)(2,1)S(1)}, bf16[24,4608]{1,0:T(8,128)(2,1)S(1)}, u32[]{:S(2)}, u32[]{:S(2)}) collective-permute-start(bf16[24,4608]{1,0:T(8,128)(2,1)S(1)} %get-tuple-element.20), channel_id=1, source_target_pairs={{192,128},{208,144},{224,160},{240,176},{72,8},{88,24},{104,40},{1... | collective-permute-start | bytes 663560 | tf_op jit(solution)/shard_map/ppermute | solution.py:321
  31.8 8.9 %collective-permute-start.4 = (bf16[24,9216]{1,0:T(8,128)(2,1)S(1)}, bf16[24,9216]{1,0:T(8,128)(2,1)S(1)}, u32[]{:S(2)}, u32[]{:S(2)}) collective-permute-start(bf16[24,9216]{1,0:T(8,128)(2,1)S(1)} %get-tuple-element.14), channel_id=1, source_target_pairs={{0,0},{128,136},{1,1},{129,137},{2,2},{130,138},{3,3},{131,139},{4... | collective-permute-start | bytes 1327112 | tf_op jit(solution)/shard_map/ppermute | solution.py:321
  33.8 15.8 %collective-permute-start.6 = (bf16[24,9216]{1,0:T(8,128)(2,1)S(1)}, bf16[24,9216]{1,0:T(8,128)(2,1)S(1)}, u32[]{:S(2)}, u32[]{:S(2)}) collective-permute-start(bf16[24,9216]{1,0:T(8,128)(2,1)S(1)} %get-tuple-element.13), channel_id=1, source_target_pairs={{0,32},{128,168},{1,33},{129,169},{2,34},{130,170},{3,35},{131,171... | collective-permute-start | bytes 1327112 | tf_op jit(solution)/shard_map/ppermute | solution.py:321
  39.1 10.5 %collective-permute-start.7 = (bf16[24,9216]{1,0:T(8,128)(2,1)S(1)}, bf16[24,9216]{1,0:T(8,128)(2,1)S(1)}, u32[]{:S(2)}, u32[]{:S(2)}) collective-permute-start(bf16[24,9216]{1,0:T(8,128)(2,1)S(1)} %get-tuple-element.12), channel_id=1, source_target_pairs={{0,48},{128,184},{1,49},{129,185},{2,50},{130,186},{3,51},{131,187... | collective-permute-start | bytes 1327112 | tf_op jit(solution)/shard_map/ppermute | solution.py:321
  40.6 18.0 %collective-permute-start.22 = (bf16[24,9216]{1,0:T(8,128)(2,1)S(1)}, bf16[24,9216]{1,0:T(8,128)(2,1)S(1)}, u32[]{:S(2)}, u32[]{:S(2)}) collective-permute-start(bf16[24,9216]{1,0:T(8,128)(2,1)S(1)} %maximum_add_fusion.refs_0_), channel_id=1, source_target_pairs={{0,16},{8,24},{16,0},{24,8},{32,48},{40,56},{48,32},{56,40},{64,80... | collective-permute-start | bytes 1327112 | tf_op jit(solution)/shard_map/ppermute | solution.py:321
  49.7 13.7 %collective-permute-start.23 = (bf16[24,9216]{1,0:T(8,128)(2,1)S(1)}, bf16[24,9216]{1,0:T(8,128)(2,1)S(1)}, u32[]{:S(2)}, u32[]{:S(2)}) collective-permute-start(bf16[24,9216]{1,0:T(8,128)(2,1)S(1)} %maximum_add_fusion.refs_0_), channel_id=1, source_target_pairs={{0,32},{8,40},{16,48},{24,56},{32,0},{40,8},{48,16},{56,24},{64,96... | collective-permute-start | bytes 1327112 | tf_op jit(solution)/shard_map/ppermute | solution.py:321
  53.8 14.4 %collective-permute-start.24 = (bf16[24,9216]{1,0:T(8,128)(2,1)S(1)}, bf16[24,9216]{1,0:T(8,128)(2,1)S(1)}, u32[]{:S(2)}, u32[]{:S(2)}) collective-permute-start(bf16[24,9216]{1,0:T(8,128)(2,1)S(1)} %maximum_add_fusion.refs_0_), channel_id=1, source_target_pairs={{0,48},{8,56},{16,32},{24,40},{32,16},{40,24},{48,0},{56,8},{64,11... | collective-permute-start | bytes 1327112 | tf_op jit(solution)/shard_map/ppermute | solution.py:321
  53.8 16.6 %collective-permute-start.12 = (bf16[24,9216]{1,0:T(8,128)(2,1)S(1)}, bf16[24,9216]{1,0:T(8,128)(2,1)S(1)}, u32[]{:S(2)}, u32[]{:S(2)}) collective-permute-start(bf16[24,9216]{1,0:T(8,128)(2,1)S(1)} %add_add_fusion), channel_id=1, source_target_pairs={{0,64},{16,80},{32,96},{48,112},{136,200},{152,216},{168,232},{184... | collective-permute-start | bytes 1327112 | tf_op jit(solution)/shard_map/ppermute | solution.py:321
  55.1 15.3 %collective-permute-start.13 = (bf16[24,9216]{1,0:T(8,128)(2,1)S(1)}, bf16[24,9216]{1,0:T(8,128)(2,1)}, u32[]{:S(2)}, u32[]{:S(2)}) collective-permute-start(bf16[24,9216]{1,0:T(8,128)(2,1)S(1)} %add_add_fusion), channel_id=1, source_target_pairs={{0,192},{16,208},{32,224},{48,240},{136,72},{152,88},{168,104},{18... | collective-permute-start | bytes 1327112 | tf_op jit(solution)/shard_map/ppermute | solution.py:321
  58.6 12.6 %collective-permute-start.14 = (bf16[24,9216]{1,0:T(8,128)(2,1)S(1)}, bf16[24,9216]{1,0:T(8,128)(2,1)}, u32[]{:S(2)}, u32[]{:S(2)}) collective-permute-start(bf16[24,9216]{1,0:T(8,128)(2,1)S(1)} %add_add_fusion), channel_id=1, source_target_pairs={{0,128},{16,144},{32,160},{48,176},{136,8},{152,24},{168,40},{184,... | collective-permute-start | bytes 1327112 | tf_op jit(solution)/shard_map/ppermute | solution.py:321
  63.4 9.2 %collective-permute-start.25 = (bf16[24,9216]{1,0:T(8,128)(2,1)S(1)}, bf16[24,9216]{1,0:T(8,128)(2,1)S(1)}, u32[]{:S(2)}, u32[]{:S(2)}) collective-permute-start(bf16[24,9216]{1,0:T(8,128)(2,1)S(1)} %maximum_add_fusion.refs_0_), channel_id=1, source_target_pairs={{0,8},{8,0},{16,24},{24,16},{32,40},{40,32},{48,56},{56,48},{64,72... | collective-permute-start | bytes 1327112 | tf_op jit(solution)/shard_map/ppermute | solution.py:321
  84.0 48.7 %all-to-all-start.2 = ((bf16[8,2,6,48,384]{4,3,2,1,0:T(8,128)(2,1)}), bf16[8,2,6,48,384]{4,3,2,1,0:T(8,128)(2,1)}, u32[]{:S(2)}, u32[]{:S(2)}) async-start(bf16[8,2,6,48,384]{4,3,2,1,0:T(8,128)(2,1)} %forward_zy.3), calls=%async_computation.2 | async-start | bytes 7077888 | tf_op jit(solution)/shard_map/all_to_all | solution.py:313
  90.5 13.0 %collective-permute-start.15 = (bf16[24,9216]{1,0:T(8,128)(2,1)S(1)}, bf16[24,9216]{1,0:T(8,128)(2,1)S(1)}, u32[]{:S(2)}, u32[]{:S(2)}) collective-permute-start(bf16[24,9216]{1,0:T(8,128)(2,1)S(1)} %add_select_fusion.refs_0_), channel_id=1, source_target_pairs={{0,16},{8,24},{16,0},{24,8},{32,48},{40,56},{48,32},{56,40},{64,80... | collective-permute-start | bytes 1327112 | tf_op jit(solution)/shard_map/ppermute | solution.py:321
  90.6 24.4 %collective-permute-start.16 = (bf16[24,9216]{1,0:T(8,128)(2,1)S(1)}, bf16[24,9216]{1,0:T(8,128)(2,1)S(1)}, u32[]{:S(2)}, u32[]{:S(2)}) collective-permute-start(bf16[24,9216]{1,0:T(8,128)(2,1)S(1)} %add_select_fusion.refs_0_), channel_id=1, source_target_pairs={{0,32},{8,40},{16,48},{24,56},{32,0},{40,8},{48,16},{56,24},{64,96... | collective-permute-start | bytes 1327112 | tf_op jit(solution)/shard_map/ppermute | solution.py:321
  95.2 22.4 %collective-permute-start.17 = (bf16[24,9216]{1,0:T(8,128)(2,1)S(1)}, bf16[24,9216]{1,0:T(8,128)(2,1)S(1)}, u32[]{:S(2)}, u32[]{:S(2)}) collective-permute-start(bf16[24,9216]{1,0:T(8,128)(2,1)S(1)} %add_select_fusion.refs_0_), channel_id=1, source_target_pairs={{0,48},{8,56},{16,32},{24,40},{32,16},{40,24},{48,0},{56,8},{64,11... | collective-permute-start | bytes 1327112 | tf_op jit(solution)/shard_map/ppermute | solution.py:321
  95.2 22.4 %collective-permute-start.18 = (bf16[24,9216]{1,0:T(8,128)(2,1)S(1)}, bf16[24,9216]{1,0:T(8,128)(2,1)S(1)}, u32[]{:S(2)}, u32[]{:S(2)}) collective-permute-start(bf16[24,9216]{1,0:T(8,128)(2,1)S(1)} %add_select_fusion.refs_0_), channel_id=1, source_target_pairs={{0,8},{8,0},{16,24},{24,16},{32,40},{40,32},{48,56},{56,48},{64,72... | collective-permute-start | bytes 1327112 | tf_op jit(solution)/shard_map/ppermute | solution.py:321
  103.5 14.1 %collective-permute-start.19 = (bf16[24,9216]{1,0:T(8,128)(2,1)S(1)}, bf16[24,9216]{1,0:T(8,128)(2,1)S(1)}, u32[]{:S(2)}, u32[]{:S(2)}) collective-permute-start(bf16[24,9216]{1,0:T(8,128)(2,1)S(1)} %collective-permute-done.15.refs_1_), channel_id=1, source_target_pairs={{0,8},{8,0},{16,24},{24,16},{32,40},{40,32},{48,56},{56,48},{64,72... | collective-permute-start | bytes 1327112 | tf_op jit(solution)/shard_map/ppermute | solution.py:321
  132.7 47.0 %all-to-all-start = ((bf16[8,2,6,48,384]{4,3,2,1,0:T(8,128)(2,1)}), bf16[8,2,6,48,384]{4,3,2,1,0:T(8,128)(2,1)}, u32[]{:S(2)}, u32[]{:S(2)}) async-start(bf16[8,2,6,48,384]{4,3,2,1,0:T(8,128)(2,1)} %forward_zy.2), calls=%async_computation | async-start | bytes 7077888 | tf_op jit(solution)/shard_map/all_to_all | solution.py:313
  179.7 46.2 %all-to-all-start.3 = ((bf16[8,2,6,48,384]{4,3,2,1,0:T(8,128)(2,1)}), bf16[8,2,6,48,384]{4,3,2,1,0:T(8,128)(2,1)}, u32[]{:S(2)}, u32[]{:S(2)}) async-start(bf16[8,2,6,48,384]{4,3,2,1,0:T(8,128)(2,1)} %middle_x.3), calls=%async_computation.3 | async-start | bytes 7077888 | tf_op jit(solution)/shard_map/all_to_all | solution.py:313
  225.9 45.4 %all-to-all-start.1 = ((bf16[8,2,6,48,384]{4,3,2,1,0:T(8,128)(2,1)}), bf16[8,2,6,48,384]{4,3,2,1,0:T(8,128)(2,1)}, u32[]{:S(2)}, u32[]{:S(2)}) async-start(bf16[8,2,6,48,384]{4,3,2,1,0:T(8,128)(2,1)} %middle_x.2), calls=%async_computation.1 | async-start | bytes 7077888 | tf_op jit(solution)/shard_map/all_to_all | solution.py:313
  (26 other events, 195.6 us)

commit v8 on v7

--- a/solution.py
+++ b/solution.py
@@ -325,14 +325,12 @@
     return lax.optimization_barrier((array, *others))[0]
 
 
-def scatter(orbitals, which):
-    return sum(
-        move(
-            orbitals[which, :, step * CUT : (step + 1) * CUT],
-            [(band_of(2 * root, 0, 0), band_of(2 * root, step, root)) for root in range(2)],
-        )
-        for step in range(4)
-    )
+def to_x(cut, step):
+    return move(cut, [(band_of(2 * root, 0, 0), band_of(2 * root, step, root)) for root in range(2)])
+
+
+def scatter(orbitals, which, first):
+    return first + sum(to_x(orbitals[which, :, step * CUT : (step + 1) * CUT], step) for step in range(1, 4))
 
 
 def beside(mine, is_root):
@@ -378,8 +376,9 @@
     kernel = coulomb(lax.axis_index("grid"))
     is_root = z_hi == 2 * core
 
-    cut_0 = scatter(orbitals, 0)
-    cut_1 = scatter(after(orbitals, cut_0), 1)
+    first = to_x(orbitals[:, :, :CUT], 0)
+    cut_0 = scatter(orbitals, 0, first[0])
+    cut_1 = scatter(after(orbitals, cut_0), 1, first[1])
     near_0 = beside(cut_0, is_root)
     full_0 = beyond(near_0)
     mine_0 = gather_x(full_0)

time: 284 us -> 283 us (level)
    ppermute x29 -> x28, starting transfers between devices: 36.6 us -> 34.5 us  [move(): return lax.ppermute(array, 'band', pairs)]
    ppermute x29 -> x28, waiting for transfers between devices: 57.3 us -> 58.4 us  [move(): return lax.ppermute(array, 'band', pairs)]
  transfers between devices with their start and end apart: 33 -> 32, of which waited for: 17 -> 17; matrix products, arithmetic and copies ran while one was open for 2% -> 2% of each run, Pallas kernels for 16% -> 16%
where the time goes in v8:
time: 283 us; the launch traced here: 280 us
  waiting for transfers between devices  147 us (52%)
  Pallas kernels  62.8 us (22%)
  starting transfers between devices  58 us (20%)
  local copies, waits for them, and re-layouts  7.68 us (3%)
  other arithmetic  4.27 us (2%)
    all_to_all x4, waiting for transfers between devices, exchange(): return lax.all_to_all(pieces, 'grid', 0, 0, tiled=True)  88.6 us
    ppermute x28, waiting for transfers between devices, move(): return lax.ppermute(array, 'band', pairs)  58.4 us
    ppermute x28, starting transfers between devices, move(): return lax.ppermute(array, 'band', pairs)  34.5 us
    pallas_call x2, Pallas kernels, middle(): pl.pallas_call(middle_body, in_specs=[FAR, FAR, VECTOR, VECTOR], out_spec...  24.4 us
    all_to_all x4, starting transfers between devices, exchange(): return lax.all_to_all(pieces, 'grid', 0, 0, tiled=True)  23.5 us
    pallas_call x2, Pallas kernels, backward(): pl.pallas_call(backward_body, in_specs=[SCALAR] + [FAR] * (1 + len(cuts)...  19.4 us
    pallas_call x2, Pallas kernels, forward(): pl.pallas_call(forward_body, in_specs=[SCALAR] + [FAR] * (1 + len(cuts))...  19 us
  transfers between devices with their start and end apart: 32, of which 17 were waited for; matrix products, arithmetic and copies ran while one was open for 2% of the time, Pallas kernels for 16%

profile of v8, /device:TPU:32, one launch (start us, length us, event | category | flops | bytes accessed | tf_op | source)
XLA Modules:
  0.0 280.4 jit_solution(733791935592871160)
XLA Ops:
  3.3 3.4 %collective-permute-start.1 = (bf16[24,9216]{1,0:T(8,128)(2,1)S(1)}, bf16[24,9216]{1,0:T(8,128)(2,1)S(1)}, u32[]{:S(2)}, u32[]{:S(2)}) collective-permute-start(bf16[24,9216]{1,0:T(8,128)(2,1)S(1)} %get-tuple-element.16), channel_id=1, source_target_pairs={{0,16},{128,152},{1,17},{129,153},{2,18},{130,154},{3,19},{131,155... | collective-permute-start | bytes 1327112 | tf_op jit(solution)/shard_map/ppermute | solution.py:321
  12.5 4.7 %collective-permute-done.2 = bf16[24,9216]{1,0:T(8,128)(2,1)S(1)} collective-permute-done((bf16[24,9216]{1,0:T(8,128)(2,1)S(1)}, bf16[24,9216]{1,0:T(8,128)(2,1)S(1)}, u32[]{:S(2)}, u32[]{:S(2)}) %collective-permute-start.2) | collective-permute-done | bytes 442400 | tf_op jit(solution)/shard_map/ppermute | solution.py:321
  20.0 8.7 %collective-permute-done.7 = bf16[24,9216]{1,0:T(8,128)(2,1)S(1)} collective-permute-done((bf16[24,9216]{1,0:T(8,128)(2,1)S(1)}, bf16[24,9216]{1,0:T(8,128)(2,1)S(1)}, u32[]{:S(2)}, u32[]{:S(2)}) %collective-permute-start.7) | collective-permute-done | bytes 442400 | tf_op jit(solution)/shard_map/ppermute | solution.py:321
  32.9 5.3 %collective-permute-start.5 = (bf16[24,9216]{1,0:T(8,128)(2,1)S(1)}, bf16[24,9216]{1,0:T(8,128)(2,1)S(1)}, u32[]{:S(2)}, u32[]{:S(2)}) collective-permute-start(bf16[24,9216]{1,0:T(8,128)(2,1)S(1)} %get-tuple-element.11), channel_id=1, source_target_pairs={{0,32},{128,168},{1,33},{129,169},{2,34},{130,170},{3,35},{131,171... | collective-permute-start | bytes 1327112 | tf_op jit(solution)/shard_map/ppermute | solution.py:321
  39.8 9.0 %collective-permute-done.5 = bf16[24,9216]{1,0:T(8,128)(2,1)S(1)} collective-permute-done((bf16[24,9216]{1,0:T(8,128)(2,1)S(1)}, bf16[24,9216]{1,0:T(8,128)(2,1)S(1)}, u32[]{:S(2)}, u32[]{:S(2)}) %collective-permute-start.5) | collective-permute-done | bytes 442400 | tf_op jit(solution)/shard_map/ppermute | solution.py:321
  48.9 4.1 %collective-permute-start.22 = (bf16[24,9216]{1,0:T(8,128)(2,1)S(1)}, bf16[24,9216]{1,0:T(8,128)(2,1)S(1)}, u32[]{:S(2)}, u32[]{:S(2)}) collective-permute-start(bf16[24,9216]{1,0:T(8,128)(2,1)S(1)} %maximum_add_fusion.refs_0_), channel_id=1, source_target_pairs={{0,32},{8,40},{16,48},{24,56},{32,0},{40,8},{48,16},{56,24},{64,96... | collective-permute-start | bytes 1327112 | tf_op jit(solution)/shard_map/ppermute | solution.py:321
  62.5 4.5 %collective-permute-done.23.refs_3_ = bf16[24,9216]{1,0:T(8,128)(2,1)S(1)} collective-permute-done((bf16[24,9216]{1,0:T(8,128)(2,1)S(1)}, bf16[24,9216]{1,0:T(8,128)(2,1)S(1)}, u32[]{:S(2)}, u32[]{:S(2)}) %collective-permute-start.23) | collective-permute-done | bytes 442400 | tf_op jit(solution)/shard_map/ppermute | solution.py:321
  73.7 9.5 %forward_zy.3 = bf16[8,2,6,48,384]{4,3,2,1,0:T(8,128)(2,1)} custom-call(s32[1]{0:T(128)} %bitcast.column, bf16[2,24,36864]{2,1,0:T(8,128)(2,1)} %far_orbitals.3, bf16[24,9216]{1,0:T(8,128)(2,1)} %copy-done.1, bf16[24,9216]{1,0:T(8,128)(2,1)} %copy-done.2, bf16[24,9216]{1,0:T(8,128)(2,1)} %copy-done.3, bf16[24,9216]{1,0:T(8,128)(2,1)} %copy-done.4, ...), custom_call_target="tpu_custom_call" | custom-call | flops 2800000000 | bytes 14000000 | tf_op jit(solution)/shard_map/forward_zy/pallas_call | solution.py:148
  83.2 6.5 %all-to-all-start.2 = ((bf16[8,2,6,48,384]{4,3,2,1,0:T(8,128)(2,1)}), bf16[8,2,6,48,384]{4,3,2,1,0:T(8,128)(2,1)}, u32[]{:S(2)}, u32[]{:S(2)}) async-start(bf16[8,2,6,48,384]{4,3,2,1,0:T(8,128)(2,1)} %forward_zy.3), calls=%async_computation.2 | async-start | bytes 7077888 | tf_op jit(solution)/shard_map/all_to_all | solution.py:313
  89.8 4.6 %collective-permute-start.15 = (bf16[24,9216]{1,0:T(8,128)(2,1)S(1)}, bf16[24,9216]{1,0:T(8,128)(2,1)S(1)}, u32[]{:S(2)}, u32[]{:S(2)}) collective-permute-start(bf16[24,9216]{1,0:T(8,128)(2,1)S(1)} %add_select_fusion.refs_0_), channel_id=1, source_target_pairs={{0,32},{8,40},{16,48},{24,56},{32,0},{40,8},{48,16},{56,24},{64,96... | collective-permute-start | bytes 1327112 | tf_op jit(solution)/shard_map/ppermute | solution.py:321
  94.4 8.3 %collective-permute-done.14.refs_1_ = bf16[24,9216]{1,0:T(8,128)(2,1)S(1)} collective-permute-done((bf16[24,9216]{1,0:T(8,128)(2,1)S(1)}, bf16[24,9216]{1,0:T(8,128)(2,1)S(1)}, u32[]{:S(2)}, u32[]{:S(2)}) %collective-permute-start.14) | collective-permute-done | bytes 442400 | tf_op jit(solution)/shard_map/ppermute | solution.py:321
  102.7 11.4 %collective-permute-done.15.refs_2_ = bf16[24,9216]{1,0:T(8,128)(2,1)S(1)} collective-permute-done((bf16[24,9216]{1,0:T(8,128)(2,1)S(1)}, bf16[24,9216]{1,0:T(8,128)(2,1)S(1)}, u32[]{:S(2)}, u32[]{:S(2)}) %collective-permute-start.15) | collective-permute-done | bytes 442400 | tf_op jit(solution)/shard_map/ppermute | solution.py:321
  118.7 9.5 %forward_zy.2 = bf16[8,2,6,48,384]{4,3,2,1,0:T(8,128)(2,1)} custom-call(s32[1]{0:T(128)} %bitcast.column, bf16[2,24,36864]{2,1,0:T(8,128)(2,1)} %far_orbitals.3, bf16[24,9216]{1,0:T(8,128)(2,1)} %copy-done, bf16[24,9216]{1,0:T(8,128)(2,1)} %copy-done.9, bf16[24,9216]{1,0:T(8,128)(2,1)} %copy-done.10, bf16[24,9216]{1,0:T(8,128)(2,1)} %copy-done.11, ...), custom_call_target="tpu_custom_call" | custom-call | flops 2800000000 | bytes 14000000 | tf_op jit(solution)/shard_map/forward_zy/pallas_call | solution.py:148
  128.2 3.8 %all-to-all-done.2.far_pieces = bf16[8,2,6,48,384]{4,3,2,1,0:T(8,128)(2,1)} async-done(((bf16[8,2,6,48,384]{4,3,2,1,0:T(8,128)(2,1)}), bf16[8,2,6,48,384]{4,3,2,1,0:T(8,128)(2,1)}, u32[]{:S(2)}, u32[]{:S(2)}) %all-to-all-start.2) | async-done | bytes 3538976 | tf_op jit(solution)/shard_map/all_to_all | solution.py:313
  131.9 5.6 %all-to-all-start = ((bf16[8,2,6,48,384]{4,3,2,1,0:T(8,128)(2,1)}), bf16[8,2,6,48,384]{4,3,2,1,0:T(8,128)(2,1)}, u32[]{:S(2)}, u32[]{:S(2)}) async-start(bf16[8,2,6,48,384]{4,3,2,1,0:T(8,128)(2,1)} %forward_zy.2), calls=%async_computation | async-start | bytes 7077888 | tf_op jit(solution)/shard_map/all_to_all | solution.py:313
  140.1 12.2 %middle_x.3 = bf16[8,2,6,48,384]{4,3,2,1,0:T(8,128)(2,1)} custom-call(bf16[8,2,6,48,384]{4,3,2,1,0:T(8,128)(2,1)} %all-to-all-done.2.far_pieces, f32[12,192,384]{2,1,0:T(8,128)} %select_multiply_fusion.far_kernel, bf16[192,192]{1,0:T(8,128)(2,1)} %constant.117.clone.refs_9_.x_table, bf16[192,192]{1,0:T(8,128)(2,1)} %constant.118.clone.x_back.refs_8_.refs_9_), custom_call_target="tpu_custom_call" | custom-call | flops 2800000000 | bytes 14000000 | tf_op jit(solution)/shard_map/middle_x/pallas_call | solution.py:222
  152.3 26.6 %all-to-all-done.far_pieces = bf16[8,2,6,48,384]{4,3,2,1,0:T(8,128)(2,1)} async-done(((bf16[8,2,6,48,384]{4,3,2,1,0:T(8,128)(2,1)}), bf16[8,2,6,48,384]{4,3,2,1,0:T(8,128)(2,1)}, u32[]{:S(2)}, u32[]{:S(2)}) %all-to-all-start) | async-done | bytes 3538976 | tf_op jit(solution)/shard_map/all_to_all | solution.py:313
  178.9 5.6 %all-to-all-start.3 = ((bf16[8,2,6,48,384]{4,3,2,1,0:T(8,128)(2,1)}), bf16[8,2,6,48,384]{4,3,2,1,0:T(8,128)(2,1)}, u32[]{:S(2)}, u32[]{:S(2)}) async-start(bf16[8,2,6,48,384]{4,3,2,1,0:T(8,128)(2,1)} %middle_x.3), calls=%async_computation.3 | async-start | bytes 7077888 | tf_op jit(solution)/shard_map/all_to_all | solution.py:313
  184.5 12.2 %middle_x.2 = bf16[8,2,6,48,384]{4,3,2,1,0:T(8,128)(2,1)} custom-call(bf16[8,2,6,48,384]{4,3,2,1,0:T(8,128)(2,1)} %all-to-all-done.far_pieces, f32[12,192,384]{2,1,0:T(8,128)} %select_multiply_fusion.far_kernel, bf16[192,192]{1,0:T(8,128)(2,1)} %constant.117.clone.refs_9_.x_table, bf16[192,192]{1,0:T(8,128)(2,1)} %constant.118.clone.x_back.refs_8_.refs_9_), custom_call_target="tpu_custom_call" | custom-call | flops 2800000000 | bytes 14000000 | tf_op jit(solution)/shard_map/middle_x/pallas_call | solution.py:222
  196.8 28.3 %all-to-all-done.3.far_pieces = bf16[8,2,6,48,384]{4,3,2,1,0:T(8,128)(2,1)} async-done(((bf16[8,2,6,48,384]{4,3,2,1,0:T(8,128)(2,1)}), bf16[8,2,6,48,384]{4,3,2,1,0:T(8,128)(2,1)}, u32[]{:S(2)}, u32[]{:S(2)}) %all-to-all-start.3) | async-done | bytes 3538976 | tf_op jit(solution)/shard_map/all_to_all | solution.py:313
  225.1 5.8 %all-to-all-start.1 = ((bf16[8,2,6,48,384]{4,3,2,1,0:T(8,128)(2,1)}), bf16[8,2,6,48,384]{4,3,2,1,0:T(8,128)(2,1)}, u32[]{:S(2)}, u32[]{:S(2)}) async-start(bf16[8,2,6,48,384]{4,3,2,1,0:T(8,128)(2,1)} %middle_x.2), calls=%async_computation.1 | async-start | bytes 7077888 | tf_op jit(solution)/shard_map/all_to_all | solution.py:313
  230.9 9.7 %backward_yz.2.refs_8_ = f32[24,36864]{1,0:T(8,128)} custom-call(s32[1]{0:T(128)} %bitcast.column, bf16[8,2,6,48,384]{4,3,2,1,0:T(8,128)(2,1)} %all-to-all-done.3.far_pieces, bf16[24,9216]{1,0:T(8,128)(2,1)} %copy-done.1, bf16[24,9216]{1,0:T(8,128)(2,1)} %copy-done.2, bf16[24,9216]{1,0:T(8,128)(2,1)} %copy-done.3, bf16[24,9216]{1,0:T(8,128)(2,1)} %copy-done.4, ...), custom_call_target="tpu_custom_call" | custom-call | flops 2800000000 | bytes 14000000 | tf_op jit(solution)/shard_map/backward_yz/pallas_call | solution.py:296
  240.6 29.9 %all-to-all-done.1.far_pieces = bf16[8,2,6,48,384]{4,3,2,1,0:T(8,128)(2,1)} async-done(((bf16[8,2,6,48,384]{4,3,2,1,0:T(8,128)(2,1)}), bf16[8,2,6,48,384]{4,3,2,1,0:T(8,128)(2,1)}, u32[]{:S(2)}, u32[]{:S(2)}) %all-to-all-start.1) | async-done | bytes 3538976 | tf_op jit(solution)/shard_map/all_to_all | solution.py:313
  270.5 9.7 %backward_yz.3 = f32[24,36864]{1,0:T(8,128)} custom-call(s32[1]{0:T(128)} %bitcast.column, bf16[8,2,6,48,384]{4,3,2,1,0:T(8,128)(2,1)} %all-to-all-done.1.far_pieces, bf16[24,9216]{1,0:T(8,128)(2,1)} %copy-done, bf16[24,9216]{1,0:T(8,128)(2,1)} %copy-done.9, bf16[24,9216]{1,0:T(8,128)(2,1)} %copy-done.10, bf16[24,9216]{1,0:T(8,128)(2,1)} %copy-done.11, ...), custom_call_target="tpu_custom_call" | custom-call | flops 2800000000 | bytes 14000000 | tf_op jit(solution)/shard_map/backward_yz/pallas_call | solution.py:296
  (96 shorter events, 40.8 us)
Async XLA Ops:
  1.2 16.1 %collective-permute-start = (bf16[2,24,9216]{2,1,0:T(8,128)(2,1)S(1)}, bf16[2,24,9216]{2,1,0:T(8,128)(2,1)S(1)}, u32[]{:S(2)}, u32[]{:S(2)}) collective-permute-start(bf16[2,24,9216]{2,1,0:T(8,128)(2,1)S(1)} %slice.33), channel_id=1, source_target_pairs={{0,0},{128,136},{1,1},{129,137},{2,2},{130,138},{3,3},{131,139},{4... | collective-permute-start | bytes 2654216 | tf_op jit(solution)/shard_map/ppermute | solution.py:321
  6.8 10.5 %collective-permute-start.2 = (bf16[24,9216]{1,0:T(8,128)(2,1)S(1)}, bf16[24,9216]{1,0:T(8,128)(2,1)S(1)}, u32[]{:S(2)}, u32[]{:S(2)}) collective-permute-start(bf16[24,9216]{1,0:T(8,128)(2,1)S(1)} %get-tuple-element.14), channel_id=1, source_target_pairs={{0,32},{128,168},{1,33},{129,169},{2,34},{130,170},{3,35},{131,171... | collective-permute-start | bytes 1327112 | tf_op jit(solution)/shard_map/ppermute | solution.py:321
  17.4 11.4 %collective-permute-start.7 = (bf16[24,9216]{1,0:T(8,128)(2,1)S(1)}, bf16[24,9216]{1,0:T(8,128)(2,1)S(1)}, u32[]{:S(2)}, u32[]{:S(2)}) collective-permute-start(bf16[24,9216]{1,0:T(8,128)(2,1)S(1)} %fusion.6), channel_id=1, source_target_pairs={{0,64},{16,80},{32,96},{48,112},{136,200},{152,216},{168,232},{184... | collective-permute-start | bytes 1327112 | tf_op jit(solution)/shard_map/ppermute | solution.py:321
  18.7 10.1 %collective-permute-start.8 = (bf16[24,9216]{1,0:T(8,128)(2,1)S(1)}, bf16[24,9216]{1,0:T(8,128)(2,1)S(1)}, u32[]{:S(2)}, u32[]{:S(2)}) collective-permute-start(bf16[24,9216]{1,0:T(8,128)(2,1)S(1)} %fusion.6), channel_id=1, source_target_pairs={{0,192},{16,208},{32,224},{48,240},{136,72},{152,88},{168,104},{18... | collective-permute-start | bytes 1327112 | tf_op jit(solution)/shard_map/ppermute | solution.py:321
  28.9 10.7 %collective-permute-start.10 = (bf16[24,4608]{1,0:T(8,128)(2,1)S(1)}, bf16[24,4608]{1,0:T(8,128)(2,1)S(1)}, u32[]{:S(2)}, u32[]{:S(2)}) collective-permute-start(bf16[24,4608]{1,0:T(8,128)(2,1)S(1)} %get-tuple-element.18), channel_id=1, source_target_pairs={{192,128},{208,144},{224,160},{240,176},{72,8},{88,24},{104,40},{1... | collective-permute-start | bytes 663560 | tf_op jit(solution)/shard_map/ppermute | solution.py:321
  29.5 10.0 %collective-permute-start.9 = (bf16[24,4608]{1,0:T(8,128)(2,1)S(1)}, bf16[24,4608]{1,0:T(8,128)(2,1)S(1)}, u32[]{:S(2)}, u32[]{:S(2)}) collective-permute-start(bf16[24,4608]{1,0:T(8,128)(2,1)S(1)} %get-tuple-element.17), channel_id=1, source_target_pairs={{64,128},{80,144},{96,160},{112,176},{200,8},{216,24},{232,40},{24... | collective-permute-start | bytes 663560 | tf_op jit(solution)/shard_map/ppermute | solution.py:321
  32.9 15.9 %collective-permute-start.5 = (bf16[24,9216]{1,0:T(8,128)(2,1)S(1)}, bf16[24,9216]{1,0:T(8,128)(2,1)S(1)}, u32[]{:S(2)}, u32[]{:S(2)}) collective-permute-start(bf16[24,9216]{1,0:T(8,128)(2,1)S(1)} %get-tuple-element.11), channel_id=1, source_target_pairs={{0,32},{128,168},{1,33},{129,169},{2,34},{130,170},{3,35},{131,171... | collective-permute-start | bytes 1327112 | tf_op jit(solution)/shard_map/ppermute | solution.py:321
  38.2 10.6 %collective-permute-start.6 = (bf16[24,9216]{1,0:T(8,128)(2,1)S(1)}, bf16[24,9216]{1,0:T(8,128)(2,1)S(1)}, u32[]{:S(2)}, u32[]{:S(2)}) collective-permute-start(bf16[24,9216]{1,0:T(8,128)(2,1)S(1)} %get-tuple-element.12), channel_id=1, source_target_pairs={{0,48},{128,184},{1,49},{129,185},{2,50},{130,186},{3,51},{131,187... | collective-permute-start | bytes 1327112 | tf_op jit(solution)/shard_map/ppermute | solution.py:321
  39.7 18.0 %collective-permute-start.21 = (bf16[24,9216]{1,0:T(8,128)(2,1)S(1)}, bf16[24,9216]{1,0:T(8,128)(2,1)S(1)}, u32[]{:S(2)}, u32[]{:S(2)}) collective-permute-start(bf16[24,9216]{1,0:T(8,128)(2,1)S(1)} %maximum_add_fusion.refs_0_), channel_id=1, source_target_pairs={{0,16},{8,24},{16,0},{24,8},{32,48},{40,56},{48,32},{56,40},{64,80... | collective-permute-start | bytes 1327112 | tf_op jit(solution)/shard_map/ppermute | solution.py:321
  48.9 13.6 %collective-permute-start.22 = (bf16[24,9216]{1,0:T(8,128)(2,1)S(1)}, bf16[24,9216]{1,0:T(8,128)(2,1)S(1)}, u32[]{:S(2)}, u32[]{:S(2)}) collective-permute-start(bf16[24,9216]{1,0:T(8,128)(2,1)S(1)} %maximum_add_fusion.refs_0_), channel_id=1, source_target_pairs={{0,32},{8,40},{16,48},{24,56},{32,0},{40,8},{48,16},{56,24},{64,96... | collective-permute-start | bytes 1327112 | tf_op jit(solution)/shard_map/ppermute | solution.py:321
  53.0 14.0 %collective-permute-start.23 = (bf16[24,9216]{1,0:T(8,128)(2,1)S(1)}, bf16[24,9216]{1,0:T(8,128)(2,1)S(1)}, u32[]{:S(2)}, u32[]{:S(2)}) collective-permute-start(bf16[24,9216]{1,0:T(8,128)(2,1)S(1)} %maximum_add_fusion.refs_0_), channel_id=1, source_target_pairs={{0,48},{8,56},{16,32},{24,40},{32,16},{40,24},{48,0},{56,8},{64,11... | collective-permute-start | bytes 1327112 | tf_op jit(solution)/shard_map/ppermute | solution.py:321
  53.0 16.6 %collective-permute-start.11 = (bf16[24,9216]{1,0:T(8,128)(2,1)S(1)}, bf16[24,9216]{1,0:T(8,128)(2,1)S(1)}, u32[]{:S(2)}, u32[]{:S(2)}) collective-permute-start(bf16[24,9216]{1,0:T(8,128)(2,1)S(1)} %fusion.7), channel_id=1, source_target_pairs={{0,64},{16,80},{32,96},{48,112},{136,200},{152,216},{168,232},{184... | collective-permute-start | bytes 1327112 | tf_op jit(solution)/shard_map/ppermute | solution.py:321
  54.3 15.3 %collective-permute-start.12 = (bf16[24,9216]{1,0:T(8,128)(2,1)S(1)}, bf16[24,9216]{1,0:T(8,128)(2,1)}, u32[]{:S(2)}, u32[]{:S(2)}) collective-permute-start(bf16[24,9216]{1,0:T(8,128)(2,1)S(1)} %fusion.7), channel_id=1, source_target_pairs={{0,192},{16,208},{32,224},{48,240},{136,72},{152,88},{168,104},{18... | collective-permute-start | bytes 1327112 | tf_op jit(solution)/shard_map/ppermute | solution.py:321
  57.7 12.6 %collective-permute-start.13 = (bf16[24,9216]{1,0:T(8,128)(2,1)S(1)}, bf16[24,9216]{1,0:T(8,128)(2,1)}, u32[]{:S(2)}, u32[]{:S(2)}) collective-permute-start(bf16[24,9216]{1,0:T(8,128)(2,1)S(1)} %fusion.7), channel_id=1, source_target_pairs={{0,128},{16,144},{32,160},{48,176},{136,8},{152,24},{168,40},{184,... | collective-permute-start | bytes 1327112 | tf_op jit(solution)/shard_map/ppermute | solution.py:321
  62.5 9.2 %collective-permute-start.24 = (bf16[24,9216]{1,0:T(8,128)(2,1)S(1)}, bf16[24,9216]{1,0:T(8,128)(2,1)S(1)}, u32[]{:S(2)}, u32[]{:S(2)}) collective-permute-start(bf16[24,9216]{1,0:T(8,128)(2,1)S(1)} %maximum_add_fusion.refs_0_), channel_id=1, source_target_pairs={{0,8},{8,0},{16,24},{24,16},{32,40},{40,32},{48,56},{56,48},{64,72... | collective-permute-start | bytes 1327112 | tf_op jit(solution)/shard_map/ppermute | solution.py:321
  83.2 48.7 %all-to-all-start.2 = ((bf16[8,2,6,48,384]{4,3,2,1,0:T(8,128)(2,1)}), bf16[8,2,6,48,384]{4,3,2,1,0:T(8,128)(2,1)}, u32[]{:S(2)}, u32[]{:S(2)}) async-start(bf16[8,2,6,48,384]{4,3,2,1,0:T(8,128)(2,1)} %forward_zy.3), calls=%async_computation.2 | async-start | bytes 7077888 | tf_op jit(solution)/shard_map/all_to_all | solution.py:313
  89.7 13.0 %collective-permute-start.14 = (bf16[24,9216]{1,0:T(8,128)(2,1)S(1)}, bf16[24,9216]{1,0:T(8,128)(2,1)S(1)}, u32[]{:S(2)}, u32[]{:S(2)}) collective-permute-start(bf16[24,9216]{1,0:T(8,128)(2,1)S(1)} %add_select_fusion.refs_0_), channel_id=1, source_target_pairs={{0,16},{8,24},{16,0},{24,8},{32,48},{40,56},{48,32},{56,40},{64,80... | collective-permute-start | bytes 1327112 | tf_op jit(solution)/shard_map/ppermute | solution.py:321
  89.8 24.4 %collective-permute-start.15 = (bf16[24,9216]{1,0:T(8,128)(2,1)S(1)}, bf16[24,9216]{1,0:T(8,128)(2,1)S(1)}, u32[]{:S(2)}, u32[]{:S(2)}) collective-permute-start(bf16[24,9216]{1,0:T(8,128)(2,1)S(1)} %add_select_fusion.refs_0_), channel_id=1, source_target_pairs={{0,32},{8,40},{16,48},{24,56},{32,0},{40,8},{48,16},{56,24},{64,96... | collective-permute-start | bytes 1327112 | tf_op jit(solution)/shard_map/ppermute | solution.py:321
  94.4 22.3 %collective-permute-start.16 = (bf16[24,9216]{1,0:T(8,128)(2,1)S(1)}, bf16[24,9216]{1,0:T(8,128)(2,1)S(1)}, u32[]{:S(2)}, u32[]{:S(2)}) collective-permute-start(bf16[24,9216]{1,0:T(8,128)(2,1)S(1)} %add_select_fusion.refs_0_), channel_id=1, source_target_pairs={{0,48},{8,56},{16,32},{24,40},{32,16},{40,24},{48,0},{56,8},{64,11... | collective-permute-start | bytes 1327112 | tf_op jit(solution)/shard_map/ppermute | solution.py:321
  94.4 22.3 %collective-permute-start.17 = (bf16[24,9216]{1,0:T(8,128)(2,1)S(1)}, bf16[24,9216]{1,0:T(8,128)(2,1)S(1)}, u32[]{:S(2)}, u32[]{:S(2)}) collective-permute-start(bf16[24,9216]{1,0:T(8,128)(2,1)S(1)} %add_select_fusion.refs_0_), channel_id=1, source_target_pairs={{0,8},{8,0},{16,24},{24,16},{32,40},{40,32},{48,56},{56,48},{64,72... | collective-permute-start | bytes 1327112 | tf_op jit(solution)/shard_map/ppermute | solution.py:321
  102.7 14.0 %collective-permute-start.18 = (bf16[24,9216]{1,0:T(8,128)(2,1)S(1)}, bf16[24,9216]{1,0:T(8,128)(2,1)S(1)}, u32[]{:S(2)}, u32[]{:S(2)}) collective-permute-start(bf16[24,9216]{1,0:T(8,128)(2,1)S(1)} %collective-permute-done.14.refs_1_), channel_id=1, source_target_pairs={{0,8},{8,0},{16,24},{24,16},{32,40},{40,32},{48,56},{56,48},{64,72... | collective-permute-start | bytes 1327112 | tf_op jit(solution)/shard_map/ppermute | solution.py:321
  131.9 47.0 %all-to-all-start = ((bf16[8,2,6,48,384]{4,3,2,1,0:T(8,128)(2,1)}), bf16[8,2,6,48,384]{4,3,2,1,0:T(8,128)(2,1)}, u32[]{:S(2)}, u32[]{:S(2)}) async-start(bf16[8,2,6,48,384]{4,3,2,1,0:T(8,128)(2,1)} %forward_zy.2), calls=%async_computation | async-start | bytes 7077888 | tf_op jit(solution)/shard_map/all_to_all | solution.py:313
  178.9 46.2 %all-to-all-start.3 = ((bf16[8,2,6,48,384]{4,3,2,1,0:T(8,128)(2,1)}), bf16[8,2,6,48,384]{4,3,2,1,0:T(8,128)(2,1)}, u32[]{:S(2)}, u32[]{:S(2)}) async-start(bf16[8,2,6,48,384]{4,3,2,1,0:T(8,128)(2,1)} %middle_x.3), calls=%async_computation.3 | async-start | bytes 7077888 | tf_op jit(solution)/shard_map/all_to_all | solution.py:313
  225.1 45.4 %all-to-all-start.1 = ((bf16[8,2,6,48,384]{4,3,2,1,0:T(8,128)(2,1)}), bf16[8,2,6,48,384]{4,3,2,1,0:T(8,128)(2,1)}, u32[]{:S(2)}, u32[]{:S(2)}) async-start(bf16[8,2,6,48,384]{4,3,2,1,0:T(8,128)(2,1)} %middle_x.2), calls=%async_computation.1 | async-start | bytes 7077888 | tf_op jit(solution)/shard_map/all_to_all | solution.py:313
  (24 other events, 157.7 us)

commit v9 on v8

--- a/solution.py
+++ b/solution.py
@@ -333,14 +333,7 @@
     return first + sum(to_x(orbitals[which, :, step * CUT : (step + 1) * CUT], step) for step in range(1, 4))
 
 
-def beside(mine, is_root):
-    away = sum(
-        move(mine, [(band_of(2 * c, x, c), band_of(2 * c + up, x, c)) for c in range(2) for x in range(4)]) for up in (1, 3)
-    )
-    return jnp.where(is_root, mine, away)
-
-
-def along_z(mine, is_root, *others):
+def along_z(mine, is_root):
     away = sum(
         move(mine, [(band_of(2 * c, x, c), band_of(2 * c + up, x, c)) for c in range(2) for x in range(4)])
         for up in (1, 3, 2)
@@ -379,12 +372,11 @@
     first = to_x(orbitals[:, :, :CUT], 0)
     cut_0 = scatter(orbitals, 0, first[0])
     cut_1 = scatter(after(orbitals, cut_0), 1, first[1])
-    near_0 = beside(cut_0, is_root)
-    full_0 = beyond(near_0)
+    full_0 = along_z(cut_0, is_root)
     mine_0 = gather_x(full_0)
     batch_0 = [mine_0, other_core(mine_0)]
     pieces_0 = forward(column, orbitals, batch_0)
-    full_1 = along_z(after(cut_1, full_0), is_root, pieces_0)
+    full_1 = along_z(after(cut_1, full_0), is_root)
     pieces_0 = after(pieces_0, full_1)
     mine_1 = gather_x(full_1)
     batch_1 = [mine_1, other_core(mine_1)]

time: 283 us -> 287 us (1.014)
  the two profiles are of different devices: /device:TPU:32 before, /device:TPU:6 now
where the time goes in v9:
time: 287 us; the launch traced here: 286 us
  waiting for transfers between devices  131 us (46%)
  starting transfers between devices  78.5 us (27%)
  Pallas kernels  62.8 us (22%)
  local copies, waits for them, and re-layouts  7.99 us (3%)
  other arithmetic  5.19 us (2%)
    all_to_all x4, waiting for transfers between devices, exchange(): return lax.all_to_all(pieces, 'grid', 0, 0, tiled=True)  92.3 us
    ppermute x27, starting transfers between devices, move(): return lax.ppermute(array, 'band', pairs)  45.6 us
    ppermute x27, waiting for transfers between devices, move(): return lax.ppermute(array, 'band', pairs)  38.4 us
    all_to_all x4, starting transfers between devices, exchange(): return lax.all_to_all(pieces, 'grid', 0, 0, tiled=True)  32.9 us
    pallas_call x2, Pallas kernels, middle(): pl.pallas_call(middle_body, in_specs=[FAR, FAR, VECTOR, VECTOR], out_spec...  24.4 us
    pallas_call x2, Pallas kernels, backward(): pl.pallas_call(backward_body, in_specs=[SCALAR] + [FAR] * (1 + len(cuts)...  19.4 us
    pallas_call x2, Pallas kernels, forward(): pl.pallas_call(forward_body, in_specs=[SCALAR] + [FAR] * (1 + len(cuts))...  19 us
  transfers between devices with their start and end apart: 31, of which 12 were waited for; matrix products, arithmetic and copies ran while one was open for 3% of the time, Pallas kernels for 15%

profile of v9, /device:TPU:6, one launch (start us, length us, event | category | flops | bytes accessed | tf_op | source)
XLA Modules:
  0.0 285.7 jit_solution(10519414813164442519)
XLA Ops:
  7.0 11.0 %collective-permute-done.3 = bf16[24,9216]{1,0:T(8,128)(2,1)S(1)} collective-permute-done((bf16[24,9216]{1,0:T(8,128)(2,1)S(1)}, bf16[24,9216]{1,0:T(8,128)(2,1)S(1)}, u32[]{:S(2)}, u32[]{:S(2)}) %collective-permute-start.3) | collective-permute-done | bytes 442400 | tf_op jit(solution)/shard_map/ppermute | solution.py:321
  26.4 9.5 %collective-permute-done.8 = bf16[24,9216]{1,0:T(8,128)(2,1)S(1)} collective-permute-done((bf16[24,9216]{1,0:T(8,128)(2,1)S(1)}, bf16[24,9216]{1,0:T(8,128)(2,1)S(1)}, u32[]{:S(2)}, u32[]{:S(2)}) %collective-permute-start.8) | collective-permute-done | bytes 442400 | tf_op jit(solution)/shard_map/ppermute | solution.py:321
  38.6 2.5 collective-permute-start.22
  43.6 6.7 %collective-permute-start.11 = (bf16[24,9216]{1,0:T(8,128)(2,1)S(1)}, bf16[24,9216]{1,0:T(8,128)(2,1)}, u32[]{:S(2)}, u32[]{:S(2)}) collective-permute-start(bf16[24,9216]{1,0:T(8,128)(2,1)S(1)} %fusion.7), channel_id=1, source_target_pairs={{0,192},{16,208},{32,224},{48,240},{136,72},{152,88},{168,104},{18... | collective-permute-start | bytes 1327112 | tf_op jit(solution)/shard_map/ppermute | solution.py:321
  52.3 5.2 %collective-permute-done.21.refs_2_ = bf16[24,9216]{1,0:T(8,128)(2,1)S(1)} collective-permute-done((bf16[24,9216]{1,0:T(8,128)(2,1)S(1)}, bf16[24,9216]{1,0:T(8,128)(2,1)S(1)}, u32[]{:S(2)}, u32[]{:S(2)}) %collective-permute-start.21) | collective-permute-done | bytes 442400 | tf_op jit(solution)/shard_map/ppermute | solution.py:321
  57.6 3.4 %collective-permute-done.22.refs_3_ = bf16[24,9216]{1,0:T(8,128)(2,1)S(1)} collective-permute-done((bf16[24,9216]{1,0:T(8,128)(2,1)S(1)}, bf16[24,9216]{1,0:T(8,128)(2,1)S(1)}, u32[]{:S(2)}, u32[]{:S(2)}) %collective-permute-start.22) | collective-permute-done | bytes 442400 | tf_op jit(solution)/shard_map/ppermute | solution.py:321
  65.2 9.5 %forward_zy.3 = bf16[8,2,6,48,384]{4,3,2,1,0:T(8,128)(2,1)} custom-call(s32[1]{0:T(128)} %bitcast.column, bf16[2,24,36864]{2,1,0:T(8,128)(2,1)} %far_orbitals.3, bf16[24,9216]{1,0:T(8,128)(2,1)} %copy-done, bf16[24,9216]{1,0:T(8,128)(2,1)} %copy-done.2, bf16[24,9216]{1,0:T(8,128)(2,1)} %copy-done.3, bf16[24,9216]{1,0:T(8,128)(2,1)} %copy-done.4, ...), custom_call_target="tpu_custom_call" | custom-call | flops 2800000000 | bytes 14000000 | tf_op jit(solution)/shard_map/forward_zy/pallas_call | solution.py:148
  74.7 16.3 %all-to-all-start.2 = ((bf16[8,2,6,48,384]{4,3,2,1,0:T(8,128)(2,1)}), bf16[8,2,6,48,384]{4,3,2,1,0:T(8,128)(2,1)}, u32[]{:S(2)}, u32[]{:S(2)}) async-start(bf16[8,2,6,48,384]{4,3,2,1,0:T(8,128)(2,1)} %forward_zy.3), calls=%async_computation.2 | async-start | bytes 7077888 | tf_op jit(solution)/shard_map/all_to_all | solution.py:313
  91.0 4.0 %collective-permute-start.14 = (bf16[24,9216]{1,0:T(8,128)(2,1)S(1)}, bf16[24,9216]{1,0:T(8,128)(2,1)S(1)}, u32[]{:S(2)}, u32[]{:S(2)}) collective-permute-start(bf16[24,9216]{1,0:T(8,128)(2,1)S(1)} %add_select_fusion.refs_0_), channel_id=1, source_target_pairs={{0,32},{8,40},{16,48},{24,56},{32,0},{40,8},{48,16},{56,24},{64,96... | collective-permute-start | bytes 1327112 | tf_op jit(solution)/shard_map/ppermute | solution.py:321
  95.7 4.7 %collective-permute-start.16 = (bf16[24,9216]{1,0:T(8,128)(2,1)S(1)}, bf16[24,9216]{1,0:T(8,128)(2,1)S(1)}, u32[]{:S(2)}, u32[]{:S(2)}) collective-permute-start(bf16[24,9216]{1,0:T(8,128)(2,1)S(1)} %add_select_fusion.refs_0_), channel_id=1, source_target_pairs={{0,8},{8,0},{16,24},{24,16},{32,40},{40,32},{48,56},{56,48},{64,72... | collective-permute-start | bytes 1327112 | tf_op jit(solution)/shard_map/ppermute | solution.py:321
  100.5 8.5 %collective-permute-start.17 = (bf16[24,9216]{1,0:T(8,128)(2,1)S(1)}, bf16[24,9216]{1,0:T(8,128)(2,1)S(1)}, u32[]{:S(2)}, u32[]{:S(2)}) collective-permute-start(bf16[24,9216]{1,0:T(8,128)(2,1)S(1)} %collective-permute-done.13.refs_1_), channel_id=1, source_target_pairs={{0,8},{8,0},{16,24},{24,16},{32,40},{40,32},{48,56},{56,48},{64,72... | collective-permute-start | bytes 1327112 | tf_op jit(solution)/shard_map/ppermute | solution.py:321
  111.2 6.1 %collective-permute-done.15.refs_3_ = bf16[24,9216]{1,0:T(8,128)(2,1)S(1)} collective-permute-done((bf16[24,9216]{1,0:T(8,128)(2,1)S(1)}, bf16[24,9216]{1,0:T(8,128)(2,1)S(1)}, u32[]{:S(2)}, u32[]{:S(2)}) %collective-permute-start.15) | collective-permute-done | bytes 442400 | tf_op jit(solution)/shard_map/ppermute | solution.py:321
  120.8 9.5 %forward_zy.2 = bf16[8,2,6,48,384]{4,3,2,1,0:T(8,128)(2,1)} custom-call(s32[1]{0:T(128)} %bitcast.column, bf16[2,24,36864]{2,1,0:T(8,128)(2,1)} %far_orbitals.3, bf16[24,9216]{1,0:T(8,128)(2,1)} %copy-done.1, bf16[24,9216]{1,0:T(8,128)(2,1)} %copy-done.9, bf16[24,9216]{1,0:T(8,128)(2,1)} %copy-done.10, bf16[24,9216]{1,0:T(8,128)(2,1)} %copy-done.11, ...), custom_call_target="tpu_custom_call" | custom-call | flops 2800000000 | bytes 14000000 | tf_op jit(solution)/shard_map/forward_zy/pallas_call | solution.py:148
  130.3 7.3 %all-to-all-start = ((bf16[8,2,6,48,384]{4,3,2,1,0:T(8,128)(2,1)}), bf16[8,2,6,48,384]{4,3,2,1,0:T(8,128)(2,1)}, u32[]{:S(2)}, u32[]{:S(2)}) async-start(bf16[8,2,6,48,384]{4,3,2,1,0:T(8,128)(2,1)} %forward_zy.2), calls=%async_computation | async-start | bytes 7077888 | tf_op jit(solution)/shard_map/all_to_all | solution.py:313
  137.6 2.5 select_multiply_fusion.far_kernel
  140.2 12.2 %middle_x.3 = bf16[8,2,6,48,384]{4,3,2,1,0:T(8,128)(2,1)} custom-call(bf16[8,2,6,48,384]{4,3,2,1,0:T(8,128)(2,1)} %all-to-all-done.2.far_pieces, f32[12,192,384]{2,1,0:T(8,128)} %select_multiply_fusion.far_kernel, bf16[192,192]{1,0:T(8,128)(2,1)} %constant.117.clone.refs_9_.x_table, bf16[192,192]{1,0:T(8,128)(2,1)} %constant.118.clone.x_back.refs_8_.refs_9_), custom_call_target="tpu_custom_call" | custom-call | flops 2800000000 | bytes 14000000 | tf_op jit(solution)/shard_map/middle_x/pallas_call | solution.py:222
  152.4 28.5 %all-to-all-done.far_pieces = bf16[8,2,6,48,384]{4,3,2,1,0:T(8,128)(2,1)} async-done(((bf16[8,2,6,48,384]{4,3,2,1,0:T(8,128)(2,1)}), bf16[8,2,6,48,384]{4,3,2,1,0:T(8,128)(2,1)}, u32[]{:S(2)}, u32[]{:S(2)}) %all-to-all-start) | async-done | bytes 3538976 | tf_op jit(solution)/shard_map/all_to_all | solution.py:313
  180.9 4.5 %all-to-all-start.3 = ((bf16[8,2,6,48,384]{4,3,2,1,0:T(8,128)(2,1)}), bf16[8,2,6,48,384]{4,3,2,1,0:T(8,128)(2,1)}, u32[]{:S(2)}, u32[]{:S(2)}) async-start(bf16[8,2,6,48,384]{4,3,2,1,0:T(8,128)(2,1)} %middle_x.3), calls=%async_computation.3 | async-start | bytes 7077888 | tf_op jit(solution)/shard_map/all_to_all | solution.py:313
  185.4 12.2 %middle_x.2 = bf16[8,2,6,48,384]{4,3,2,1,0:T(8,128)(2,1)} custom-call(bf16[8,2,6,48,384]{4,3,2,1,0:T(8,128)(2,1)} %all-to-all-done.far_pieces, f32[12,192,384]{2,1,0:T(8,128)} %select_multiply_fusion.far_kernel, bf16[192,192]{1,0:T(8,128)(2,1)} %constant.117.clone.refs_9_.x_table, bf16[192,192]{1,0:T(8,128)(2,1)} %constant.118.clone.x_back.refs_8_.refs_9_), custom_call_target="tpu_custom_call" | custom-call | flops 2800000000 | bytes 14000000 | tf_op jit(solution)/shard_map/middle_x/pallas_call | solution.py:222
  197.7 31.1 %all-to-all-done.3.far_pieces = bf16[8,2,6,48,384]{4,3,2,1,0:T(8,128)(2,1)} async-done(((bf16[8,2,6,48,384]{4,3,2,1,0:T(8,128)(2,1)}), bf16[8,2,6,48,384]{4,3,2,1,0:T(8,128)(2,1)}, u32[]{:S(2)}, u32[]{:S(2)}) %all-to-all-start.3) | async-done | bytes 3538976 | tf_op jit(solution)/shard_map/all_to_all | solution.py:313
  228.7 4.7 %all-to-all-start.1 = ((bf16[8,2,6,48,384]{4,3,2,1,0:T(8,128)(2,1)}), bf16[8,2,6,48,384]{4,3,2,1,0:T(8,128)(2,1)}, u32[]{:S(2)}, u32[]{:S(2)}) async-start(bf16[8,2,6,48,384]{4,3,2,1,0:T(8,128)(2,1)} %middle_x.2), calls=%async_computation.1 | async-start | bytes 7077888 | tf_op jit(solution)/shard_map/all_to_all | solution.py:313
  233.5 9.7 %backward_yz.2.refs_8_ = f32[24,36864]{1,0:T(8,128)} custom-call(s32[1]{0:T(128)} %bitcast.column, bf16[8,2,6,48,384]{4,3,2,1,0:T(8,128)(2,1)} %all-to-all-done.3.far_pieces, bf16[24,9216]{1,0:T(8,128)(2,1)} %copy-done, bf16[24,9216]{1,0:T(8,128)(2,1)} %copy-done.2, bf16[24,9216]{1,0:T(8,128)(2,1)} %copy-done.3, bf16[24,9216]{1,0:T(8,128)(2,1)} %copy-done.4, ...), custom_call_target="tpu_custom_call" | custom-call | flops 2800000000 | bytes 14000000 | tf_op jit(solution)/shard_map/backward_yz/pallas_call | solution.py:296
  243.1 32.6 %all-to-all-done.1.far_pieces = bf16[8,2,6,48,384]{4,3,2,1,0:T(8,128)(2,1)} async-done(((bf16[8,2,6,48,384]{4,3,2,1,0:T(8,128)(2,1)}), bf16[8,2,6,48,384]{4,3,2,1,0:T(8,128)(2,1)}, u32[]{:S(2)}, u32[]{:S(2)}) %all-to-all-start.1) | async-done | bytes 3538976 | tf_op jit(solution)/shard_map/all_to_all | solution.py:313
  275.8 9.7 %backward_yz.3 = f32[24,36864]{1,0:T(8,128)} custom-call(s32[1]{0:T(128)} %bitcast.column, bf16[8,2,6,48,384]{4,3,2,1,0:T(8,128)(2,1)} %all-to-all-done.1.far_pieces, bf16[24,9216]{1,0:T(8,128)(2,1)} %copy-done.1, bf16[24,9216]{1,0:T(8,128)(2,1)} %copy-done.9, bf16[24,9216]{1,0:T(8,128)(2,1)} %copy-done.10, bf16[24,9216]{1,0:T(8,128)(2,1)} %copy-done.11, ...), custom_call_target="tpu_custom_call" | custom-call | flops 2800000000 | bytes 14000000 | tf_op jit(solution)/shard_map/backward_yz/pallas_call | solution.py:296
  (94 shorter events, 33.1 us)
Async XLA Ops:
  1.2 16.7 %collective-permute-start = (bf16[2,24,9216]{2,1,0:T(8,128)(2,1)S(1)}, bf16[2,24,9216]{2,1,0:T(8,128)(2,1)S(1)}, u32[]{:S(2)}, u32[]{:S(2)}) collective-permute-start(bf16[2,24,9216]{2,1,0:T(8,128)(2,1)S(1)} %slice.27), channel_id=1, source_target_pairs={{0,0},{128,136},{1,1},{129,137},{2,2},{130,138},{3,3},{131,139},{4... | collective-permute-start | bytes 2654216 | tf_op jit(solution)/shard_map/ppermute | solution.py:321
  5.6 12.3 %collective-permute-start.3 = (bf16[24,9216]{1,0:T(8,128)(2,1)S(1)}, bf16[24,9216]{1,0:T(8,128)(2,1)S(1)}, u32[]{:S(2)}, u32[]{:S(2)}) collective-permute-start(bf16[24,9216]{1,0:T(8,128)(2,1)S(1)} %get-tuple-element.15), channel_id=1, source_target_pairs={{0,48},{128,184},{1,49},{129,185},{2,50},{130,186},{3,51},{131,187... | collective-permute-start | bytes 1327112 | tf_op jit(solution)/shard_map/ppermute | solution.py:321
  18.0 7.1 %collective-permute-start.7 = (bf16[24,9216]{1,0:T(8,128)(2,1)S(1)}, bf16[24,9216]{1,0:T(8,128)(2,1)S(1)}, u32[]{:S(2)}, u32[]{:S(2)}) collective-permute-start(bf16[24,9216]{1,0:T(8,128)(2,1)S(1)} %fusion.6), channel_id=1, source_target_pairs={{0,64},{16,80},{32,96},{48,112},{136,200},{152,216},{168,232},{184... | collective-permute-start | bytes 1327112 | tf_op jit(solution)/shard_map/ppermute | solution.py:321
  19.3 16.6 %collective-permute-start.8 = (bf16[24,9216]{1,0:T(8,128)(2,1)S(1)}, bf16[24,9216]{1,0:T(8,128)(2,1)S(1)}, u32[]{:S(2)}, u32[]{:S(2)}) collective-permute-start(bf16[24,9216]{1,0:T(8,128)(2,1)S(1)} %fusion.6), channel_id=1, source_target_pairs={{0,192},{16,208},{32,224},{48,240},{136,72},{152,88},{168,104},{18... | collective-permute-start | bytes 1327112 | tf_op jit(solution)/shard_map/ppermute | solution.py:321
  20.7 15.3 %collective-permute-start.9 = (bf16[24,9216]{1,0:T(8,128)(2,1)S(1)}, bf16[24,9216]{1,0:T(8,128)(2,1)S(1)}, u32[]{:S(2)}, u32[]{:S(2)}) collective-permute-start(bf16[24,9216]{1,0:T(8,128)(2,1)S(1)} %fusion.6), channel_id=1, source_target_pairs={{0,128},{16,144},{32,160},{48,176},{136,8},{152,24},{168,40},{184,... | collective-permute-start | bytes 1327112 | tf_op jit(solution)/shard_map/ppermute | solution.py:321
  23.4 15.3 %collective-permute-start.4 = (bf16[24,9216]{1,0:T(8,128)(2,1)S(1)}, bf16[24,9216]{1,0:T(8,128)(2,1)S(1)}, u32[]{:S(2)}, u32[]{:S(2)}) collective-permute-start(bf16[24,9216]{1,0:T(8,128)(2,1)S(1)} %get-tuple-element.13), channel_id=1, source_target_pairs={{0,16},{128,152},{1,17},{129,153},{2,18},{130,154},{3,19},{131,155... | collective-permute-start | bytes 1327112 | tf_op jit(solution)/shard_map/ppermute | solution.py:321
  24.1 17.1 %collective-permute-start.5 = (bf16[24,9216]{1,0:T(8,128)(2,1)S(1)}, bf16[24,9216]{1,0:T(8,128)(2,1)S(1)}, u32[]{:S(2)}, u32[]{:S(2)}) collective-permute-start(bf16[24,9216]{1,0:T(8,128)(2,1)S(1)} %get-tuple-element.11), channel_id=1, source_target_pairs={{0,32},{128,168},{1,33},{129,169},{2,34},{130,170},{3,35},{131,171... | collective-permute-start | bytes 1327112 | tf_op jit(solution)/shard_map/ppermute | solution.py:321
  25.2 16.0 %collective-permute-start.6 = (bf16[24,9216]{1,0:T(8,128)(2,1)S(1)}, bf16[24,9216]{1,0:T(8,128)(2,1)S(1)}, u32[]{:S(2)}, u32[]{:S(2)}) collective-permute-start(bf16[24,9216]{1,0:T(8,128)(2,1)S(1)} %get-tuple-element.12), channel_id=1, source_target_pairs={{0,48},{128,184},{1,49},{129,185},{2,50},{130,186},{3,51},{131,187... | collective-permute-start | bytes 1327112 | tf_op jit(solution)/shard_map/ppermute | solution.py:321
  36.0 14.2 %collective-permute-start.20 = (bf16[24,9216]{1,0:T(8,128)(2,1)S(1)}, bf16[24,9216]{1,0:T(8,128)(2,1)S(1)}, u32[]{:S(2)}, u32[]{:S(2)}) collective-permute-start(bf16[24,9216]{1,0:T(8,128)(2,1)S(1)} %add_select_fusion.1.refs_0_), channel_id=1, source_target_pairs={{0,16},{8,24},{16,0},{24,8},{32,48},{40,56},{48,32},{56,40},{64,80... | collective-permute-start | bytes 1327112 | tf_op jit(solution)/shard_map/ppermute | solution.py:321
  38.4 19.2 %collective-permute-start.21 = (bf16[24,9216]{1,0:T(8,128)(2,1)S(1)}, bf16[24,9216]{1,0:T(8,128)(2,1)S(1)}, u32[]{:S(2)}, u32[]{:S(2)}) collective-permute-start(bf16[24,9216]{1,0:T(8,128)(2,1)S(1)} %add_select_fusion.1.refs_0_), channel_id=1, source_target_pairs={{0,32},{8,40},{16,48},{24,56},{32,0},{40,8},{48,16},{56,24},{64,96... | collective-permute-start | bytes 1327112 | tf_op jit(solution)/shard_map/ppermute | solution.py:321
  38.6 22.3 %collective-permute-start.22 = (bf16[24,9216]{1,0:T(8,128)(2,1)S(1)}, bf16[24,9216]{1,0:T(8,128)(2,1)S(1)}, u32[]{:S(2)}, u32[]{:S(2)}) collective-permute-start(bf16[24,9216]{1,0:T(8,128)(2,1)S(1)} %add_select_fusion.1.refs_0_), channel_id=1, source_target_pairs={{0,48},{8,56},{16,32},{24,40},{32,16},{40,24},{48,0},{56,8},{64,11... | collective-permute-start | bytes 1327112 | tf_op jit(solution)/shard_map/ppermute | solution.py:321
  42.3 18.7 %collective-permute-start.10 = (bf16[24,9216]{1,0:T(8,128)(2,1)S(1)}, bf16[24,9216]{1,0:T(8,128)(2,1)S(1)}, u32[]{:S(2)}, u32[]{:S(2)}) collective-permute-start(bf16[24,9216]{1,0:T(8,128)(2,1)S(1)} %fusion.7), channel_id=1, source_target_pairs={{0,64},{16,80},{32,96},{48,112},{136,200},{152,216},{168,232},{184... | collective-permute-start | bytes 1327112 | tf_op jit(solution)/shard_map/ppermute | solution.py:321
  43.6 17.9 %collective-permute-start.11 = (bf16[24,9216]{1,0:T(8,128)(2,1)S(1)}, bf16[24,9216]{1,0:T(8,128)(2,1)}, u32[]{:S(2)}, u32[]{:S(2)}) collective-permute-start(bf16[24,9216]{1,0:T(8,128)(2,1)S(1)} %fusion.7), channel_id=1, source_target_pairs={{0,192},{16,208},{32,224},{48,240},{136,72},{152,88},{168,104},{18... | collective-permute-start | bytes 1327112 | tf_op jit(solution)/shard_map/ppermute | solution.py:321
  50.2 11.5 %collective-permute-start.12 = (bf16[24,9216]{1,0:T(8,128)(2,1)S(1)}, bf16[24,9216]{1,0:T(8,128)(2,1)}, u32[]{:S(2)}, u32[]{:S(2)}) collective-permute-start(bf16[24,9216]{1,0:T(8,128)(2,1)S(1)} %fusion.7), channel_id=1, source_target_pairs={{0,128},{16,144},{32,160},{48,176},{136,8},{152,24},{168,40},{184,... | collective-permute-start | bytes 1327112 | tf_op jit(solution)/shard_map/ppermute | solution.py:321
  74.7 55.6 %all-to-all-start.2 = ((bf16[8,2,6,48,384]{4,3,2,1,0:T(8,128)(2,1)}), bf16[8,2,6,48,384]{4,3,2,1,0:T(8,128)(2,1)}, u32[]{:S(2)}, u32[]{:S(2)}) async-start(bf16[8,2,6,48,384]{4,3,2,1,0:T(8,128)(2,1)} %forward_zy.3), calls=%async_computation.2 | async-start | bytes 7077888 | tf_op jit(solution)/shard_map/all_to_all | solution.py:313
  91.0 9.4 %collective-permute-start.13 = (bf16[24,9216]{1,0:T(8,128)(2,1)S(1)}, bf16[24,9216]{1,0:T(8,128)(2,1)S(1)}, u32[]{:S(2)}, u32[]{:S(2)}) collective-permute-start(bf16[24,9216]{1,0:T(8,128)(2,1)S(1)} %add_select_fusion.refs_0_), channel_id=1, source_target_pairs={{0,16},{8,24},{16,0},{24,8},{32,48},{40,56},{48,32},{56,40},{64,80... | collective-permute-start | bytes 1327112 | tf_op jit(solution)/shard_map/ppermute | solution.py:321
  91.0 19.9 %collective-permute-start.14 = (bf16[24,9216]{1,0:T(8,128)(2,1)S(1)}, bf16[24,9216]{1,0:T(8,128)(2,1)S(1)}, u32[]{:S(2)}, u32[]{:S(2)}) collective-permute-start(bf16[24,9216]{1,0:T(8,128)(2,1)S(1)} %add_select_fusion.refs_0_), channel_id=1, source_target_pairs={{0,32},{8,40},{16,48},{24,56},{32,0},{40,8},{48,16},{56,24},{64,96... | collective-permute-start | bytes 1327112 | tf_op jit(solution)/shard_map/ppermute | solution.py:321
  95.0 22.3 %collective-permute-start.15 = (bf16[24,9216]{1,0:T(8,128)(2,1)S(1)}, bf16[24,9216]{1,0:T(8,128)(2,1)S(1)}, u32[]{:S(2)}, u32[]{:S(2)}) collective-permute-start(bf16[24,9216]{1,0:T(8,128)(2,1)S(1)} %add_select_fusion.refs_0_), channel_id=1, source_target_pairs={{0,48},{8,56},{16,32},{24,40},{32,16},{40,24},{48,0},{56,8},{64,11... | collective-permute-start | bytes 1327112 | tf_op jit(solution)/shard_map/ppermute | solution.py:321
  95.7 23.3 %collective-permute-start.16 = (bf16[24,9216]{1,0:T(8,128)(2,1)S(1)}, bf16[24,9216]{1,0:T(8,128)(2,1)S(1)}, u32[]{:S(2)}, u32[]{:S(2)}) collective-permute-start(bf16[24,9216]{1,0:T(8,128)(2,1)S(1)} %add_select_fusion.refs_0_), channel_id=1, source_target_pairs={{0,8},{8,0},{16,24},{24,16},{32,40},{40,32},{48,56},{56,48},{64,72... | collective-permute-start | bytes 1327112 | tf_op jit(solution)/shard_map/ppermute | solution.py:321
  100.5 18.6 %collective-permute-start.17 = (bf16[24,9216]{1,0:T(8,128)(2,1)S(1)}, bf16[24,9216]{1,0:T(8,128)(2,1)S(1)}, u32[]{:S(2)}, u32[]{:S(2)}) collective-permute-start(bf16[24,9216]{1,0:T(8,128)(2,1)S(1)} %collective-permute-done.13.refs_1_), channel_id=1, source_target_pairs={{0,8},{8,0},{16,24},{24,16},{32,40},{40,32},{48,56},{56,48},{64,72... | collective-permute-start | bytes 1327112 | tf_op jit(solution)/shard_map/ppermute | solution.py:321
  110.9 8.1 %collective-permute-start.18 = (bf16[24,9216]{1,0:T(8,128)(2,1)S(1)}, bf16[24,9216]{1,0:T(8,128)(2,1)S(1)}, u32[]{:S(2)}, u32[]{:S(2)}) collective-permute-start(bf16[24,9216]{1,0:T(8,128)(2,1)S(1)} %collective-permute-done.14.refs_2_), channel_id=1, source_target_pairs={{0,8},{8,0},{16,24},{24,16},{32,40},{40,32},{48,56},{56,48},{64,72... | collective-permute-start | bytes 1327112 | tf_op jit(solution)/shard_map/ppermute | solution.py:321
  130.3 50.6 %all-to-all-start = ((bf16[8,2,6,48,384]{4,3,2,1,0:T(8,128)(2,1)}), bf16[8,2,6,48,384]{4,3,2,1,0:T(8,128)(2,1)}, u32[]{:S(2)}, u32[]{:S(2)}) async-start(bf16[8,2,6,48,384]{4,3,2,1,0:T(8,128)(2,1)} %forward_zy.2), calls=%async_computation | async-start | bytes 7077888 | tf_op jit(solution)/shard_map/all_to_all | solution.py:313
  180.9 47.9 %all-to-all-start.3 = ((bf16[8,2,6,48,384]{4,3,2,1,0:T(8,128)(2,1)}), bf16[8,2,6,48,384]{4,3,2,1,0:T(8,128)(2,1)}, u32[]{:S(2)}, u32[]{:S(2)}) async-start(bf16[8,2,6,48,384]{4,3,2,1,0:T(8,128)(2,1)} %middle_x.3), calls=%async_computation.3 | async-start | bytes 7077888 | tf_op jit(solution)/shard_map/all_to_all | solution.py:313
  228.7 47.0 %all-to-all-start.1 = ((bf16[8,2,6,48,384]{4,3,2,1,0:T(8,128)(2,1)}), bf16[8,2,6,48,384]{4,3,2,1,0:T(8,128)(2,1)}, u32[]{:S(2)}, u32[]{:S(2)}) async-start(bf16[8,2,6,48,384]{4,3,2,1,0:T(8,128)(2,1)} %middle_x.2), calls=%async_computation.1 | async-start | bytes 7077888 | tf_op jit(solution)/shard_map/all_to_all | solution.py:313
  (24 other events, 166.0 us)
